TPU v7x, 512 devices: a whole 4x8x8 slice. The times are simulated.
512 devices in a mesh: depth: 16 (over z, core), height: 32 (over x, y).
Axes of the slice: x: 4, y: 8, z: 8, core: 2. Of those that a mesh axis runs over, the one named last changes fastest.
Arguments:
- density: float32 [128, 2048, 128], P('depth', 'height'), may hold values from -6 to 6
- light_vector: float32 [3], replicated, may hold values from -1 to 1
- colour_gain: float32 [3], replicated, may hold values from 0.5 to 3
- colour_bias: float32 [3], replicated, may hold values from -1 to 1
- shear_step: int32 [4], replicated, may hold values from 0 to 32
- reverse_view: int32 [4], replicated, may hold values from 0 to 1
Outputs:
- images: float32 [4, 4, 2048, 128], P(None, None, ('height', 'depth'))
All inputs are finite; a program needn't handle non-finite values.
Results may differ from a plain program's by a relative error of at most 0.0003.
Values sent between devices are 32-bit elements; how exact they have to be, the bound alone decides.
No kernel may reach another device: no remote copies, remote signals or barrier semaphores. Data moves between devices by JAX's collectives and lax.ppermute only.
A program may use at most 64 MiB of HBM per device.

v0:
```python
import jax
import jax.numpy as jnp
from jax import lax
from jax.sharding import PartitionSpec as P

EXTINCTION = 2.5


def with_halo(value, sides, width):
    for axis, dim in sides:
        peers, length = (lax.axis_size(axis), value.shape[dim])
        up = [(i, (i + 1) % peers) for i in range(peers - 1)]
        down = [(j, i) for i, j in up]
        last = lax.slice_in_dim(value, length - width, length, axis=dim)
        first = lax.slice_in_dim(value, 0, width, axis=dim)
        before = lax.ppermute(last, axis, up)
        after = lax.ppermute(first, axis, down)
        value = jnp.concatenate([before, value, after], axis=dim)
    return value


def shifted(block, axis, distance):
    devices = range(lax.axis_size(axis))
    route = [(i - distance, i) for i in devices if i - distance in devices]
    return lax.ppermute(block, axis, route)


def from_partner(block, axis, distance):
    count = lax.axis_size(axis)
    route = []
    for low in range(count):
        high = low | 1 << distance
        if high != low and high < count:
            route += [(low, high), (high, low)]
    return lax.ppermute(block, axis, route)


def shade_block(padded, light_vector, colour_gain, colour_bias, extinction):
    centre = padded[1:-1, 1:-1, 1:-1]
    tilt_depth = 0.5 * (padded[2:, 1:-1, 1:-1] - padded[:-2, 1:-1, 1:-1])
    tilt_rows = 0.5 * (padded[1:-1, 2:, 1:-1] - padded[1:-1, :-2, 1:-1])
    tilt_cols = 0.5 * (padded[1:-1, 1:-1, 2:] - padded[1:-1, 1:-1, :-2])
    facing = (
        light_vector[0] * tilt_depth + light_vector[1] * tilt_rows + light_vector[2] * tilt_cols
    ) * lax.rsqrt(1.0 + tilt_depth * tilt_depth + tilt_rows * tilt_rows + tilt_cols * tilt_cols)
    shading = 0.25 + 1.5 * jnp.maximum(facing, 0.0)
    optical = extinction * jax.nn.softplus(centre)
    opacity = -jnp.expm1(-optical)
    colour = jax.nn.sigmoid(
        colour_gain[:, None, None, None] * centre[None] + colour_bias[:, None, None, None]
    )
    emitted = (opacity * shading)[None] * colour
    return jnp.concatenate([emitted, optical[None]], 0)


def over_front(front, behind):
    return jnp.concatenate(
        [front[:3] + jnp.exp(-front[3:4]) * behind[:3], front[3:4] + behind[3:4]], 0
    )


def on_device(density, light_vector, colour_gain, colour_bias, shear_step, reverse_view):
    planes, rows, cols = density.shape
    groups = lax.axis_size("depth")
    total_planes = planes * groups
    extinction = EXTINCTION / total_planes
    margin_rows = rows // 2
    views = shear_step.shape[0]
    padded = with_halo(density, (("depth", 0), ("height", 1)), 1)
    padded = jnp.pad(padded, ((0, 0), (0, 0), (1, 1)))
    fields = shade_block(padded, light_vector, colour_gain, colour_bias, extinction)
    upper = shifted(fields[:, :, :margin_rows, :], "height", -1)
    extended = jnp.concatenate([fields, upper], 2)
    extra = rows // (2 * groups) + 1
    extended = jnp.pad(extended, ((0, 0), (0, 0), (0, extra), (0, 0)))
    first_plane = lax.axis_index("depth") * planes
    plane_index = jnp.arange(planes, dtype=jnp.int32)

    def view_partial(view):
        step = shear_step[view]
        backward = reverse_view[view]
        base = first_plane * step // total_planes
        zero = jnp.zeros((), jnp.int32)
        window = lax.dynamic_slice(
            extended, (zero, zero, base, zero), (4, planes, rows + extra, cols)
        )
        relative = (first_plane + plane_index) * step // total_planes - base
        sample = jnp.zeros((4, planes, rows, cols), jnp.float32)
        for shift_rows in range(extra + 1):
            picked = (relative == shift_rows)[None, :, None, None]
            sample = jnp.where(picked, window[:, :, shift_rows : shift_rows + rows, :], sample)
        optical = sample[3]
        running = jnp.cumsum(optical, 0)
        depth_sum = running[-1]
        before = jnp.where(backward == 1, depth_sum[None] - running, running - optical)
        colour_sum = jnp.sum(sample[:3] * jnp.exp(-before)[None], 1)
        return jnp.concatenate([colour_sum, depth_sum[None]], 0)

    partial_image = jnp.stack([view_partial(view) for view in range(views)], 1)
    share = rows // groups
    blocks = partial_image.reshape(4, views, groups, share * cols)
    device = lax.axis_index("depth")
    current = blocks
    for level in range(groups.bit_length() - 1):
        count = current.shape[2]
        paired = current.reshape(4, views, count // 2, 2, share * cols)
        digit = device // 2**level % 2
        kept = lax.dynamic_index_in_dim(paired, digit, 3, keepdims=False)
        given = lax.dynamic_index_in_dim(paired, 1 - digit, 3, keepdims=False)
        partner = from_partner(given, "depth", level)
        mine_front = (reverse_view == digit)[None, :, None, None]
        front = jnp.where(mine_front, kept, partner)
        behind = jnp.where(mine_front, partner, kept)
        current = over_front(front, behind)
    final = current[:, :, 0]
    final = final.reshape(4, views, share, cols)
    return jnp.concatenate([final[:3], -jnp.expm1(-final[3:4])], 0)


def solution(mesh):
    placed = (P("depth", "height", None), P(), P(), P(), P(), P())
    return jax.shard_map(
        on_device,
        mesh=mesh,
        in_specs=placed,
        out_specs=P(None, None, ("height", "depth"), None),
        check_vma=False,
    )
```

profile of v0, /device:TPU:6, one launch (start us, length us, event | category | flops | bytes accessed | tf_op | source)
XLA Modules:
  0.0 85.2 jit_solution(584065559494488265)
XLA Ops:
  0.0 0.0 copy-start
  0.0 0.8 fusion.67
  0.8 1.7 %collective-permute-start.1 = (f32[1,64,128]{2,1,0:T(8,128)S(1)}, f32[1,64,128]{2,1,0:T(8,128)S(1)}, u32[]{:S(2)}, u32[]{:S(2)}) collective-permute-start(f32[1,64,128]{2,1,0:T(8,128)S(1)} %get-tuple-element.38), channel_id=1, source_target_pairs={{0,32},{32,64},{64,96},{96,128},{128,160},{160,192},{192,224},{224... | collective-permute-start | bytes 98312 | tf_op jit(solution)/shard_map/ppermute | solution.py:16
  2.6 1.3 %collective-permute-start = (f32[1,64,128]{2,1,0:T(8,128)S(1)}, f32[1,64,128]{2,1,0:T(8,128)S(1)}, u32[]{:S(2)}, u32[]{:S(2)}) collective-permute-start(f32[1,64,128]{2,1,0:T(8,128)S(1)} %get-tuple-element.37), channel_id=1, source_target_pairs={{32,0},{64,32},{96,64},{128,96},{160,128},{192,160},{224,192},{256... | collective-permute-start | bytes 98312 | tf_op jit(solution)/shard_map/ppermute | solution.py:17
  3.9 1.5 %fusion.69 = (s32[1]{0:T(128)}, s32[1]{0:T(128)}, s32[1]{0:T(128)}, s32[1]{0:T(128)}) fusion(s32[4]{0:T(128)} %param.10), kind=kLoop, calls=%fused_computation.181 | loop fusion | bytes 32 | tf_op jit(solution)/shard_map/slice | solution.py:80
  6.7 1.3 %broadcast_compare_fusion.4 = (pred[8]{0:T(512)(128)(4,1)S(1)}, s32[8]{0:T(128)S(1)}, pred[8]{0:T(512)(128)(4,1)S(1)}, s32[8]{0:T(128)S(1)}) fusion(s32[]{:T(128)S(6)} %select_n.295, s32[]{:T(128)} %bitcast.22, s32[]{:T(128)S(6)} %mul.258, s32[]{:T(128)S(6)} %select_n.286, s32[]{:T(128)} %bitcast.16), kind=kLoop, calls=%fused_computation.158 | loop fusion | flops 296 | bytes 100 | tf_op jit(solution)/shard_map/eq | solution.py:90
  8.1 1.5 %fusion.68 = (s32[1]{0:T(128)}, s32[1]{0:T(128)}, s32[1]{0:T(128)}, s32[1]{0:T(128)}) fusion(s32[4]{0:T(128)} %param.11), kind=kLoop, calls=%fused_computation.180 | loop fusion | bytes 32 | tf_op jit(solution)/shard_map/slice | solution.py:81
  9.6 0.0 collective-permute-done.1
  9.6 0.0 copy-start.2
  9.6 0.0 copy-start.3
  9.6 1.0 %constant_dynamic-update-slice_fusion.1 = f32[10,64,128]{2,1,0:T(8,128)S(1)} fusion(f32[10,64,128]{2,1,0:T(8,128)S(1)} %constant_dynamic-update-slice_fusion.2, f32[8,64,128]{2,1,0:T(8,128)} %param.6), kind=kLoop, calls=%fused_computation.117 | loop fusion | bytes 524288
  10.6 0.0 collective-permute-done
  10.7 5.6 %collective-permute-start.2 = (f32[10,1,128]{2,1,0:T(1,128)S(1)}, f32[10,1,128]{2,1,0:T(1,128)S(1)}, u32[]{:S(2)}, u32[]{:S(2)}) collective-permute-start(f32[10,1,128]{2,1,0:T(1,128)S(1)} %get-tuple-element.24), channel_id=1, source_target_pairs={{1,0},{2,1},{3,2},{4,3},{5,4},{6,5},{7,6},{8,7},{9,8},{10,9},{11,1... | collective-permute-start | bytes 15368 | tf_op jit(solution)/shard_map/ppermute | solution.py:17
  16.3 1.9 %collective-permute-start.3 = (f32[10,1,128]{2,1,0:T(1,128)S(1)}, f32[10,1,128]{2,1,0:T(1,128)S(1)}, u32[]{:S(2)}, u32[]{:S(2)}) collective-permute-start(f32[10,1,128]{2,1,0:T(1,128)S(1)} %get-tuple-element.23), channel_id=1, source_target_pairs={{0,1},{1,2},{2,3},{3,4},{4,5},{5,6},{6,7},{7,8},{8,9},{9,10},{10,1... | collective-permute-start | bytes 15368 | tf_op jit(solution)/shard_map/ppermute | solution.py:16
  18.2 1.4 %fusion.70 = (f32[1]{0:T(128)}, f32[1]{0:T(128)}, f32[1]{0:T(128)}) fusion(f32[3]{0:T(128)} %param.7), kind=kLoop, calls=%fused_computation.182 | loop fusion | bytes 24 | tf_op jit(solution)/shard_map/slice | solution.py:44
  25.3 0.0 collective-permute-done.2
  25.3 0.0 collective-permute-done.3
  25.3 0.3 select_maximum_fusion.2
  25.6 0.0 copy-done
  25.7 0.5 add_multiply_fusion
  26.2 0.0 copy-done.2
  26.2 0.0 copy-done.3
  26.2 0.3 divide_multiply_fusion
  26.6 6.0 %collective-permute-start.4 = (f32[4,8,32,128]{3,2,1,0:T(8,128)S(1)}, f32[4,8,32,128]{3,2,1,0:T(8,128)S(1)}, u32[]{:S(2)}, u32[]{:S(2)}) collective-permute-start(f32[4,8,32,128]{3,2,1,0:T(8,128)S(1)} %pad_maximum_fusion), channel_id=1, source_target_pairs={{1,0},{2,1},{3,2},{4,3},{5,4},{6,5},{7,6},{8,7},{9,8},{10,9},{11,1... | collective-permute-start | bytes 1572872 | tf_op jit(solution)/shard_map/ppermute | solution.py:25
  32.6 1.2 %broadcast_compare_fusion.6 = (pred[8]{0:T(512)(128)(4,1)S(1)}, s32[8]{0:T(128)S(1)}, pred[8]{0:T(512)(128)(4,1)S(1)}, s32[8]{0:T(128)S(1)}) fusion(s32[]{:T(128)S(6)} %select_n.277, s32[]{:T(128)} %bitcast.10, s32[]{:T(128)S(6)} %mul.258, s32[]{:T(128)S(6)} %select_n.267, s32[]{:T(128)} %bitcast), kind=kLoop, calls=%fused_computation.160 | loop fusion | flops 296 | bytes 100 | tf_op jit(solution)/shard_map/eq | solution.py:90
  33.9 9.2 %collective-permute-done.4 = f32[4,8,32,128]{3,2,1,0:T(8,128)S(1)} collective-permute-done((f32[4,8,32,128]{3,2,1,0:T(8,128)S(1)}, f32[4,8,32,128]{3,2,1,0:T(8,128)S(1)}, u32[]{:S(2)}, u32[]{:S(2)}) %collective-permute-start.4) | collective-permute-done | bytes 524320 | tf_op jit(solution)/shard_map/ppermute | solution.py:25
  43.1 0.1 select_maximum_fusion
  43.2 1.3 %fusion.2 = (f32[4,8,64,128]{3,2,1,0:T(8,128)S(1)}, f32[4,8,64,128]{3,2,1,0:T(8,128)S(1)}) fusion(f32[4,8,99,128]{3,2,1,0:T(8,128)S(1)} %select_maximum_fusion, s32[]{:T(128)S(6)} %select_n.296, s32[]{:T(128)S(6)} %add.298, s32[]{:T(128)S(6)} %add.297, s32[]{:T(128)S(6)} %add.296, pred[8]{0:T(512)(128)(4,1)S(1)} %get-tuple-element.59, ...), kind=kLoop, calls=%fused_computation.8 | loop fusion | flops 2097152 | bytes 10485856 | tf_op jit(solution)/shard_map/jit(_where)/select_n | solution.py:91
  44.6 0.1 fusion.23
  44.6 0.1 fusion.12
  44.7 0.1 stack.18
  44.9 0.1 fusion.29
  44.9 0.1 fusion.13
  45.0 0.1 stack.17
  45.1 1.3 %fusion.8 = (f32[4,8,64,128]{3,2,1,0:T(8,128)S(1)}, f32[4,8,64,128]{3,2,1,0:T(8,128)S(1)}) fusion(f32[4,8,99,128]{3,2,1,0:T(8,128)S(1)} %select_maximum_fusion, s32[]{:T(128)S(6)} %select_n.278, s32[]{:T(128)S(6)} %add.292, s32[]{:T(128)S(6)} %add.291, s32[]{:T(128)S(6)} %add.290, pred[8]{0:T(512)(128)(4,1)S(1)} %get-tuple-element.69, ...), kind=kLoop, calls=%fused_computation.16 | loop fusion | flops 2097152 | bytes 10485856 | tf_op jit(solution)/shard_map/jit(_where)/select_n | solution.py:91
  46.5 0.1 fusion.35
  46.5 0.1 fusion.14
  46.6 0.1 stack.16
  46.7 0.1 fusion.41
  46.8 0.1 fusion.15
  46.9 0.0 copy-start.1
  46.9 0.1 stack.15
  47.1 0.6 constant_dynamic-slice_fusion.1
  47.7 3.8 %collective-permute-start.5 = (f32[4,4,8,512]{3,2,1,0:T(8,128)S(1)}, f32[4,4,8,512]{3,2,1,0:T(8,128)S(1)}, u32[]{:S(2)}, u32[]{:S(2)}) collective-permute-start(f32[4,4,8,512]{3,2,1,0:T(8,128)S(1)} %bitcast.127), channel_id=1, source_target_pairs={{0,32},{32,0},{64,96},{96,64},{128,160},{160,128},{192,224},{224,1... | collective-permute-start | bytes 786440 | tf_op jit(solution)/shard_map/ppermute | solution.py:35
  51.6 0.0 copy-done.1
  51.6 1.0 %collective-permute-done.5 = f32[4,4,8,512]{3,2,1,0:T(8,128)S(1)} collective-permute-done((f32[4,4,8,512]{3,2,1,0:T(8,128)S(1)}, f32[4,4,8,512]{3,2,1,0:T(8,128)S(1)}, u32[]{:S(2)}, u32[]{:S(2)}) %collective-permute-start.5) | collective-permute-done | bytes 262176 | tf_op jit(solution)/shard_map/ppermute | solution.py:35
  52.7 0.1 bitcast_select_fusion.1
  52.9 0.2 copy.9
  53.1 6.3 %collective-permute-start.6 = (f32[4,4,4,512]{3,1,2,0:T(4,128)S(1)}, f32[4,4,4,512]{3,1,2,0:T(4,128)S(1)}, u32[]{:S(2)}, u32[]{:S(2)}) collective-permute-start(f32[4,4,4,512]{3,1,2,0:T(4,128)S(1)} %dynamic-slice_bitcast_fusion), channel_id=1, source_target_pairs={{0,64},{64,0},{32,96},{96,32},{128,192},{192,128},{160,224},{224,1... | collective-permute-start | bytes 393224 | tf_op jit(solution)/shard_map/ppermute | solution.py:35
  59.4 3.8 %collective-permute-done.6 = f32[4,4,4,512]{3,1,2,0:T(4,128)S(1)} collective-permute-done((f32[4,4,4,512]{3,1,2,0:T(4,128)S(1)}, f32[4,4,4,512]{3,1,2,0:T(4,128)S(1)}, u32[]{:S(2)}, u32[]{:S(2)}) %collective-permute-start.6) | collective-permute-done | bytes 131104 | tf_op jit(solution)/shard_map/ppermute | solution.py:35
  63.2 0.1 bitcast_select_fusion.3
  63.4 7.5 %collective-permute-start.7 = (f32[4,4,2,512]{3,1,2,0:T(4,128)S(1)}, f32[4,4,2,512]{3,1,2,0:T(4,128)S(1)}, u32[]{:S(2)}, u32[]{:S(2)}) collective-permute-start(f32[4,4,2,512]{3,1,2,0:T(4,128)S(1)} %dynamic-slice_bitcast_fusion.1), channel_id=1, source_target_pairs={{0,128},{128,0},{32,160},{160,32},{64,192},{192,64},{96,224},{224,... | collective-permute-start | bytes 196616 | tf_op jit(solution)/shard_map/ppermute | solution.py:35
  70.9 3.6 %collective-permute-done.7 = f32[4,4,2,512]{3,1,2,0:T(4,128)S(1)} collective-permute-done((f32[4,4,2,512]{3,1,2,0:T(4,128)S(1)}, f32[4,4,2,512]{3,1,2,0:T(4,128)S(1)}, u32[]{:S(2)}, u32[]{:S(2)}) %collective-permute-start.7) | collective-permute-done | bytes 65568 | tf_op jit(solution)/shard_map/ppermute | solution.py:35
  74.5 0.1 bitcast_select_fusion.5
  74.7 5.9 %collective-permute-start.8 = (f32[4,4,1,512]{3,1,2,0:T(4,128)S(1)}, f32[4,4,1,512]{3,1,2,0:T(4,128)S(1)}, u32[]{:S(2)}, u32[]{:S(2)}) collective-permute-start(f32[4,4,1,512]{3,1,2,0:T(4,128)S(1)} %fusion.52), channel_id=1, source_target_pairs={{0,256},{256,0},{32,288},{288,32},{64,320},{320,64},{96,352},{352,... | collective-permute-start | bytes 98312 | tf_op jit(solution)/shard_map/ppermute | solution.py:35
  80.6 3.8 %collective-permute-done.8 = f32[4,4,1,512]{3,1,2,0:T(4,128)S(1)} collective-permute-done((f32[4,4,1,512]{3,1,2,0:T(4,128)S(1)}, f32[4,4,1,512]{3,1,2,0:T(4,128)S(1)}, u32[]{:S(2)}, u32[]{:S(2)}) %collective-permute-start.8) | collective-permute-done | bytes 32800 | tf_op jit(solution)/shard_map/ppermute | solution.py:35
  84.4 0.1 broadcast_select_fusion.1
  84.6 0.6 pad_maximum_fusion.11
  (41 shorter events, 0.6 us)
Async XLA Ops:
  0.0 25.6 %copy-start = (f32[8,64,128]{2,1,0:T(8,128)S(1)}, f32[8,64,128]{2,1,0:T(8,128)}, u32[]{:S(2)}) copy-start(f32[8,64,128]{2,1,0:T(8,128)} %param.6) | copy-start | bytes 786436
  0.8 8.8 %collective-permute-start.1 = (f32[1,64,128]{2,1,0:T(8,128)S(1)}, f32[1,64,128]{2,1,0:T(8,128)S(1)}, u32[]{:S(2)}, u32[]{:S(2)}) collective-permute-start(f32[1,64,128]{2,1,0:T(8,128)S(1)} %get-tuple-element.38), channel_id=1, source_target_pairs={{0,32},{32,64},{64,96},{96,128},{128,160},{160,192},{192,224},{224... | collective-permute-start | bytes 98312 | tf_op jit(solution)/shard_map/ppermute | solution.py:16
  2.6 8.0 %collective-permute-start = (f32[1,64,128]{2,1,0:T(8,128)S(1)}, f32[1,64,128]{2,1,0:T(8,128)S(1)}, u32[]{:S(2)}, u32[]{:S(2)}) collective-permute-start(f32[1,64,128]{2,1,0:T(8,128)S(1)} %get-tuple-element.37), channel_id=1, source_target_pairs={{32,0},{64,32},{96,64},{128,96},{160,128},{192,160},{224,192},{256... | collective-permute-start | bytes 98312 | tf_op jit(solution)/shard_map/ppermute | solution.py:17
  9.6 16.6 %copy-start.2 = (f32[3]{0:T(128)S(1)}, f32[3]{0:T(128)}, u32[]{:S(2)}) copy-start(f32[3]{0:T(128)} %param.9) | copy-start | bytes 40
  9.6 16.6 %copy-start.3 = (f32[3]{0:T(128)S(1)}, f32[3]{0:T(128)}, u32[]{:S(2)}) copy-start(f32[3]{0:T(128)} %param.8) | copy-start | bytes 40
  10.7 14.7 %collective-permute-start.2 = (f32[10,1,128]{2,1,0:T(1,128)S(1)}, f32[10,1,128]{2,1,0:T(1,128)S(1)}, u32[]{:S(2)}, u32[]{:S(2)}) collective-permute-start(f32[10,1,128]{2,1,0:T(1,128)S(1)} %get-tuple-element.24), channel_id=1, source_target_pairs={{1,0},{2,1},{3,2},{4,3},{5,4},{6,5},{7,6},{8,7},{9,8},{10,9},{11,1... | collective-permute-start | bytes 15368 | tf_op jit(solution)/shard_map/ppermute | solution.py:17
  16.3 9.0 %collective-permute-start.3 = (f32[10,1,128]{2,1,0:T(1,128)S(1)}, f32[10,1,128]{2,1,0:T(1,128)S(1)}, u32[]{:S(2)}, u32[]{:S(2)}) collective-permute-start(f32[10,1,128]{2,1,0:T(1,128)S(1)} %get-tuple-element.23), channel_id=1, source_target_pairs={{0,1},{1,2},{2,3},{3,4},{4,5},{5,6},{6,7},{7,8},{8,9},{9,10},{10,1... | collective-permute-start | bytes 15368 | tf_op jit(solution)/shard_map/ppermute | solution.py:16
  26.6 16.5 %collective-permute-start.4 = (f32[4,8,32,128]{3,2,1,0:T(8,128)S(1)}, f32[4,8,32,128]{3,2,1,0:T(8,128)S(1)}, u32[]{:S(2)}, u32[]{:S(2)}) collective-permute-start(f32[4,8,32,128]{3,2,1,0:T(8,128)S(1)} %pad_maximum_fusion), channel_id=1, source_target_pairs={{1,0},{2,1},{3,2},{4,3},{5,4},{6,5},{7,6},{8,7},{9,8},{10,9},{11,1... | collective-permute-start | bytes 1572872 | tf_op jit(solution)/shard_map/ppermute | solution.py:25
  46.9 4.7 %copy-start.1 = (s32[4]{0:T(128)S(1)}, s32[4]{0:T(128)}, u32[]{:S(2)}) copy-start(s32[4]{0:T(128)} %param.11) | copy-start | bytes 52
  47.7 5.0 %collective-permute-start.5 = (f32[4,4,8,512]{3,2,1,0:T(8,128)S(1)}, f32[4,4,8,512]{3,2,1,0:T(8,128)S(1)}, u32[]{:S(2)}, u32[]{:S(2)}) collective-permute-start(f32[4,4,8,512]{3,2,1,0:T(8,128)S(1)} %bitcast.127), channel_id=1, source_target_pairs={{0,32},{32,0},{64,96},{96,64},{128,160},{160,128},{192,224},{224,1... | collective-permute-start | bytes 786440 | tf_op jit(solution)/shard_map/ppermute | solution.py:35
  53.1 10.1 %collective-permute-start.6 = (f32[4,4,4,512]{3,1,2,0:T(4,128)S(1)}, f32[4,4,4,512]{3,1,2,0:T(4,128)S(1)}, u32[]{:S(2)}, u32[]{:S(2)}) collective-permute-start(f32[4,4,4,512]{3,1,2,0:T(4,128)S(1)} %dynamic-slice_bitcast_fusion), channel_id=1, source_target_pairs={{0,64},{64,0},{32,96},{96,32},{128,192},{192,128},{160,224},{224,1... | collective-permute-start | bytes 393224 | tf_op jit(solution)/shard_map/ppermute | solution.py:35
  63.4 11.1 %collective-permute-start.7 = (f32[4,4,2,512]{3,1,2,0:T(4,128)S(1)}, f32[4,4,2,512]{3,1,2,0:T(4,128)S(1)}, u32[]{:S(2)}, u32[]{:S(2)}) collective-permute-start(f32[4,4,2,512]{3,1,2,0:T(4,128)S(1)} %dynamic-slice_bitcast_fusion.1), channel_id=1, source_target_pairs={{0,128},{128,0},{32,160},{160,32},{64,192},{192,64},{96,224},{224,... | collective-permute-start | bytes 196616 | tf_op jit(solution)/shard_map/ppermute | solution.py:35
  74.7 9.7 %collective-permute-start.8 = (f32[4,4,1,512]{3,1,2,0:T(4,128)S(1)}, f32[4,4,1,512]{3,1,2,0:T(4,128)S(1)}, u32[]{:S(2)}, u32[]{:S(2)}) collective-permute-start(f32[4,4,1,512]{3,1,2,0:T(4,128)S(1)} %fusion.52), channel_id=1, source_target_pairs={{0,256},{256,0},{32,288},{288,32},{64,320},{320,64},{96,352},{352,... | collective-permute-start | bytes 98312 | tf_op jit(solution)/shard_map/ppermute | solution.py:35
where the time goes:
time: 86.2 us; the launch traced here: 85.2 us
  starting transfers between devices  40.1 us (47%)
  waiting for transfers between devices  21.5 us (25%)
  other arithmetic  8.47 us (10%)
  between operations  7.84 us (9%)
  local copies, waits for them, and re-layouts  7.37 us (9%)
    ppermute x4, starting transfers between devices, from_partner(): return lax.ppermute(block, axis, route)  23.5 us
    ppermute x4, waiting for transfers between devices, from_partner(): return lax.ppermute(block, axis, route)  12.3 us
    ppermute x1, waiting for transfers between devices, shifted(): return lax.ppermute(block, axis, route)  9.2 us
    ppermute x2, starting transfers between devices, with_halo(): after = lax.ppermute(first, axis, down)  6.93 us
    ppermute x1, starting transfers between devices, shifted(): return lax.ppermute(block, axis, route)  6.03 us
    ppermute x2, starting transfers between devices, with_halo(): before = lax.ppermute(last, axis, up)  3.65 us
    select_n x2, other arithmetic, view_partial(): jnp.where(picked, window[:, :, shift_rows:shift_rows + rows, :], sample)  2.63 us
    eq x6, other arithmetic, view_partial(): picked = (relative == shift_rows)[None, :, None, None]  2.62 us
  transfers between devices with their start and end apart: 9, of which 5 were waited for; matrix products, arithmetic and copies ran while one was open for 9% of the time, Pallas kernels for 0%

commit v1 on v0

v1 whole, which is shorter than its diff:
```python
import functools

import jax
import jax.numpy as jnp
from jax import lax
from jax.experimental import pallas as pl
from jax.experimental.pallas import tpu as pltpu
from jax.sharding import PartitionSpec as P

EXTINCTION = 2.5
SMEM = pl.BlockSpec(memory_space=pltpu.SMEM)
VMEM = pl.BlockSpec(memory_space=pltpu.VMEM)
PLANES, ROWS, COLS, SHEAR, VIEWS, GROUPS = 8, 64, 128, 32, 4, 16
TOP = 8
TALL = ROWS + SHEAR
PADDED = TOP + TALL + 8
SLABS = PLANES + 1
CHIPS = GROUPS // 2
SHARE = ROWS // GROUPS


def opacity_of(optical):
    series = 1.0 - optical * (1.0 / 6.0)
    for term in (5.0, 4.0, 3.0, 2.0):
        series = 1.0 - optical * (1.0 / term) * series
    return optical * series


def render_kernel(
    place, light, gain, bias, shear, reverse, own, low, high, before, given, kept, brick, fields, starts
):
    depth, height = place[0], place[1]
    total_planes = PLANES * GROUPS
    zeros = jnp.zeros((8, COLS), jnp.float32)
    for plane in range(PLANES):
        brick[plane + 2, TOP - 8 : TOP, :] = jnp.broadcast_to(low[plane : plane + 1, :], (8, COLS))
        brick[plane + 2, TOP : TOP + ROWS, :] = own[plane]
        brick[plane + 2, TOP + ROWS : TOP + TALL, :] = high[plane]
        brick[plane + 2, TOP + TALL :, :] = zeros
    for plane in range(2):
        brick[plane, TOP - 8 : TOP, :] = jnp.broadcast_to(before[plane, TALL : TALL + 1, :], (8, COLS))
        brick[plane, TOP : TOP + TALL, :] = before[plane, :TALL, :]
        brick[plane, TOP + TALL :, :] = zeros
    brick[PLANES + 2] = jnp.zeros((PADDED, COLS), jnp.float32)

    chunk = 32
    lane = lax.broadcasted_iota(jnp.int32, (chunk, COLS), 1)

    def shade(step, _):
        plane = 1 + step // (TALL // chunk)
        row = step % (TALL // chunk) * chunk
        row = pl.multiple_of(row, chunk)
        inside = jnp.where(plane == 1, depth > 0, jnp.where(plane == SLABS, depth == GROUPS - 1, True))
        beyond = jnp.logical_and(height == 31, row >= ROWS)
        extinction = jnp.where(jnp.logical_and(inside, jnp.logical_not(beyond)), EXTINCTION / total_planes, 0.0)
        window = brick[plane, pl.ds(row, chunk + 16), :]
        centre = window[TOP : TOP + chunk]
        tilt_rows = 0.5 * (window[TOP + 1 : TOP + 1 + chunk] - window[TOP - 1 : TOP - 1 + chunk])
        tilt_depth = 0.5 * (brick[plane + 1, pl.ds(row + TOP, chunk), :] - brick[plane - 1, pl.ds(row + TOP, chunk), :])
        right = jnp.where(lane == COLS - 1, 0.0, pltpu.roll(centre, COLS - 1, 1))
        left = jnp.where(lane == 0, 0.0, pltpu.roll(centre, 1, 1))
        tilt_cols = 0.5 * (right - left)
        facing = (light[0] * tilt_depth + light[1] * tilt_rows + light[2] * tilt_cols) * lax.rsqrt(
            1.0 + tilt_depth * tilt_depth + tilt_rows * tilt_rows + tilt_cols * tilt_cols
        )
        shading = 0.25 + 1.5 * jnp.maximum(facing, 0.0)
        optical = extinction * (jnp.maximum(centre, 0.0) + jnp.log1p(jnp.exp(-jnp.abs(centre))))
        strength = opacity_of(optical) * shading
        place_of = pl.multiple_of((plane - 1) * TALL + row, chunk)
        for colour in range(3):
            tone = jax.nn.sigmoid(gain[colour] * centre + bias[colour])
            fields[colour, pl.ds(place_of, chunk), :] = strength * tone
        fields[3, pl.ds(place_of, chunk), :] = optical
        return 0

    lax.fori_loop(0, SLABS * (TALL // chunk), shade, 0)

    for view in range(VIEWS):
        for step in range(SLABS):
            plane = jnp.where(reverse[view] == 1, SLABS - 1 - step, step)
            depth_plane = jnp.maximum(depth * PLANES - 1 + plane, 0)
            offset = lax.shift_right_logical(depth_plane * shear[view], 7)
            starts[view * SLABS + step] = plane * TALL + offset

    core = depth % 2
    upper = lax.broadcasted_iota(jnp.int32, (8, COLS), 0) < SHARE

    def render(tile, _):
        for pair in range(VIEWS // 2):
            sums = []
            for view in (2 * pair, 2 * pair + 1):
                red = green = blue = optical = jnp.zeros((8, COLS), jnp.float32)
                for step in range(SLABS):
                    rows = pl.ds(starts[view * SLABS + step] + 8 * tile, 8)
                    through = jnp.exp(-optical)
                    red = red + fields[0, rows, :] * through
                    green = green + fields[1, rows, :] * through
                    blue = blue + fields[2, rows, :] * through
                    optical = optical + fields[3, rows, :]
                sums.append((red, green, blue, optical))
            for kind in range(4):
                first, second = sums[0][kind], sums[1][kind]
                low_rows = jnp.where(upper, first, pltpu.roll(second, SHARE, 0))
                high_rows = jnp.where(upper, pltpu.roll(first, SHARE, 0), second)
                kept[tile, kind, pair] = jnp.where(core == 1, high_rows, low_rows)
                given[tile, kind, pair] = jnp.where(core == 1, low_rows, high_rows)
        return 0

    lax.fori_loop(0, ROWS // 8, render, 0)


def view_mask(reverse, pair, digit):
    upper = lax.broadcasted_iota(jnp.int32, (8, COLS), 0) < SHARE
    first = jnp.where(reverse[2 * pair] == digit, 1, 0)
    second = jnp.where(reverse[2 * pair + 1] == digit, 1, 0)
    return jnp.where(upper, first, second) == 1


def pair_kernel(place, reverse, kept, gathered, out):
    core = place[0] % 2
    for pair in range(VIEWS // 2):
        mine_front = view_mask(reverse, pair, core)

        def merge(chip, _):
            mine = [kept[chip, kind, pair] for kind in range(4)]
            other = [gathered[1 - core, chip, kind, pair] for kind in range(4)]
            through = jnp.exp(-jnp.where(mine_front, mine[3], other[3]))
            for kind in range(3):
                front = jnp.where(mine_front, mine[kind], other[kind])
                behind = jnp.where(mine_front, other[kind], mine[kind])
                out[chip, kind, pair] = front + through * behind
            out[chip, 3, pair] = mine[3] + other[3]
            return 0

        lax.fori_loop(0, CHIPS, merge, 0, unroll=True)


def final_kernel(reverse, slabs, out):
    for pair in range(VIEWS // 2):
        backward = view_mask(reverse, pair, 1)
        optical = [slabs[chip, 3, pair] for chip in range(CHIPS)]
        ahead, behind = [jnp.zeros((8, COLS), jnp.float32)], [jnp.zeros((8, COLS), jnp.float32)]
        for chip in range(CHIPS - 1):
            ahead.append(ahead[-1] + optical[chip])
            behind.append(behind[-1] + optical[CHIPS - 1 - chip])
        total = ahead[-1] + optical[-1]
        sums = [jnp.zeros((8, COLS), jnp.float32)] * 3
        for chip in range(CHIPS):
            through = jnp.exp(-jnp.where(backward, behind[CHIPS - 1 - chip], ahead[chip]))
            sums = [sums[kind] + slabs[chip, kind, pair] * through for kind in range(3)]
        small = total * (1.0 - total * 0.5 * (1.0 - total * (1.0 / 3.0) * (1.0 - total * 0.25 * (1.0 - total * 0.2))))
        cover = jnp.where(total < 0.0625, small, 1.0 - jnp.exp(-total))
        for kind, value in enumerate((*sums, cover)):
            out[kind, 2 * pair] = value[:SHARE]
            out[kind, 2 * pair + 1] = value[SHARE:]


def on_device(density, light_vector, colour_gain, colour_bias, shear_step, reverse_view):
    depth, height = lax.axis_index("depth"), lax.axis_index("height")
    place = jnp.stack([depth, height]).astype(jnp.int32)
    heights, depths = lax.axis_size("height"), lax.axis_size("depth")
    up = [(i, i + 1) for i in range(heights - 1)]
    down = [(i + 1, i) for i in range(heights - 1)]
    low = lax.ppermute(density[:, ROWS - 1, :], "height", up)
    high = lax.ppermute(density[:, :SHEAR, :], "height", down)
    last = jnp.concatenate(
        [density[PLANES - 2 :], high[PLANES - 2 :], jnp.broadcast_to(low[PLANES - 2 :, None], (2, 8, COLS))], 1
    )
    before = lax.ppermute(last, "depth", [(i, i + 1) for i in range(depths - 1)])

    part = jax.ShapeDtypeStruct((CHIPS, 4, VIEWS // 2, 8, COLS), jnp.float32)
    given, kept = pl.pallas_call(
        render_kernel,
        out_shape=(part, part),
        in_specs=[SMEM] * 6 + [VMEM] * 4,
        out_specs=(VMEM, VMEM),
        scratch_shapes=[
            pltpu.VMEM((PLANES + 3, PADDED, COLS), jnp.float32),
            pltpu.VMEM((4, SLABS * TALL, COLS), jnp.float32),
            pltpu.SMEM((VIEWS * SLABS,), jnp.int32),
        ],
        name="render",
    )(place, light_vector, colour_gain, colour_bias, shear_step, reverse_view, density, low, high, before)

    cores = [[2 * chip, 2 * chip + 1] for chip in range(CHIPS)]
    gathered = lax.all_gather(given, "depth", axis=0, axis_index_groups=cores)
    merged = pl.pallas_call(
        pair_kernel, out_shape=part, in_specs=[SMEM] * 2 + [VMEM] * 2, out_specs=VMEM, name="merge"
    )(place, reverse_view, kept, gathered)
    chips = [[core + 2 * chip for chip in range(CHIPS)] for core in range(2)]
    slabs = lax.all_to_all(merged, "depth", 0, 0, tiled=True, axis_index_groups=chips)
    return pl.pallas_call(
        final_kernel,
        out_shape=jax.ShapeDtypeStruct((4, VIEWS, SHARE, COLS), jnp.float32),
        in_specs=[SMEM, VMEM],
        out_specs=VMEM,
        name="composite",
    )(reverse_view, slabs)


def solution(mesh):
    placed = (P("depth", "height", None), P(), P(), P(), P(), P())
    return jax.shard_map(
        on_device,
        mesh=mesh,
        in_specs=placed,
        out_specs=P(None, None, ("height", "depth"), None),
        check_vma=False,
    )
```

time: 86.2 us -> 60.2 us (0.70)
  blocking collectives: 0 us -> 32.9 us
  starting transfers between devices: 40.1 us -> 8.85 us
  waiting for transfers between devices: 21.5 us -> 5.98 us
  Pallas kernels: 0 us -> 8.91 us
  other arithmetic: 8.47 us -> 0.63 us
  between operations: 7.84 us -> 0.09 us
  local copies, waits for them, and re-layouts: 7.37 us -> 2.27 us
    ppermute x9 -> x3, starting transfers between devices: 40.1 us -> 8.85 us  [the longest x1 5.64 us: on_device(): high = lax.ppermute(density[:, :SHEAR, :], 'height', down)]
    all_to_all x0 -> x1, blocking collectives: none -> 24.1 us  [on_device(): lax.all_to_all(merged, 'depth', 0, 0, tiled=True, axis_index_groups=chips)]
    ppermute x9 -> x3, waiting for transfers between devices: 21.5 us -> 5.98 us  [the longest x1 5.66 us: on_device(): low = lax.ppermute(density[:, ROWS - 1, :], 'height', up)]
    pallas_call x0 -> x3, Pallas kernels: none -> 8.91 us  [the longest x1 5.42 us: on_device(): pl.pallas_call(render_kernel, out_shape=(part, part), in_specs=[SMEM] * 6...]
    all_gather x0 -> x1, blocking collectives: none -> 8.8 us  [on_device(): gathered = lax.all_gather(given, 'depth', axis=0, axis_index_groups=cores)]
    slice x6, local copies, waits for them, and re-layouts: 5.18 us -> 1.01 us  [the longest x1 0.99 us: on_device(): high = lax.ppermute(density[:, :SHEAR, :], 'height', down)]
    select_n x6 -> x0, other arithmetic: 3.03 us -> none  [the longest x2 2.63 us: view_partial(): jnp.where(picked, window[:, :, shift_rows:shift_rows + rows, :], sample)]
    eq x7 -> x0, other arithmetic: 2.63 us -> none  [the longest x6 2.62 us: view_partial(): picked = (relative == shift_rows)[None, :, None, None]]
  transfers between devices with their start and end apart: 9 -> 3, of which waited for: 5 -> 2; matrix products, arithmetic and copies ran while one was open for 9% -> 1% of each run, Pallas kernels for 0% -> 0%
where the time goes in v1:
time: 60.2 us; the launch traced here: 59.6 us
  blocking collectives  32.9 us (55%)
  Pallas kernels  8.91 us (15%)
  starting transfers between devices  8.85 us (15%)
  waiting for transfers between devices  5.98 us (10%)
  local copies, waits for them, and re-layouts  2.27 us (4%)
  other arithmetic  0.63 us (1%)
    all_to_all x1, blocking collectives, on_device(): lax.all_to_all(merged, 'depth', 0, 0, tiled=True, axis_index_groups=chips)  24.1 us
    all_gather x1, blocking collectives, on_device(): gathered = lax.all_gather(given, 'depth', axis=0, axis_index_groups=cores)  8.8 us
    ppermute x1, waiting for transfers between devices, on_device(): low = lax.ppermute(density[:, ROWS - 1, :], 'height', up)  5.66 us
    ppermute x1, starting transfers between devices, on_device(): high = lax.ppermute(density[:, :SHEAR, :], 'height', down)  5.64 us
    pallas_call x1, Pallas kernels, on_device(): pl.pallas_call(render_kernel, out_shape=(part, part), in_specs=[SMEM] * 6...  5.42 us
    ppermute x1, starting transfers between devices, on_device(): low = lax.ppermute(density[:, ROWS - 1, :], 'height', up)  1.92 us
    pallas_call x1, Pallas kernels, on_device(): pl.pallas_call(pair_kernel, out_shape=part, in_specs=[SMEM] * 2 + [VMEM]...  1.88 us
    pallas_call x1, Pallas kernels, on_device(): pl.pallas_call(final_kernel, out_shape=jax.ShapeDtypeStruct((4, VIEWS, SH...  1.61 us
  transfers between devices with their start and end apart: 3, of which 2 were waited for; matrix products, arithmetic and copies ran while one was open for 1% of the time, Pallas kernels for 0%

profile of v1, /device:TPU:6, one launch (start us, length us, event | category | flops | bytes accessed | tf_op | source)
XLA Modules:
  0.0 59.6 jit_solution(4593539640044155495)
XLA Ops:
  0.0 0.0 copy-start
  0.0 1.0 %slice.16 = f32[8,32,128]{2,1,0:T(8,128)S(1)} slice(f32[8,64,128]{2,1,0:T(8,128)} %own.1), slice={[0:8], [0:32], [0:128]} | slice | bytes 262144 | tf_op jit(solution)/shard_map/slice | solution.py:165
  1.0 5.6 %collective-permute-start.1 = (f32[8,32,128]{2,1,0:T(8,128)S(1)}, f32[8,32,128]{2,1,0:T(8,128)S(1)}, u32[]{:S(2)}, u32[]{:S(2)}) collective-permute-start(f32[8,32,128]{2,1,0:T(8,128)S(1)} %slice.16), channel_id=1, source_target_pairs={{1,0},{2,1},{3,2},{4,3},{5,4},{6,5},{7,6},{8,7},{9,8},{10,9},{11,1... | collective-permute-start | bytes 393224 | tf_op jit(solution)/shard_map/ppermute | solution.py:165
  6.6 0.0 copy-done
  6.7 1.9 %collective-permute-start = (f32[8,128]{1,0:T(8,128)S(1)}, f32[8,128]{1,0:T(8,128)S(1)}, u32[]{:S(2)}, u32[]{:S(2)}) collective-permute-start(f32[8,128]{1,0:T(8,128)S(1)} %bitcast.7), channel_id=1, source_target_pairs={{0,1},{1,2},{2,3},{3,4},{4,5},{5,6},{6,7},{7,8},{8,9},{9,10},{10,1... | collective-permute-start | bytes 12296 | tf_op jit(solution)/shard_map/ppermute | solution.py:164
  8.6 0.0 slice-start
  8.6 5.7 %collective-permute-done.low = f32[8,128]{1,0:T(8,128)S(1)} collective-permute-done((f32[8,128]{1,0:T(8,128)S(1)}, f32[8,128]{1,0:T(8,128)S(1)}, u32[]{:S(2)}, u32[]{:S(2)}) %collective-permute-start) | collective-permute-done | bytes 4128 | tf_op jit(solution)/shard_map/ppermute | solution.py:164
  14.3 0.0 copy-start.3
  14.3 0.0 collective-permute-done.1.high
  14.3 0.0 copy-start.1
  14.3 0.6 copy-done.3
  14.9 0.0 slice-done
  14.9 0.0 copy-done.1
  14.9 1.3 %collective-permute-start.2 = (f32[2,104,128]{2,1,0:T(8,128)S(1)}, f32[2,104,128]{2,1,0:T(8,128)S(1)}, u32[]{:S(2)}, u32[]{:S(2)}) collective-permute-start(f32[2,104,128]{2,1,0:T(8,128)S(1)} %pad_maximum_fusion), channel_id=1, source_target_pairs={{0,32},{32,64},{64,96},{96,128},{128,160},{160,192},{192,224},{224... | collective-permute-start | bytes 319496 | tf_op jit(solution)/shard_map/ppermute | solution.py:169
  16.2 0.6 %pad_add_fusion.place = s32[2]{0:T(128)} fusion(s32[1]{0:T(128)} %bitcast.1, s32[1]{0:T(128)} %bitcast), kind=kLoop, calls=%fused_computation.1 | loop fusion | flops 2 | bytes 16 | tf_op jit(solution)/shard_map/stack | solution.py:160
  16.8 0.3 collective-permute-done.2.before
  17.2 0.0 copy-start.2
  17.2 0.6 %copy-done.2 = f32[2,104,128]{2,1,0:T(8,128)} copy-done((f32[2,104,128]{2,1,0:T(8,128)}, f32[2,104,128]{2,1,0:T(8,128)S(1)}, u32[]{:S(2)}) %copy-start.2) | copy-done | bytes 106520
  17.8 5.4 %render.1 = (f32[8,4,2,8,128]{4,3,2,1,0:T(8,128)}, f32[8,4,2,8,128]{4,3,2,1,0:T(8,128)}) custom-call(s32[2]{0:T(128)} %pad_add_fusion.place, f32[3]{0:T(128)} %light.1, f32[3]{0:T(128)} %gain.1, f32[3]{0:T(128)} %bias.1, s32[4]{0:T(128)} %shear.1, s32[4]{0:T(128)} %reverse.5, f32[8,64,128]{2,1,0:T(8,128)} %own.1, f32[8,128]{1,0:T(8,128)} %copy-done.3, ...), custom_call_target="tpu_custom_call" | custom-call | tf_op jit(solution)/shard_map/render/pallas_call | solution.py:172
  23.2 8.8 %all-gather = f32[16,4,2,8,128]{4,3,2,1,0:T(8,128)} all-gather(f32[8,4,2,8,128]{4,3,2,1,0:T(8,128)} %get-tuple-element.8), channel_id=2, replica_groups={{0,32},{64,96},{128,160},{192,224},{256,288},{320,352},{384,416},{448,4..., dimensions={0}, use_global_device_ids=true | all-gather | bytes 786432 | tf_op jit(solution)/shard_map/all_gather | solution.py:186
  32.0 1.9 %merge.1 = f32[8,4,2,8,128]{4,3,2,1,0:T(8,128)} custom-call(s32[2]{0:T(128)} %pad_add_fusion.place, s32[4]{0:T(128)} %reverse.5, f32[8,4,2,8,128]{4,3,2,1,0:T(8,128)} %get-tuple-element.7.kept, f32[2,8,4,2,8,128]{5,4,3,2,1,0:T(8,128)} %bitcast.6), custom_call_target="tpu_custom_call" | custom-call | tf_op jit(solution)/shard_map/merge/pallas_call | solution.py:187
  33.9 24.1 %all_to_all.5.slabs = f32[8,4,2,8,128]{4,3,2,1,0:T(8,128)} all-to-all(f32[8,4,2,8,128]{4,3,2,1,0:T(8,128)} %merge.1), channel_id=1, replica_groups={{0,64,128,192,256,320,384,448},{32,96,160,224,288,352,416,480},{1,65,12..., dimensions={0} | all-to-all | bytes 524288 | tf_op jit(solution)/shard_map/all_to_all | solution.py:191
  58.0 1.6 %composite.1 = f32[4,4,4,128]{3,2,1,0:T(4,128)} custom-call(s32[4]{0:T(128)} %reverse.5, f32[8,4,2,8,128]{4,3,2,1,0:T(8,128)} %all_to_all.5.slabs), custom_call_target="tpu_custom_call" | custom-call | tf_op jit(solution)/shard_map/composite/pallas_call | solution.py:192
  (5 shorter events, 0.0 us)
Async XLA Ops:
  0.0 6.6 %copy-start = (f32[8,64,128]{2,1,0:T(8,128)S(1)}, f32[8,64,128]{2,1,0:T(8,128)}, u32[]{:S(2)}) copy-start(f32[8,64,128]{2,1,0:T(8,128)} %own.1) | copy-start | bytes 786436
  1.0 13.3 %collective-permute-start.1 = (f32[8,32,128]{2,1,0:T(8,128)S(1)}, f32[8,32,128]{2,1,0:T(8,128)S(1)}, u32[]{:S(2)}, u32[]{:S(2)}) collective-permute-start(f32[8,32,128]{2,1,0:T(8,128)S(1)} %slice.16), channel_id=1, source_target_pairs={{1,0},{2,1},{3,2},{4,3},{5,4},{6,5},{7,6},{8,7},{9,8},{10,9},{11,1... | collective-permute-start | bytes 393224 | tf_op jit(solution)/shard_map/ppermute | solution.py:165
  6.7 7.6 %collective-permute-start = (f32[8,128]{1,0:T(8,128)S(1)}, f32[8,128]{1,0:T(8,128)S(1)}, u32[]{:S(2)}, u32[]{:S(2)}) collective-permute-start(f32[8,128]{1,0:T(8,128)S(1)} %bitcast.7), channel_id=1, source_target_pairs={{0,1},{1,2},{2,3},{3,4},{4,5},{5,6},{6,7},{7,8},{8,9},{9,10},{10,1... | collective-permute-start | bytes 12296 | tf_op jit(solution)/shard_map/ppermute | solution.py:164
  8.6 6.3 %slice-start = ((f32[8,64,128]{2,1,0:T(8,128)}), f32[2,64,128]{2,1,0:T(8,128)S(1)}, s32[]{:S(2)}) async-start(f32[8,64,128]{2,1,0:T(8,128)} %own.1), calls=%async_computation.1 | async-start | bytes 131072 | tf_op jit(solution)/shard_map/slice | solution.py:167
  14.3 0.6 copy-start.3
  14.3 0.6 %copy-start.1 = (f32[8,32,128]{2,1,0:T(8,128)}, f32[8,32,128]{2,1,0:T(8,128)S(1)}, u32[]{:S(2)}) copy-start(f32[8,32,128]{2,1,0:T(8,128)S(1)} %collective-permute-done.1.high) | copy-start | bytes 393220
  14.9 2.2 %collective-permute-start.2 = (f32[2,104,128]{2,1,0:T(8,128)S(1)}, f32[2,104,128]{2,1,0:T(8,128)S(1)}, u32[]{:S(2)}, u32[]{:S(2)}) collective-permute-start(f32[2,104,128]{2,1,0:T(8,128)S(1)} %pad_maximum_fusion), channel_id=1, source_target_pairs={{0,32},{32,64},{64,96},{96,128},{128,160},{160,192},{192,224},{224... | collective-permute-start | bytes 319496 | tf_op jit(solution)/shard_map/ppermute | solution.py:169
  17.2 0.6 %copy-start.2 = (f32[2,104,128]{2,1,0:T(8,128)}, f32[2,104,128]{2,1,0:T(8,128)S(1)}, u32[]{:S(2)}) copy-start(f32[2,104,128]{2,1,0:T(8,128)S(1)} %collective-permute-done.2.before) | copy-start | bytes 319492

commit v2 on v1

--- a/solution.py
+++ b/solution.py
@@ -17,6 +17,7 @@
 SLABS = PLANES + 1
 CHIPS = GROUPS // 2
 SHARE = ROWS // GROUPS
+LIMIT = 8 * 2**20
 
 
 def opacity_of(optical):
@@ -179,13 +180,15 @@
             pltpu.VMEM((4, SLABS * TALL, COLS), jnp.float32),
             pltpu.SMEM((VIEWS * SLABS,), jnp.int32),
         ],
+        compiler_params=pltpu.CompilerParams(vmem_limit_bytes=LIMIT),
         name="render",
     )(place, light_vector, colour_gain, colour_bias, shear_step, reverse_view, density, low, high, before)
 
     cores = [[2 * chip, 2 * chip + 1] for chip in range(CHIPS)]
     gathered = lax.all_gather(given, "depth", axis=0, axis_index_groups=cores)
     merged = pl.pallas_call(
-        pair_kernel, out_shape=part, in_specs=[SMEM] * 2 + [VMEM] * 2, out_specs=VMEM, name="merge"
+        pair_kernel, out_shape=part, in_specs=[SMEM] * 2 + [VMEM] * 2, out_specs=VMEM,
+        compiler_params=pltpu.CompilerParams(vmem_limit_bytes=LIMIT), name="merge"
     )(place, reverse_view, kept, gathered)
     chips = [[core + 2 * chip for chip in range(CHIPS)] for core in range(2)]
     slabs = lax.all_to_all(merged, "depth", 0, 0, tiled=True, axis_index_groups=chips)
@@ -194,6 +197,7 @@
         out_shape=jax.ShapeDtypeStruct((4, VIEWS, SHARE, COLS), jnp.float32),
         in_specs=[SMEM, VMEM],
         out_specs=VMEM,
+        compiler_params=pltpu.CompilerParams(vmem_limit_bytes=LIMIT),
         name="composite",
     )(reverse_view, slabs)
 

time: 60.2 us -> 53.2 us (0.88)
  blocking collectives: 32.9 us -> 29.4 us
  Pallas kernels: 8.91 us -> 5.94 us
    all_gather x1, blocking collectives: 8.8 us -> 5.67 us  [on_device(): gathered = lax.all_gather(given, 'depth', axis=0, axis_index_groups=cores)]
    pallas_call x1, Pallas kernels: 1.88 us -> 0.6 us  [on_device(): pl.pallas_call(pair_kernel, out_shape=part, in_specs=[SMEM] * 2 + [VMEM]...]
    pallas_call x1, Pallas kernels: 5.42 us -> 4.15 us  [on_device(): pl.pallas_call(render_kernel, out_shape=(part, part), in_specs=[SMEM] * 6...]
    unnamed x8 -> x14, local copies, waits for them, and re-layouts: 1.26 us -> 0.98 us
  transfers between devices with their start and end apart: 3 -> 3, of which waited for: 2 -> 2; matrix products, arithmetic and copies ran while one was open for 1% -> 0% of each run, Pallas kernels for 0% -> 0%
where the time goes in v2:
time: 53.2 us; the launch traced here: 53 us
  blocking collectives  29.4 us (55%)
  starting transfers between devices  8.86 us (17%)
  waiting for transfers between devices  6.48 us (12%)
  Pallas kernels  5.94 us (11%)
  local copies, waits for them, and re-layouts  1.99 us (4%)
    all_to_all x1, blocking collectives, on_device(): lax.all_to_all(merged, 'depth', 0, 0, tiled=True, axis_index_groups=chips)  23.8 us
    all_gather x1, blocking collectives, on_device(): gathered = lax.all_gather(given, 'depth', axis=0, axis_index_groups=cores)  5.67 us
    ppermute x1, waiting for transfers between devices, on_device(): low = lax.ppermute(density[:, ROWS - 1, :], 'height', up)  5.66 us
    ppermute x1, starting transfers between devices, on_device(): high = lax.ppermute(density[:, :SHEAR, :], 'height', down)  5.64 us
    pallas_call x1, Pallas kernels, on_device(): pl.pallas_call(render_kernel, out_shape=(part, part), in_specs=[SMEM] * 6...  4.15 us
    ppermute x1, starting transfers between devices, on_device(): low = lax.ppermute(density[:, ROWS - 1, :], 'height', up)  1.92 us
    ppermute x1, starting transfers between devices, on_device(): lax.ppermute(last, 'depth', [(i, i + 1) for i in range(depths - 1)])  1.3 us
    pallas_call x1, Pallas kernels, on_device(): pl.pallas_call(final_kernel, out_shape=jax.ShapeDtypeStruct((4, VIEWS, SH...  1.2 us
  transfers between devices with their start and end apart: 3, of which 2 were waited for; matrix products, arithmetic and copies ran while one was open for 0% of the time, Pallas kernels for 0%

profile of v2, /device:TPU:6, one launch (start us, length us, event | category | flops | bytes accessed | tf_op | source)
XLA Modules:
  0.0 53.0 jit_solution(13730466348476777245)
XLA Ops:
  0.0 0.0 copy-start
  0.0 1.0 %slice.16 = f32[8,32,128]{2,1,0:T(8,128)S(1)} slice(f32[8,64,128]{2,1,0:T(8,128)} %own.1), slice={[0:8], [0:32], [0:128]} | slice | bytes 262144 | tf_op jit(solution)/shard_map/slice | solution.py:166
  1.0 5.6 %collective-permute-start.1 = (f32[8,32,128]{2,1,0:T(8,128)S(1)}, f32[8,32,128]{2,1,0:T(8,128)S(1)}, u32[]{:S(2)}, u32[]{:S(2)}) collective-permute-start(f32[8,32,128]{2,1,0:T(8,128)S(1)} %slice.16), channel_id=1, source_target_pairs={{1,0},{2,1},{3,2},{4,3},{5,4},{6,5},{7,6},{8,7},{9,8},{10,9},{11,1... | collective-permute-start | bytes 393224 | tf_op jit(solution)/shard_map/ppermute | solution.py:166
  6.6 0.0 copy-done
  6.7 1.9 %collective-permute-start = (f32[8,128]{1,0:T(8,128)S(1)}, f32[8,128]{1,0:T(8,128)S(1)}, u32[]{:S(2)}, u32[]{:S(2)}) collective-permute-start(f32[8,128]{1,0:T(8,128)S(1)} %bitcast.7), channel_id=1, source_target_pairs={{0,1},{1,2},{2,3},{3,4},{4,5},{5,6},{6,7},{7,8},{8,9},{9,10},{10,1... | collective-permute-start | bytes 12296 | tf_op jit(solution)/shard_map/ppermute | solution.py:165
  8.6 0.0 slice-start
  8.6 5.7 %collective-permute-done.low = f32[8,128]{1,0:T(8,128)S(1)} collective-permute-done((f32[8,128]{1,0:T(8,128)S(1)}, f32[8,128]{1,0:T(8,128)S(1)}, u32[]{:S(2)}, u32[]{:S(2)}) %collective-permute-start) | collective-permute-done | bytes 4128 | tf_op jit(solution)/shard_map/ppermute | solution.py:165
  14.3 0.0 collective-permute-done.1.high
  14.3 0.0 slice-done
  14.3 0.0 copy-start.5
  14.3 0.0 copy-start.6
  14.4 1.3 %collective-permute-start.2 = (f32[2,104,128]{2,1,0:T(8,128)S(1)}, f32[2,104,128]{2,1,0:T(8,128)S(1)}, u32[]{:S(2)}, u32[]{:S(2)}) collective-permute-start(f32[2,104,128]{2,1,0:T(8,128)S(1)} %pad_maximum_fusion), channel_id=1, source_target_pairs={{0,32},{32,64},{64,96},{96,128},{128,160},{160,192},{192,224},{224... | collective-permute-start | bytes 319496 | tf_op jit(solution)/shard_map/ppermute | solution.py:170
  15.7 0.0 copy-start.2
  15.7 0.0 copy-start.3
  15.7 0.0 copy-start.4
  15.7 0.1 pad_add_fusion.place
  15.8 0.8 %collective-permute-done.2.before = f32[2,104,128]{2,1,0:T(8,128)S(1)} collective-permute-done((f32[2,104,128]{2,1,0:T(8,128)S(1)}, f32[2,104,128]{2,1,0:T(8,128)S(1)}, u32[]{:S(2)}, u32[]{:S(2)}) %collective-permute-start.2) | collective-permute-done | bytes 106528 | tf_op jit(solution)/shard_map/ppermute | solution.py:170
  16.6 0.0 copy-done.5
  16.6 0.0 copy-done.6
  16.6 0.0 copy-done.2
  16.6 0.0 copy-done.3
  16.6 0.0 copy-done.4
  16.6 0.0 copy-start.1
  16.6 0.9 %copy-done.1 = f32[8,64,128]{2,1,0:T(8,128)S(1)} copy-done((f32[8,64,128]{2,1,0:T(8,128)S(1)}, f32[8,64,128]{2,1,0:T(8,128)}, u32[]{:S(2)}) %copy-start.1) | copy-done | bytes 262168
  17.6 4.2 %render.1 = (f32[8,4,2,8,128]{4,3,2,1,0:T(8,128)S(1)}, f32[8,4,2,8,128]{4,3,2,1,0:T(8,128)S(1)}) custom-call(s32[2]{0:T(128)S(1)} %pad_add_fusion.place, f32[3]{0:T(128)S(1)} %copy-done.3, f32[3]{0:T(128)S(1)} %copy-done.4, f32[3]{0:T(128)S(1)} %copy-done.5, s32[4]{0:T(128)S(1)} %copy-done.6, s32[4]{0:T(128)S(1)} %copy-done.2, f32[8,64,128]{2,1,0:T(8,128)S(1)} %copy-done.1, ...), custom_call_target="tpu_custom_call" | custom-call | tf_op jit(solution)/shard_map/render/pallas_call | solution.py:173
  21.7 5.7 %all-gather = f32[16,4,2,8,128]{4,3,2,1,0:T(8,128)S(1)} all-gather(f32[8,4,2,8,128]{4,3,2,1,0:T(8,128)S(1)} %get-tuple-element.8), channel_id=2, replica_groups={{0,32},{64,96},{128,160},{192,224},{256,288},{320,352},{384,416},{448,4..., dimensions={0}, use_global_device_ids=true | all-gather | bytes 786432 | tf_op jit(solution)/shard_map/all_gather | solution.py:188
  27.4 0.6 %merge.1 = f32[8,4,2,8,128]{4,3,2,1,0:T(8,128)S(1)} custom-call(s32[2]{0:T(128)S(1)} %pad_add_fusion.place, s32[4]{0:T(128)S(1)} %copy-done.2, f32[8,4,2,8,128]{4,3,2,1,0:T(8,128)S(1)} %get-tuple-element.7.kept, f32[2,8,4,2,8,128]{5,4,3,2,1,0:T(8,128)S(1)} %bitcast.6), custom_call_target="tpu_custom_call" | custom-call | tf_op jit(solution)/shard_map/merge/pallas_call | solution.py:189
  28.0 23.8 %all_to_all.5.slabs = f32[8,4,2,8,128]{4,3,2,1,0:T(8,128)S(1)} all-to-all(f32[8,4,2,8,128]{4,3,2,1,0:T(8,128)S(1)} %merge.1), channel_id=1, replica_groups={{0,64,128,192,256,320,384,448},{32,96,160,224,288,352,416,480},{1,65,12..., dimensions={0} | all-to-all | bytes 524288 | tf_op jit(solution)/shard_map/all_to_all | solution.py:194
  51.8 1.2 %composite.1 = f32[4,4,4,128]{3,2,1,0:T(4,128)} custom-call(s32[4]{0:T(128)S(1)} %copy-done.2, f32[8,4,2,8,128]{4,3,2,1,0:T(8,128)S(1)} %all_to_all.5.slabs), custom_call_target="tpu_custom_call" | custom-call | tf_op jit(solution)/shard_map/composite/pallas_call | solution.py:195
  (5 shorter events, 0.0 us)
Async XLA Ops:
  0.0 6.6 %copy-start = (f32[8,64,128]{2,1,0:T(8,128)S(1)}, f32[8,64,128]{2,1,0:T(8,128)}, u32[]{:S(2)}) copy-start(f32[8,64,128]{2,1,0:T(8,128)} %own.1) | copy-start | bytes 786436
  1.0 13.3 %collective-permute-start.1 = (f32[8,32,128]{2,1,0:T(8,128)S(1)}, f32[8,32,128]{2,1,0:T(8,128)S(1)}, u32[]{:S(2)}, u32[]{:S(2)}) collective-permute-start(f32[8,32,128]{2,1,0:T(8,128)S(1)} %slice.16), channel_id=1, source_target_pairs={{1,0},{2,1},{3,2},{4,3},{5,4},{6,5},{7,6},{8,7},{9,8},{10,9},{11,1... | collective-permute-start | bytes 393224 | tf_op jit(solution)/shard_map/ppermute | solution.py:166
  6.7 7.6 %collective-permute-start = (f32[8,128]{1,0:T(8,128)S(1)}, f32[8,128]{1,0:T(8,128)S(1)}, u32[]{:S(2)}, u32[]{:S(2)}) collective-permute-start(f32[8,128]{1,0:T(8,128)S(1)} %bitcast.7), channel_id=1, source_target_pairs={{0,1},{1,2},{2,3},{3,4},{4,5},{5,6},{6,7},{7,8},{8,9},{9,10},{10,1... | collective-permute-start | bytes 12296 | tf_op jit(solution)/shard_map/ppermute | solution.py:165
  8.6 5.7 %slice-start = ((f32[8,64,128]{2,1,0:T(8,128)}), f32[2,64,128]{2,1,0:T(8,128)S(1)}, s32[]{:S(2)}) async-start(f32[8,64,128]{2,1,0:T(8,128)} %own.1), calls=%async_computation.1 | async-start | bytes 131072 | tf_op jit(solution)/shard_map/slice | solution.py:168
  14.3 2.3 %copy-start.5 = (f32[3]{0:T(128)S(1)}, f32[3]{0:T(128)}, u32[]{:S(2)}) copy-start(f32[3]{0:T(128)} %bias.1) | copy-start | bytes 40
  14.3 2.3 %copy-start.6 = (s32[4]{0:T(128)S(1)}, s32[4]{0:T(128)}, u32[]{:S(2)}) copy-start(s32[4]{0:T(128)} %shear.1) | copy-start | bytes 52
  14.4 2.2 %collective-permute-start.2 = (f32[2,104,128]{2,1,0:T(8,128)S(1)}, f32[2,104,128]{2,1,0:T(8,128)S(1)}, u32[]{:S(2)}, u32[]{:S(2)}) collective-permute-start(f32[2,104,128]{2,1,0:T(8,128)S(1)} %pad_maximum_fusion), channel_id=1, source_target_pairs={{0,32},{32,64},{64,96},{96,128},{128,160},{160,192},{192,224},{224... | collective-permute-start | bytes 319496 | tf_op jit(solution)/shard_map/ppermute | solution.py:170
  15.7 0.9 %copy-start.2 = (s32[4]{0:T(128)S(1)}, s32[4]{0:T(128)}, u32[]{:S(2)}) copy-start(s32[4]{0:T(128)} %reverse.5) | copy-start | bytes 52
  15.7 0.9 %copy-start.3 = (f32[3]{0:T(128)S(1)}, f32[3]{0:T(128)}, u32[]{:S(2)}) copy-start(f32[3]{0:T(128)} %light.1) | copy-start | bytes 40
  15.7 0.9 %copy-start.4 = (f32[3]{0:T(128)S(1)}, f32[3]{0:T(128)}, u32[]{:S(2)}) copy-start(f32[3]{0:T(128)} %gain.1) | copy-start | bytes 40
  16.6 1.0 %copy-start.1 = (f32[8,64,128]{2,1,0:T(8,128)S(1)}, f32[8,64,128]{2,1,0:T(8,128)}, u32[]{:S(2)}) copy-start(f32[8,64,128]{2,1,0:T(8,128)} %own.1) | copy-start | bytes 786436

commit v3 on v1

v3 whole, which is shorter than its diff:
```python
import jax
import jax.numpy as jnp
from jax import lax
from jax.experimental import pallas as pl
from jax.experimental.pallas import tpu as pltpu
from jax.sharding import PartitionSpec as P

EXTINCTION = 2.5
SMEM = pl.BlockSpec(memory_space=pltpu.SMEM)
VMEM = pl.BlockSpec(memory_space=pltpu.VMEM)
ANY = pl.BlockSpec(memory_space=pl.ANY)
HBM = pl.BlockSpec(memory_space=pltpu.HBM)
PLANES, ROWS, COLS, SHEAR, VIEWS, GROUPS, BRICKS = 8, 64, 128, 32, 4, 16, 32
TOP = 8
TALL = ROWS + SHEAR
PADDED = TOP + TALL + 8
SLABS = PLANES + 1
CHIPS = GROUPS // 2
SHARE = ROWS // GROUPS
PARAMS = pltpu.CompilerParams(vmem_limit_bytes=8 * 2**20)
LIGHT, GAIN, BIAS, PLAIN, BEYOND, NEXT, NEXT_BEYOND = 0, 3, 6, 9, 10, 11, 12
FRONT, BACK, CORE = 0, 2, 4
FIRST = VIEWS * SLABS


def array(*shape):
    return jax.ShapeDtypeStruct(shape, jnp.float32)


def opacity_of(optical):
    series = 1.0 - optical * (1.0 / 6.0)
    for term in (5.0, 4.0, 3.0, 2.0):
        series = 1.0 - optical * (1.0 / term) * series
    return optical * series


def shade(coefficient, extinction, centre, above, below, before, after):
    lane = lax.broadcasted_iota(jnp.int32, centre.shape, 1)
    tilt_rows = 0.5 * (below - above)
    tilt_depth = 0.5 * (after - before)
    right = jnp.where(lane == COLS - 1, 0.0, pltpu.roll(centre, COLS - 1, 1))
    left = jnp.where(lane == 0, 0.0, pltpu.roll(centre, 1, 1))
    tilt_cols = 0.5 * (right - left)
    slope = coefficient(LIGHT) * tilt_depth + coefficient(LIGHT + 1) * tilt_rows + coefficient(LIGHT + 2) * tilt_cols
    facing = slope * lax.rsqrt(1.0 + tilt_depth * tilt_depth + tilt_rows * tilt_rows + tilt_cols * tilt_cols)
    shading = 0.25 + 1.5 * jnp.maximum(facing, 0.0)
    optical = extinction * (jnp.maximum(centre, 0.0) + jnp.log1p(jnp.exp(-jnp.abs(centre))))
    strength = opacity_of(optical) * shading
    tones = [jax.nn.sigmoid(coefficient(GAIN + i) * centre + coefficient(BIAS + i)) for i in range(3)]
    return [strength * tone for tone in tones] + [optical]


def load_kernel(density, own, low, high, semaphore):
    copy = pltpu.make_async_copy(density, own, semaphore)
    copy.start()
    copy.wait()
    high[...] = own[:, :SHEAR, :]
    for plane in range(PLANES):
        low[plane : plane + 1, :] = own[plane, ROWS - 1 : ROWS, :]


def inner_kernel(*refs):
    arguments, (own, fields, table, masks, starts), scalars, semaphores = refs[:5], refs[5:10], refs[10:15], refs[15]
    copies = [pltpu.make_async_copy(arguments[i], scalars[i], semaphores.at[i]) for i in range(5)]
    for copy in copies:
        copy.start()
    depth, height = lax.axis_index("depth"), lax.axis_index("height")
    for copy in copies:
        copy.wait()
    light, gain, bias, shear, reverse = scalars
    extinction = EXTINCTION / (PLANES * GROUPS)
    beyond = jnp.where(height == BRICKS - 1, 0.0, extinction)
    following = jnp.where(depth == GROUPS - 1, 0.0, extinction)
    both = jnp.where(depth == GROUPS - 1, 0.0, beyond)
    values_of = [ref[i] for ref in (light, gain, bias) for i in range(3)] + [extinction, beyond, following, both]
    for row, scalar in enumerate(values_of):
        table[row : row + 1, :] = jnp.full((1, COLS), scalar, jnp.float32)
    upper = lax.broadcasted_iota(jnp.int32, (8, COLS), 0) < SHARE
    core = depth % 2
    for base, digit in ((FRONT, core), (BACK, 1)):
        for pair in range(VIEWS // 2):
            first = jnp.where(reverse[2 * pair] == digit, 1.0, 0.0)
            second = jnp.where(reverse[2 * pair + 1] == digit, 1.0, 0.0)
            masks[base + pair] = jnp.where(upper, first, second)
    masks[CORE] = jnp.full((8, COLS), core, jnp.float32)
    first = jnp.where(depth == 0, 0, 1)
    starts[FIRST] = first
    for view in range(VIEWS):
        for step in range(SLABS):
            slot = jnp.where(reverse[view] == 1, SLABS - 1 - step, jnp.minimum(first + step, SLABS - 1))
            offset = lax.shift_right_logical((depth * PLANES + slot) * shear[view], 7)
            starts[view * SLABS + step] = slot * TALL + jnp.minimum(offset, SHEAR)

    def plane_of(step, _):
        plane = step + 1
        inner = slice(8, ROWS - 8)
        values = shade(
            lambda row: values_of[row],
            extinction,
            own[plane, inner, :],
            own[plane, 7 : ROWS - 9, :],
            own[plane, 9 : ROWS - 7, :],
            own[plane - 1, inner, :],
            own[plane + 1, inner, :],
        )
        rows = pl.ds(pl.multiple_of(plane * TALL + 8, 8), ROWS - 16)
        for kind in range(4):
            fields[kind, rows, :] = values[kind]
        return 0

    lax.fori_loop(0, PLANES - 2, plane_of, 0)


def join_kernel(own, low, high, table, brick, first):
    del table
    for plane in range(PLANES):
        parts = (
            (0, jnp.broadcast_to(low[plane : plane + 1, :], (8, COLS))),
            (TOP, own[plane]),
            (TOP + ROWS, high[plane]),
            (TOP + TALL, jnp.zeros((8, COLS), jnp.float32)),
        )
        for start, part in parts:
            brick[plane, start : start + part.shape[0], :] = part
            if plane < 2:
                first[plane, start : start + part.shape[0], :] = part


def shade_rows(table, extinction, row, count, plane, before, after, fields, slot):
    start = row + TOP
    values = shade(
        lambda at: table[at : at + 1, :],
        table[extinction : extinction + 1, :],
        plane[start : start + count, :],
        plane[start - 1 : start - 1 + count, :],
        plane[start + 1 : start + 1 + count, :],
        0.0 if before is None else before[start : start + count, :],
        after[start : start + count, :],
    )
    rows = pl.ds(pl.multiple_of(slot * TALL + row, 8), count)
    for kind in range(4):
        fields[kind, rows, :] = values[kind]


def edge_kernel(table, brick, held, fields):
    del held

    def plane_of(step, _):
        plane = step + 1
        refs = (brick.at[plane], brick.at[plane - 1], brick.at[plane + 1], fields, plane)
        shade_rows(table, PLAIN, 0, 8, *refs)
        shade_rows(table, PLAIN, ROWS - 8, 8, *refs)
        shade_rows(table, BEYOND, ROWS, SHEAR, *refs)
        return 0

    lax.fori_loop(0, PLANES - 2, plane_of, 0)


def render_kernel(table, masks, starts_in, brick, coming, held, given, kept, fields, starts, semaphore):
    del held
    copy = pltpu.make_async_copy(starts_in, starts, semaphore)
    copy.start()

    def whole_plane(slot, plane, before, after, own, beyond):
        refs = (plane, before, after, fields, slot)
        shade_rows(table, own, 0, SHEAR, *refs)
        shade_rows(table, own, SHEAR, SHEAR, *refs)
        shade_rows(table, beyond, ROWS, SHEAR, *refs)

    whole_plane(PLANES - 1, brick.at[PLANES - 1], brick.at[PLANES - 2], coming.at[0], PLAIN, BEYOND)
    whole_plane(PLANES, coming.at[0], brick.at[PLANES - 1], coming.at[1], NEXT, NEXT_BEYOND)
    copy.wait()
    leading = starts[FIRST] == 0

    @pl.when(leading)
    def _():
        whole_plane(0, brick.at[0], None, brick.at[1], PLAIN, BEYOND)

    def render(planes):
        upper = lax.broadcasted_iota(jnp.int32, (8, COLS), 0) < SHARE
        odd = masks[CORE] > 0.5

        def tile_of(tile, _):
            for pair in range(VIEWS // 2):
                sums = []
                for view in (2 * pair, 2 * pair + 1):
                    red = green = blue = optical = jnp.zeros((8, COLS), jnp.float32)
                    for step in range(planes):
                        rows = pl.ds(starts[view * SLABS + step] + 8 * tile, 8)
                        through = jnp.exp(-optical)
                        red = red + fields[0, rows, :] * through
                        green = green + fields[1, rows, :] * through
                        blue = blue + fields[2, rows, :] * through
                        optical = optical + fields[3, rows, :]
                    sums.append((red, green, blue, optical))
                for kind in range(4):
                    first, second = sums[0][kind], sums[1][kind]
                    even_rows = jnp.where(upper, first, pltpu.roll(second, SHARE, 0))
                    odd_rows = jnp.where(upper, pltpu.roll(first, SHARE, 0), second)
                    kept[tile, kind, pair] = jnp.where(odd, odd_rows, even_rows)
                    given[tile, kind, pair] = jnp.where(odd, even_rows, odd_rows)
            return 0

        lax.fori_loop(0, ROWS // 8, tile_of, 0)

    @pl.when(leading)
    def _():
        render(SLABS)

    @pl.when(jnp.logical_not(leading))
    def _():
        render(PLANES)


def merge_kernel(masks, kept, gathered, out):
    odd = masks[CORE] > 0.5
    for pair in range(VIEWS // 2):
        mine_front = masks[FRONT + pair] > 0.5

        def merge(chip, _):
            mine = [kept[chip, kind, pair] for kind in range(4)]
            other = [jnp.where(odd, gathered[0, chip, kind, pair], gathered[1, chip, kind, pair]) for kind in range(4)]
            through = jnp.exp(-jnp.where(mine_front, mine[3], other[3]))
            for kind in range(3):
                front = jnp.where(mine_front, mine[kind], other[kind])
                behind = jnp.where(mine_front, other[kind], mine[kind])
                out[chip, kind, pair] = front + through * behind
            out[chip, 3, pair] = mine[3] + other[3]
            return 0

        lax.fori_loop(0, CHIPS, merge, 0, unroll=True)


def final_kernel(masks, slabs, out):
    for pair in range(VIEWS // 2):
        backward = masks[BACK + pair] > 0.5
        optical = [slabs[chip, 3, pair] for chip in range(CHIPS)]
        ahead, behind = [jnp.zeros((8, COLS), jnp.float32)], [jnp.zeros((8, COLS), jnp.float32)]
        for chip in range(CHIPS - 1):
            ahead.append(ahead[-1] + optical[chip])
            behind.append(behind[-1] + optical[CHIPS - 1 - chip])
        total = ahead[-1] + optical[-1]
        sums = [jnp.zeros((8, COLS), jnp.float32)] * 3
        for chip in range(CHIPS):
            through = jnp.exp(-jnp.where(backward, behind[CHIPS - 1 - chip], ahead[chip]))
            sums = [sums[kind] + slabs[chip, kind, pair] * through for kind in range(3)]
        cover = jnp.where(total < 0.0625, opacity_of(total), 1.0 - jnp.exp(-total))
        for kind, value in enumerate((*sums, cover)):
            out[kind, 2 * pair] = value[:SHARE]
            out[kind, 2 * pair + 1] = value[SHARE:]


def kernel(body, name, out_shape, in_specs, out_specs, flops=0, **more):
    estimate = pl.CostEstimate(flops=flops, bytes_accessed=2**20, transcendentals=0)
    return pl.pallas_call(
        body,
        out_shape=out_shape,
        in_specs=in_specs,
        out_specs=out_specs,
        compiler_params=PARAMS,
        cost_estimate=estimate,
        name=name,
        **more,
    )


def on_device(density, light_vector, colour_gain, colour_bias, shear_step, reverse_view):
    heights, depths = lax.axis_size("height"), lax.axis_size("depth")

    own, own_low, own_high = kernel(
        load_kernel,
        "load",
        (array(PLANES, ROWS, COLS), array(PLANES, COLS), array(PLANES, SHEAR, COLS)),
        [HBM],
        (VMEM,) * 3,
        flops=10**9,
        scratch_shapes=[pltpu.SemaphoreType.DMA],
    )(density)
    high = lax.ppermute(own_high, "height", [(i + 1, i) for i in range(heights - 1)])
    low = lax.ppermute(own_low, "height", [(i, i + 1) for i in range(heights - 1)])

    fields, table, masks, starts = kernel(
        inner_kernel,
        "inner",
        (
            array(4, SLABS * TALL, COLS),
            array(16, COLS),
            array(5, 8, COLS),
            jax.ShapeDtypeStruct((64,), jnp.int32),
        ),
        [HBM] * 5 + [VMEM],
        (VMEM, VMEM, VMEM, SMEM),
        flops=10**7,
        scratch_shapes=[pltpu.SMEM((3,), jnp.float32)] * 3
        + [pltpu.SMEM((VIEWS,), jnp.int32)] * 2
        + [pltpu.SemaphoreType.DMA((5,))],
    )(light_vector, colour_gain, colour_bias, shear_step, reverse_view, own)

    brick, first = kernel(
        join_kernel, "join", (array(PLANES, PADDED, COLS), array(2, PADDED, COLS)), [VMEM] * 4, (VMEM,) * 2
    )(own, low, high, table)
    coming = lax.ppermute(first, "depth", [(i + 1, i) for i in range(depths - 1)])

    fields = kernel(
        edge_kernel,
        "edge",
        array(4, SLABS * TALL, COLS),
        [VMEM] * 3,
        VMEM,
        flops=10**7,
        input_output_aliases={2: 0},
    )(table, brick, fields)

    part = array(CHIPS, 4, VIEWS // 2, 8, COLS)
    given, kept, _ = kernel(
        render_kernel,
        "render",
        (part, part, array(4, SLABS * TALL, COLS)),
        [VMEM, VMEM, ANY, VMEM, VMEM, VMEM],
        (VMEM,) * 3,
        input_output_aliases={5: 2},
        scratch_shapes=[pltpu.SMEM((64,), jnp.int32), pltpu.SemaphoreType.DMA],
    )(table, masks, starts, brick, coming, fields)

    cores = [[2 * chip, 2 * chip + 1] for chip in range(CHIPS)]
    gathered = lax.all_gather(given, "depth", axis=0, axis_index_groups=cores)
    merged = kernel(merge_kernel, "merge", part, [VMEM] * 3, VMEM)(masks, kept, gathered)
    chips = [[core + 2 * chip for chip in range(CHIPS)] for core in range(2)]
    slabs = lax.all_to_all(merged, "depth", 0, 0, tiled=True, axis_index_groups=chips)
    return kernel(final_kernel, "composite", array(4, VIEWS, SHARE, COLS), [VMEM] * 2, VMEM)(masks, slabs)


def solution(mesh):
    placed = (P("depth", "height", None), P(), P(), P(), P(), P())
    return jax.shard_map(
        on_device,
        mesh=mesh,
        in_specs=placed,
        out_specs=P(None, None, ("height", "depth"), None),
        check_vma=False,
    )
```

time: 60.2 us -> 46.9 us (0.78)
  blocking collectives: 32.9 us -> 26.9 us
  Pallas kernels: 8.91 us -> 4.59 us
  local copies, waits for them, and re-layouts: 2.27 us -> 1.01 us
  waiting for transfers between devices: 5.98 us -> 5.12 us
  other arithmetic: 0.63 us -> 0 us
    pallas_call x3 -> x7, Pallas kernels: 8.91 us -> 4.59 us  [the longest x1 1.84 us: on_device(): kernel(inner_kernel, 'inner', (array(4, SLABS * TALL, COLS), array(16, CO...]
    all_gather x1, blocking collectives: 8.8 us -> 5.27 us  [on_device(): gathered = lax.all_gather(given, 'depth', axis=0, axis_index_groups=cores)]
    all_to_all x1, blocking collectives: 24.1 us -> 21.6 us  [on_device(): lax.all_to_all(merged, 'depth', 0, 0, tiled=True, axis_index_groups=chips)]
    slice x6 -> x0, local copies, waits for them, and re-layouts: 1.01 us -> none  [the longest x1 0.99 us: on_device(): high = lax.ppermute(density[:, :SHEAR, :], 'height', down)]
    ppermute x3, waiting for transfers between devices: 5.98 us -> 5.12 us  [the longest x1 3.79 us: on_device(): lax.ppermute(own_low, 'height', [(i, i + 1) for i in range(heights - 1)])]
    another operation x1 -> x0, other arithmetic: 0.62 us -> none  [on_device(): place = jnp.stack([depth, height]).astype(jnp.int32)]
    unnamed x8 -> x12, local copies, waits for them, and re-layouts: 1.26 us -> 1.01 us
  transfers between devices with their start and end apart: 3 -> 3, of which waited for: 2 -> 2; matrix products, arithmetic and copies ran while one was open for 1% -> 0% of each run, Pallas kernels for 0% -> 5%
where the time goes in v3:
time: 46.9 us; the launch traced here: 46.6 us
  blocking collectives  26.9 us (57%)
  starting transfers between devices  8.86 us (19%)
  waiting for transfers between devices  5.12 us (11%)
  Pallas kernels  4.59 us (10%)
  local copies, waits for them, and re-layouts  1.01 us (2%)
    all_to_all x1, blocking collectives, on_device(): lax.all_to_all(merged, 'depth', 0, 0, tiled=True, axis_index_groups=chips)  21.6 us
    ppermute x1, starting transfers between devices, on_device(): lax.ppermute(own_high, 'height', [(i + 1, i) for i in range(heights - 1)])  5.64 us
    all_gather x1, blocking collectives, on_device(): gathered = lax.all_gather(given, 'depth', axis=0, axis_index_groups=cores)  5.27 us
    ppermute x1, waiting for transfers between devices, on_device(): lax.ppermute(own_low, 'height', [(i, i + 1) for i in range(heights - 1)])  3.79 us
    ppermute x1, starting transfers between devices, on_device(): lax.ppermute(own_low, 'height', [(i, i + 1) for i in range(heights - 1)])  1.92 us
    pallas_call x1, Pallas kernels, on_device(): kernel(inner_kernel, 'inner', (array(4, SLABS * TALL, COLS), array(16, CO...  1.84 us
    pallas_call x1, Pallas kernels, on_device(): kernel(render_kernel, 'render', (part, part, array(4, SLABS * TALL, COLS)...  1.38 us
    ppermute x1, waiting for transfers between devices, on_device(): lax.ppermute(first, 'depth', [(i + 1, i) for i in range(depths - 1)])  1.33 us
  transfers between devices with their start and end apart: 3, of which 2 were waited for; matrix products, arithmetic and copies ran while one was open for 0% of the time, Pallas kernels for 5%

profile of v3, /device:TPU:6, one launch (start us, length us, event | category | flops | bytes accessed | tf_op | source)
XLA Modules:
  0.0 46.6 jit_solution(4149370495394124587)
XLA Ops:
  0.0 0.0 copy-start.4
  0.0 0.0 copy-start.3
  0.0 0.0 copy-start.2
  0.0 0.0 copy-start.1
  0.0 0.0 copy-start.5
  0.0 1.0 %copy-done.5 = f32[8,64,128]{2,1,0:T(8,128)S(1)} copy-done((f32[8,64,128]{2,1,0:T(8,128)S(1)}, f32[8,64,128]{2,1,0:T(8,128)}, u32[]{:S(2)}) %copy-start.5) | copy-done | bytes 262168
  1.0 0.0 copy-start
  1.1 5.6 %collective-permute-start.1 = (f32[8,32,128]{2,1,0:T(8,128)S(1)}, f32[8,32,128]{2,1,0:T(8,128)S(1)}, u32[]{:S(2)}, u32[]{:S(2)}) collective-permute-start(f32[8,32,128]{2,1,0:T(8,128)S(1)} %get-tuple-element.21), channel_id=1, source_target_pairs={{1,0},{2,1},{3,2},{4,3},{5,4},{6,5},{7,6},{8,7},{9,8},{10,9},{11,1... | collective-permute-start | bytes 393224 | tf_op jit(solution)/shard_map/ppermute | solution.py:279
  6.7 1.9 %collective-permute-start = (f32[8,128]{1,0:T(8,128)S(1)}, f32[8,128]{1,0:T(8,128)S(1)}, u32[]{:S(2)}, u32[]{:S(2)}) collective-permute-start(f32[8,128]{1,0:T(8,128)S(1)} %get-tuple-element.20), channel_id=1, source_target_pairs={{0,1},{1,2},{2,3},{3,4},{4,5},{5,6},{6,7},{7,8},{8,9},{9,10},{10,1... | collective-permute-start | bytes 12296 | tf_op jit(solution)/shard_map/ppermute | solution.py:280
  8.6 0.0 copy-done.4
  8.7 0.0 copy-done.3
  8.7 0.0 copy-done.2
  8.7 0.0 copy-done.1
  8.7 0.0 copy-done
  8.7 1.8 %inner.1 = (f32[4,864,128]{2,1,0:T(8,128)S(1)}, f32[16,128]{1,0:T(8,128)S(1)}, f32[5,8,128]{2,1,0:T(8,128)S(1)}, s32[64]{0:T(128)S(1)}) custom-call(f32[3]{0:T(128)S(1)} %copy-done, f32[3]{0:T(128)S(1)} %copy-done.1, f32[3]{0:T(128)S(1)} %copy-done.2, s32[4]{0:T(128)S(1)} %copy-done.3, s32[4]{0:T(128)S(1)} %copy-done.4, ...), custom_call_target="tpu_custom_call" | custom-call | flops 10000000 | bytes 1048576 | tf_op jit(solution)/shard_map/inner/pallas_call | solution.py:282
  10.5 3.8 %collective-permute-done.low = f32[8,128]{1,0:T(8,128)S(1)} collective-permute-done((f32[8,128]{1,0:T(8,128)S(1)}, f32[8,128]{1,0:T(8,128)S(1)}, u32[]{:S(2)}, u32[]{:S(2)}) %collective-permute-start) | collective-permute-done | bytes 4128 | tf_op jit(solution)/shard_map/ppermute | solution.py:280
  14.3 0.0 collective-permute-done.1.high
  14.4 1.3 %collective-permute-start.2 = (f32[2,112,128]{2,1,0:T(8,128)S(1)}, f32[2,112,128]{2,1,0:T(8,128)S(1)}, u32[]{:S(2)}, u32[]{:S(2)}) collective-permute-start(f32[2,112,128]{2,1,0:T(8,128)S(1)} %get-tuple-element.23), channel_id=1, source_target_pairs={{32,0},{64,32},{96,64},{128,96},{160,128},{192,160},{224,192},{256... | collective-permute-start | bytes 344072 | tf_op jit(solution)/shard_map/ppermute | solution.py:302
  15.7 0.6 %edge.1.held = f32[4,864,128]{2,1,0:T(8,128)S(1)} custom-call(f32[16,128]{1,0:T(8,128)S(1)} %get-tuple-element.18.table, f32[8,112,128]{2,1,0:T(8,128)S(1)} %get-tuple-element.22.brick, f32[4,864,128]{2,1,0:T(8,128)S(1)} %get-tuple-element.24.held), custom_call_target="tpu_custom_call", output_to_operand_aliasing={{}: (2, {})} | custom-call | flops 10000000 | bytes 1048576 | tf_op jit(solution)/shard_map/edge/pallas_call | solution.py:304
  16.3 1.3 %collective-permute-done.2.coming = f32[2,112,128]{2,1,0:T(8,128)S(1)} collective-permute-done((f32[2,112,128]{2,1,0:T(8,128)S(1)}, f32[2,112,128]{2,1,0:T(8,128)S(1)}, u32[]{:S(2)}, u32[]{:S(2)}) %collective-permute-start.2) | collective-permute-done | bytes 114720 | tf_op jit(solution)/shard_map/ppermute | solution.py:302
  17.6 1.4 %render.1 = (f32[8,4,2,8,128]{4,3,2,1,0:T(8,128)S(1)}, f32[8,4,2,8,128]{4,3,2,1,0:T(8,128)S(1)}, f32[4,864,128]{2,1,0:T(8,128)S(1)}) custom-call(f32[16,128]{1,0:T(8,128)S(1)} %get-tuple-element.18.table, f32[5,8,128]{2,1,0:T(8,128)S(1)} %get-tuple-element.17.masks, s32[64]{0:T(128)S(1)} %get-tuple-element.19.starts_in, ...), custom_call_target="tpu_custom_call", output_to_operand_aliasing={{2}: (5, {})} | custom-call | bytes 1048576 | tf_op jit(solution)/shard_map/render/pallas_call | solution.py:315
  19.0 5.3 %all-gather = f32[16,4,2,8,128]{4,3,2,1,0:T(8,128)S(1)} all-gather(f32[8,4,2,8,128]{4,3,2,1,0:T(8,128)S(1)} %get-tuple-element.26), channel_id=2, replica_groups={{0,32},{64,96},{128,160},{192,224},{256,288},{320,352},{384,416},{448,4..., dimensions={0}, use_global_device_ids=true | all-gather | bytes 786432 | tf_op jit(solution)/shard_map/all_gather | solution.py:326
  24.2 0.1 merge.1
  24.3 21.6 %all_to_all.5.slabs = f32[8,4,2,8,128]{4,3,2,1,0:T(8,128)S(1)} all-to-all(f32[8,4,2,8,128]{4,3,2,1,0:T(8,128)S(1)} %merge.1), channel_id=1, replica_groups={{0,64,128,192,256,320,384,448},{32,96,160,224,288,352,416,480},{1,65,12..., dimensions={0} | all-to-all | bytes 524288 | tf_op jit(solution)/shard_map/all_to_all | solution.py:329
  45.9 0.7 %composite.1 = f32[4,4,4,128]{3,2,1,0:T(4,128)} custom-call(f32[5,8,128]{2,1,0:T(8,128)S(1)} %get-tuple-element.17.masks, f32[8,4,2,8,128]{4,3,2,1,0:T(8,128)S(1)} %all_to_all.5.slabs), custom_call_target="tpu_custom_call" | custom-call | bytes 1048576 | tf_op jit(solution)/shard_map/composite/pallas_call | solution.py:330
  (2 shorter events, 0.1 us)
Async XLA Ops:
  0.0 8.6 %copy-start.4 = (s32[4]{0:T(128)S(1)}, s32[4]{0:T(128)}, u32[]{:S(2)}) copy-start(s32[4]{0:T(128)} %refs_4_.1) | copy-start | bytes 52
  0.0 8.7 %copy-start.3 = (s32[4]{0:T(128)S(1)}, s32[4]{0:T(128)}, u32[]{:S(2)}) copy-start(s32[4]{0:T(128)} %refs_3_.1) | copy-start | bytes 52
  0.0 8.7 %copy-start.2 = (f32[3]{0:T(128)S(1)}, f32[3]{0:T(128)}, u32[]{:S(2)}) copy-start(f32[3]{0:T(128)} %refs_2_.1) | copy-start | bytes 40
  0.0 8.7 %copy-start.1 = (f32[3]{0:T(128)S(1)}, f32[3]{0:T(128)}, u32[]{:S(2)}) copy-start(f32[3]{0:T(128)} %refs_1_.1) | copy-start | bytes 40
  0.0 1.0 %copy-start.5 = (f32[8,64,128]{2,1,0:T(8,128)S(1)}, f32[8,64,128]{2,1,0:T(8,128)}, u32[]{:S(2)}) copy-start(f32[8,64,128]{2,1,0:T(8,128)} %density.1) | copy-start | bytes 786436
  1.0 7.7 %copy-start = (f32[3]{0:T(128)S(1)}, f32[3]{0:T(128)}, u32[]{:S(2)}) copy-start(f32[3]{0:T(128)} %refs_0_.1) | copy-start | bytes 40
  1.1 13.3 %collective-permute-start.1 = (f32[8,32,128]{2,1,0:T(8,128)S(1)}, f32[8,32,128]{2,1,0:T(8,128)S(1)}, u32[]{:S(2)}, u32[]{:S(2)}) collective-permute-start(f32[8,32,128]{2,1,0:T(8,128)S(1)} %get-tuple-element.21), channel_id=1, source_target_pairs={{1,0},{2,1},{3,2},{4,3},{5,4},{6,5},{7,6},{8,7},{9,8},{10,9},{11,1... | collective-permute-start | bytes 393224 | tf_op jit(solution)/shard_map/ppermute | solution.py:279
  6.7 7.6 %collective-permute-start = (f32[8,128]{1,0:T(8,128)S(1)}, f32[8,128]{1,0:T(8,128)S(1)}, u32[]{:S(2)}, u32[]{:S(2)}) collective-permute-start(f32[8,128]{1,0:T(8,128)S(1)} %get-tuple-element.20), channel_id=1, source_target_pairs={{0,1},{1,2},{2,3},{3,4},{4,5},{5,6},{6,7},{7,8},{8,9},{9,10},{10,1... | collective-permute-start | bytes 12296 | tf_op jit(solution)/shard_map/ppermute | solution.py:280
  14.4 3.2 %collective-permute-start.2 = (f32[2,112,128]{2,1,0:T(8,128)S(1)}, f32[2,112,128]{2,1,0:T(8,128)S(1)}, u32[]{:S(2)}, u32[]{:S(2)}) collective-permute-start(f32[2,112,128]{2,1,0:T(8,128)S(1)} %get-tuple-element.23), channel_id=1, source_target_pairs={{32,0},{64,32},{96,64},{128,96},{160,128},{192,160},{224,192},{256... | collective-permute-start | bytes 344072 | tf_op jit(solution)/shard_map/ppermute | solution.py:302

commit v4 on v3

--- a/solution.py
+++ b/solution.py
@@ -50,17 +50,16 @@
     return [strength * tone for tone in tones] + [optical]
 
 
-def load_kernel(density, own, low, high, semaphore):
+def load_kernel(density, own, low, semaphore):
     copy = pltpu.make_async_copy(density, own, semaphore)
     copy.start()
     copy.wait()
-    high[...] = own[:, :SHEAR, :]
     for plane in range(PLANES):
         low[plane : plane + 1, :] = own[plane, ROWS - 1 : ROWS, :]
 
 
-def inner_kernel(*refs):
-    arguments, (own, fields, table, masks, starts), scalars, semaphores = refs[:5], refs[5:10], refs[10:15], refs[15]
+def table_kernel(*refs):
+    arguments, (table, masks, starts), scalars, semaphores = refs[:5], refs[5:8], refs[8:13], refs[13]
     copies = [pltpu.make_async_copy(arguments[i], scalars[i], semaphores.at[i]) for i in range(5)]
     for copy in copies:
         copy.start()
@@ -72,9 +71,9 @@
     beyond = jnp.where(height == BRICKS - 1, 0.0, extinction)
     following = jnp.where(depth == GROUPS - 1, 0.0, extinction)
     both = jnp.where(depth == GROUPS - 1, 0.0, beyond)
-    values_of = [ref[i] for ref in (light, gain, bias) for i in range(3)] + [extinction, beyond, following, both]
-    for row, scalar in enumerate(values_of):
-        table[row : row + 1, :] = jnp.full((1, COLS), scalar, jnp.float32)
+    values = [ref[i] for ref in (light, gain, bias) for i in range(3)] + [extinction, beyond, following, both]
+    for row, value in enumerate(values):
+        table[row : row + 1, :] = jnp.full((1, COLS), value, jnp.float32)
     upper = lax.broadcasted_iota(jnp.int32, (8, COLS), 0) < SHARE
     core = depth % 2
     for base, digit in ((FRONT, core), (BACK, 1)):
@@ -91,28 +90,40 @@
             offset = lax.shift_right_logical((depth * PLANES + slot) * shear[view], 7)
             starts[view * SLABS + step] = slot * TALL + jnp.minimum(offset, SHEAR)
 
+
+def cut_kernel(own, low, table, high):
+    del low, table
+    high[...] = own[:, :SHEAR, :]
+
+
+def inner_kernel(table, own, low, fields):
+    top = lax.broadcasted_iota(jnp.int32, (8, COLS), 0) == 0
+
     def plane_of(step, _):
         plane = step + 1
-        inner = slice(8, ROWS - 8)
-        values = shade(
-            lambda row: values_of[row],
-            extinction,
-            own[plane, inner, :],
-            own[plane, 7 : ROWS - 9, :],
-            own[plane, 9 : ROWS - 7, :],
-            own[plane - 1, inner, :],
-            own[plane + 1, inner, :],
-        )
-        rows = pl.ds(pl.multiple_of(plane * TALL + 8, 8), ROWS - 16)
-        for kind in range(4):
-            fields[kind, rows, :] = values[kind]
+        for inner, above in (
+            (slice(0, 8), jnp.where(top, low[pl.ds(plane, 1), :], pltpu.roll(own[plane, :8, :], 1, 0))),
+            (slice(8, ROWS - 8), own[plane, 7 : ROWS - 9, :]),
+        ):
+            values = shade(
+                lambda at: table[at : at + 1, :],
+                table[PLAIN : PLAIN + 1, :],
+                own[plane, inner, :],
+                above,
+                own[plane, inner.start + 1 : inner.stop + 1, :],
+                own[plane - 1, inner, :],
+                own[plane + 1, inner, :],
+            )
+            rows = pl.ds(pl.multiple_of(plane * TALL + inner.start, 8), inner.stop - inner.start)
+            for kind in range(4):
+                fields[kind, rows, :] = values[kind]
         return 0
 
     lax.fori_loop(0, PLANES - 2, plane_of, 0)
 
 
-def join_kernel(own, low, high, table, brick, first):
-    del table
+def join_kernel(own, low, high, held, brick, first):
+    del held
     for plane in range(PLANES):
         parts = (
             (0, jnp.broadcast_to(low[plane : plane + 1, :], (8, COLS))),
@@ -148,7 +159,6 @@
     def plane_of(step, _):
         plane = step + 1
         refs = (brick.at[plane], brick.at[plane - 1], brick.at[plane + 1], fields, plane)
-        shade_rows(table, PLAIN, 0, 8, *refs)
         shade_rows(table, PLAIN, ROWS - 8, 8, *refs)
         shade_rows(table, BEYOND, ROWS, SHEAR, *refs)
         return 0
@@ -267,38 +277,36 @@
 def on_device(density, light_vector, colour_gain, colour_bias, shear_step, reverse_view):
     heights, depths = lax.axis_size("height"), lax.axis_size("depth")
 
-    own, own_low, own_high = kernel(
+    own, own_low = kernel(
         load_kernel,
         "load",
-        (array(PLANES, ROWS, COLS), array(PLANES, COLS), array(PLANES, SHEAR, COLS)),
+        (array(PLANES, ROWS, COLS), array(PLANES, COLS)),
         [HBM],
-        (VMEM,) * 3,
+        (VMEM,) * 2,
         flops=10**9,
         scratch_shapes=[pltpu.SemaphoreType.DMA],
     )(density)
-    high = lax.ppermute(own_high, "height", [(i + 1, i) for i in range(heights - 1)])
     low = lax.ppermute(own_low, "height", [(i, i + 1) for i in range(heights - 1)])
-
-    fields, table, masks, starts = kernel(
-        inner_kernel,
-        "inner",
-        (
-            array(4, SLABS * TALL, COLS),
-            array(16, COLS),
-            array(5, 8, COLS),
-            jax.ShapeDtypeStruct((64,), jnp.int32),
-        ),
-        [HBM] * 5 + [VMEM],
-        (VMEM, VMEM, VMEM, SMEM),
+    table, masks, starts = kernel(
+        table_kernel,
+        "table",
+        (array(16, COLS), array(5, 8, COLS), jax.ShapeDtypeStruct((64,), jnp.int32)),
+        [HBM] * 5,
+        (VMEM, VMEM, SMEM),
         flops=10**7,
         scratch_shapes=[pltpu.SMEM((3,), jnp.float32)] * 3
         + [pltpu.SMEM((VIEWS,), jnp.int32)] * 2
         + [pltpu.SemaphoreType.DMA((5,))],
-    )(light_vector, colour_gain, colour_bias, shear_step, reverse_view, own)
+    )(light_vector, colour_gain, colour_bias, shear_step, reverse_view)
+    own_high = kernel(cut_kernel, "cut", array(PLANES, SHEAR, COLS), [VMEM] * 3, VMEM)(own, low, table)
+    high = lax.ppermute(own_high, "height", [(i + 1, i) for i in range(heights - 1)])
+    fields = kernel(
+        inner_kernel, "inner", array(4, SLABS * TALL, COLS), [VMEM] * 3, VMEM, flops=10**7
+    )(table, own, low)
 
     brick, first = kernel(
         join_kernel, "join", (array(PLANES, PADDED, COLS), array(2, PADDED, COLS)), [VMEM] * 4, (VMEM,) * 2
-    )(own, low, high, table)
+    )(own, low, high, fields)
     coming = lax.ppermute(first, "depth", [(i + 1, i) for i in range(depths - 1)])
 
     fields = kernel(

time: 46.9 us -> 48.2 us (1.028)
  waiting for transfers between devices: 5.12 us -> 6.76 us
    ppermute x1, waiting for transfers between devices: 0.01 us -> 2.69 us  [on_device(): lax.ppermute(own_high, 'height', [(i + 1, i) for i in range(heights - 1)])]
    ppermute x1, starting transfers between devices: 5.64 us -> 3.53 us  [on_device(): lax.ppermute(own_high, 'height', [(i + 1, i) for i in range(heights - 1)])]
    ppermute x1, starting transfers between devices: 1.92 us -> 3.62 us  [on_device(): lax.ppermute(own_low, 'height', [(i, i + 1) for i in range(heights - 1)])]
    ppermute x1, waiting for transfers between devices: 3.79 us -> 2.73 us  [on_device(): lax.ppermute(own_low, 'height', [(i, i + 1) for i in range(heights - 1)])]
    pallas_call x1 -> x3, Pallas kernels: 1.84 us -> 1.96 us  [the longest x1 1.33 us: on_device(): kernel(table_kernel, 'table', (array(16, COLS), array(5, 8, COLS), jax.Sh...]
  transfers between devices with their start and end apart: 3 -> 3, of which waited for: 2 -> 3; matrix products, arithmetic and copies ran while one was open for 0% -> 0% of each run, Pallas kernels for 5% -> 5%
where the time goes in v4:
time: 48.2 us; the launch traced here: 47.9 us
  blocking collectives  26.9 us (56%)
  starting transfers between devices  8.44 us (18%)
  waiting for transfers between devices  6.76 us (14%)
  Pallas kernels  4.71 us (10%)
  local copies, waits for them, and re-layouts  0.97 us (2%)
    all_to_all x1, blocking collectives, on_device(): lax.all_to_all(merged, 'depth', 0, 0, tiled=True, axis_index_groups=chips)  21.6 us
    all_gather x1, blocking collectives, on_device(): gathered = lax.all_gather(given, 'depth', axis=0, axis_index_groups=cores)  5.27 us
    ppermute x1, starting transfers between devices, on_device(): lax.ppermute(own_low, 'height', [(i, i + 1) for i in range(heights - 1)])  3.62 us
    ppermute x1, starting transfers between devices, on_device(): lax.ppermute(own_high, 'height', [(i + 1, i) for i in range(heights - 1)])  3.53 us
    ppermute x1, waiting for transfers between devices, on_device(): lax.ppermute(own_low, 'height', [(i, i + 1) for i in range(heights - 1)])  2.73 us
    ppermute x1, waiting for transfers between devices, on_device(): lax.ppermute(own_high, 'height', [(i + 1, i) for i in range(heights - 1)])  2.69 us
    pallas_call x1, Pallas kernels, on_device(): kernel(render_kernel, 'render', (part, part, array(4, SLABS * TALL, COLS)...  1.38 us
    ppermute x1, waiting for transfers between devices, on_device(): lax.ppermute(first, 'depth', [(i + 1, i) for i in range(depths - 1)])  1.34 us
  transfers between devices with their start and end apart: 3, of which 3 were waited for; matrix products, arithmetic and copies ran while one was open for 0% of the time, Pallas kernels for 5%

profile of v4, /device:TPU:6, one launch (start us, length us, event | category | flops | bytes accessed | tf_op | source)
XLA Modules:
  0.0 47.9 jit_solution(905519038990593996)
XLA Ops:
  0.0 0.0 copy-start
  0.0 0.9 %copy-done = f32[8,64,128]{2,1,0:T(8,128)S(1)} copy-done((f32[8,64,128]{2,1,0:T(8,128)S(1)}, f32[8,64,128]{2,1,0:T(8,128)}, u32[]{:S(2)}) %copy-start) | copy-done | bytes 262168
  1.0 0.0 copy-start.1
  1.0 0.0 copy-start.2
  1.0 0.0 copy-start.3
  1.0 0.0 copy-start.4
  1.0 0.0 copy-start.5
  1.0 3.6 %collective-permute-start = (f32[8,128]{1,0:T(8,128)S(1)}, f32[8,128]{1,0:T(8,128)S(1)}, u32[]{:S(2)}, u32[]{:S(2)}) collective-permute-start(f32[8,128]{1,0:T(8,128)S(1)} %get-tuple-element.18), channel_id=1, source_target_pairs={{0,1},{1,2},{2,3},{3,4},{4,5},{5,6},{6,7},{7,8},{8,9},{9,10},{10,1... | collective-permute-start | bytes 12296 | tf_op jit(solution)/shard_map/ppermute | solution.py:289
  4.6 0.0 copy-done.1
  4.7 0.0 copy-done.2
  4.7 0.0 copy-done.3
  4.7 0.0 copy-done.4
  4.7 0.0 copy-done.5
  4.7 1.3 %table.1 = (f32[16,128]{1,0:T(8,128)S(1)}, f32[5,8,128]{2,1,0:T(8,128)S(1)}, s32[64]{0:T(128)S(1)}) custom-call(f32[3]{0:T(128)S(1)} %copy-done.1, f32[3]{0:T(128)S(1)} %copy-done.2, f32[3]{0:T(128)S(1)} %copy-done.3, s32[4]{0:T(128)S(1)} %copy-done.4, s32[4]{0:T(128)S(1)} %copy-done.5), custom_call_target="tpu_custom_call" | custom-call | flops 10000000 | bytes 1048576 | tf_op jit(solution)/shard_map/table/pallas_call | solution.py:290
  6.0 2.7 %collective-permute-done.low = f32[8,128]{1,0:T(8,128)S(1)} collective-permute-done((f32[8,128]{1,0:T(8,128)S(1)}, f32[8,128]{1,0:T(8,128)S(1)}, u32[]{:S(2)}, u32[]{:S(2)}) %collective-permute-start) | collective-permute-done | bytes 4128 | tf_op jit(solution)/shard_map/ppermute | solution.py:289
  8.8 3.5 %collective-permute-start.1 = (f32[8,32,128]{2,1,0:T(8,128)S(1)}, f32[8,32,128]{2,1,0:T(8,128)S(1)}, u32[]{:S(2)}, u32[]{:S(2)}) collective-permute-start(f32[8,32,128]{2,1,0:T(8,128)S(1)} %cut.1), channel_id=1, source_target_pairs={{1,0},{2,1},{3,2},{4,3},{5,4},{6,5},{7,6},{8,7},{9,8},{10,9},{11,1... | collective-permute-start | bytes 393224 | tf_op jit(solution)/shard_map/ppermute | solution.py:302
  12.3 0.6 %inner.1.held = f32[4,864,128]{2,1,0:T(8,128)S(1)} custom-call(f32[16,128]{1,0:T(8,128)S(1)} %get-tuple-element.15.table, f32[8,64,128]{2,1,0:T(8,128)S(1)} %get-tuple-element.17.own, f32[8,128]{1,0:T(8,128)S(1)} %collective-permute-done.low), custom_call_target="tpu_custom_call" | custom-call | flops 10000000 | bytes 1048576 | tf_op jit(solution)/shard_map/inner/pallas_call | solution.py:303
  12.9 2.7 %collective-permute-done.1.high = f32[8,32,128]{2,1,0:T(8,128)S(1)} collective-permute-done((f32[8,32,128]{2,1,0:T(8,128)S(1)}, f32[8,32,128]{2,1,0:T(8,128)S(1)}, u32[]{:S(2)}, u32[]{:S(2)}) %collective-permute-start.1) | collective-permute-done | bytes 131104 | tf_op jit(solution)/shard_map/ppermute | solution.py:302
  15.7 1.3 %collective-permute-start.2 = (f32[2,112,128]{2,1,0:T(8,128)S(1)}, f32[2,112,128]{2,1,0:T(8,128)S(1)}, u32[]{:S(2)}, u32[]{:S(2)}) collective-permute-start(f32[2,112,128]{2,1,0:T(8,128)S(1)} %get-tuple-element.20), channel_id=1, source_target_pairs={{32,0},{64,32},{96,64},{128,96},{160,128},{192,160},{224,192},{256... | collective-permute-start | bytes 344072 | tf_op jit(solution)/shard_map/ppermute | solution.py:310
  17.0 0.6 %edge.1.held = f32[4,864,128]{2,1,0:T(8,128)S(1)} custom-call(f32[16,128]{1,0:T(8,128)S(1)} %get-tuple-element.15.table, f32[8,112,128]{2,1,0:T(8,128)S(1)} %get-tuple-element.19.brick, f32[4,864,128]{2,1,0:T(8,128)S(1)} %inner.1.held), custom_call_target="tpu_custom_call", output_to_operand_aliasing={{}: (2, {})} | custom-call | flops 10000000 | bytes 1048576 | tf_op jit(solution)/shard_map/edge/pallas_call | solution.py:312
  17.6 1.3 %collective-permute-done.2.coming = f32[2,112,128]{2,1,0:T(8,128)S(1)} collective-permute-done((f32[2,112,128]{2,1,0:T(8,128)S(1)}, f32[2,112,128]{2,1,0:T(8,128)S(1)}, u32[]{:S(2)}, u32[]{:S(2)}) %collective-permute-start.2) | collective-permute-done | bytes 114720 | tf_op jit(solution)/shard_map/ppermute | solution.py:310
  18.9 1.4 %render.1 = (f32[8,4,2,8,128]{4,3,2,1,0:T(8,128)S(1)}, f32[8,4,2,8,128]{4,3,2,1,0:T(8,128)S(1)}, f32[4,864,128]{2,1,0:T(8,128)S(1)}) custom-call(f32[16,128]{1,0:T(8,128)S(1)} %get-tuple-element.15.table, f32[5,8,128]{2,1,0:T(8,128)S(1)} %get-tuple-element.14.masks, s32[64]{0:T(128)S(1)} %get-tuple-element.16.starts_in, ...), custom_call_target="tpu_custom_call", output_to_operand_aliasing={{2}: (5, {})} | custom-call | bytes 1048576 | tf_op jit(solution)/shard_map/render/pallas_call | solution.py:323
  20.3 5.3 %all-gather = f32[16,4,2,8,128]{4,3,2,1,0:T(8,128)S(1)} all-gather(f32[8,4,2,8,128]{4,3,2,1,0:T(8,128)S(1)} %get-tuple-element.22), channel_id=2, replica_groups={{0,32},{64,96},{128,160},{192,224},{256,288},{320,352},{384,416},{448,4..., dimensions={0}, use_global_device_ids=true | all-gather | bytes 786432 | tf_op jit(solution)/shard_map/all_gather | solution.py:334
  25.6 0.1 merge.1
  25.6 21.6 %all_to_all.5.slabs = f32[8,4,2,8,128]{4,3,2,1,0:T(8,128)S(1)} all-to-all(f32[8,4,2,8,128]{4,3,2,1,0:T(8,128)S(1)} %merge.1), channel_id=1, replica_groups={{0,64,128,192,256,320,384,448},{32,96,160,224,288,352,416,480},{1,65,12..., dimensions={0} | all-to-all | bytes 524288 | tf_op jit(solution)/shard_map/all_to_all | solution.py:337
  47.2 0.7 %composite.1 = f32[4,4,4,128]{3,2,1,0:T(4,128)} custom-call(f32[5,8,128]{2,1,0:T(8,128)S(1)} %get-tuple-element.14.masks, f32[8,4,2,8,128]{4,3,2,1,0:T(8,128)S(1)} %all_to_all.5.slabs), custom_call_target="tpu_custom_call" | custom-call | bytes 1048576 | tf_op jit(solution)/shard_map/composite/pallas_call | solution.py:338
  (3 shorter events, 0.1 us)
Async XLA Ops:
  0.0 0.9 %copy-start = (f32[8,64,128]{2,1,0:T(8,128)S(1)}, f32[8,64,128]{2,1,0:T(8,128)}, u32[]{:S(2)}) copy-start(f32[8,64,128]{2,1,0:T(8,128)} %density.1) | copy-start | bytes 786436
  1.0 3.7 %copy-start.1 = (f32[3]{0:T(128)S(1)}, f32[3]{0:T(128)}, u32[]{:S(2)}) copy-start(f32[3]{0:T(128)} %refs_0_.1) | copy-start | bytes 40
  1.0 3.7 %copy-start.2 = (f32[3]{0:T(128)S(1)}, f32[3]{0:T(128)}, u32[]{:S(2)}) copy-start(f32[3]{0:T(128)} %refs_1_.1) | copy-start | bytes 40
  1.0 3.7 %copy-start.3 = (f32[3]{0:T(128)S(1)}, f32[3]{0:T(128)}, u32[]{:S(2)}) copy-start(f32[3]{0:T(128)} %refs_2_.1) | copy-start | bytes 40
  1.0 3.7 %copy-start.4 = (s32[4]{0:T(128)S(1)}, s32[4]{0:T(128)}, u32[]{:S(2)}) copy-start(s32[4]{0:T(128)} %refs_3_.1) | copy-start | bytes 52
  1.0 3.7 %copy-start.5 = (s32[4]{0:T(128)S(1)}, s32[4]{0:T(128)}, u32[]{:S(2)}) copy-start(s32[4]{0:T(128)} %refs_4_.1) | copy-start | bytes 52
  1.0 7.7 %collective-permute-start = (f32[8,128]{1,0:T(8,128)S(1)}, f32[8,128]{1,0:T(8,128)S(1)}, u32[]{:S(2)}, u32[]{:S(2)}) collective-permute-start(f32[8,128]{1,0:T(8,128)S(1)} %get-tuple-element.18), channel_id=1, source_target_pairs={{0,1},{1,2},{2,3},{3,4},{4,5},{5,6},{6,7},{7,8},{8,9},{9,10},{10,1... | collective-permute-start | bytes 12296 | tf_op jit(solution)/shard_map/ppermute | solution.py:289
  8.8 6.9 %collective-permute-start.1 = (f32[8,32,128]{2,1,0:T(8,128)S(1)}, f32[8,32,128]{2,1,0:T(8,128)S(1)}, u32[]{:S(2)}, u32[]{:S(2)}) collective-permute-start(f32[8,32,128]{2,1,0:T(8,128)S(1)} %cut.1), channel_id=1, source_target_pairs={{1,0},{2,1},{3,2},{4,3},{5,4},{6,5},{7,6},{8,7},{9,8},{10,9},{11,1... | collective-permute-start | bytes 393224 | tf_op jit(solution)/shard_map/ppermute | solution.py:302
  15.7 3.2 %collective-permute-start.2 = (f32[2,112,128]{2,1,0:T(8,128)S(1)}, f32[2,112,128]{2,1,0:T(8,128)S(1)}, u32[]{:S(2)}, u32[]{:S(2)}) collective-permute-start(f32[2,112,128]{2,1,0:T(8,128)S(1)} %get-tuple-element.20), channel_id=1, source_target_pairs={{32,0},{64,32},{96,64},{128,96},{160,128},{192,160},{224,192},{256... | collective-permute-start | bytes 344072 | tf_op jit(solution)/shard_map/ppermute | solution.py:310

commit v5 on v3

--- a/solution.py
+++ b/solution.py
@@ -60,7 +60,7 @@
 
 
 def inner_kernel(*refs):
-    arguments, (own, fields, table, masks, starts), scalars, semaphores = refs[:5], refs[5:10], refs[10:15], refs[15]
+    arguments, (own, low, fields, table, masks, starts), scalars, semaphores = refs[:5], refs[5:11], refs[11:16], refs[16]
     copies = [pltpu.make_async_copy(arguments[i], scalars[i], semaphores.at[i]) for i in range(5)]
     for copy in copies:
         copy.start()
@@ -93,20 +93,25 @@
 
     def plane_of(step, _):
         plane = step + 1
-        inner = slice(8, ROWS - 8)
-        values = shade(
-            lambda row: values_of[row],
-            extinction,
-            own[plane, inner, :],
-            own[plane, 7 : ROWS - 9, :],
-            own[plane, 9 : ROWS - 7, :],
-            own[plane - 1, inner, :],
-            own[plane + 1, inner, :],
-        )
-        rows = pl.ds(pl.multiple_of(plane * TALL + 8, 8), ROWS - 16)
-        for kind in range(4):
-            fields[kind, rows, :] = values[kind]
+        for inner, above in (
+            (slice(0, 8), jnp.where(top, low[pl.ds(plane, 1), :], pltpu.roll(own[plane, :8, :], 1, 0))),
+            (slice(8, ROWS - 8), own[plane, 7 : ROWS - 9, :]),
+        ):
+            values = shade(
+                lambda row: values_of[row],
+                extinction,
+                own[plane, inner, :],
+                above,
+                own[plane, inner.start + 1 : inner.stop + 1, :],
+                own[plane - 1, inner, :],
+                own[plane + 1, inner, :],
+            )
+            rows = pl.ds(pl.multiple_of(plane * TALL + inner.start, 8), inner.stop - inner.start)
+            for kind in range(4):
+                fields[kind, rows, :] = values[kind]
         return 0
+
+    top = lax.broadcasted_iota(jnp.int32, (8, COLS), 0) == 0
 
     lax.fori_loop(0, PLANES - 2, plane_of, 0)
 
@@ -148,7 +153,6 @@
     def plane_of(step, _):
         plane = step + 1
         refs = (brick.at[plane], brick.at[plane - 1], brick.at[plane + 1], fields, plane)
-        shade_rows(table, PLAIN, 0, 8, *refs)
         shade_rows(table, PLAIN, ROWS - 8, 8, *refs)
         shade_rows(table, BEYOND, ROWS, SHEAR, *refs)
         return 0
@@ -288,13 +292,13 @@
             array(5, 8, COLS),
             jax.ShapeDtypeStruct((64,), jnp.int32),
         ),
-        [HBM] * 5 + [VMEM],
+        [HBM] * 5 + [VMEM] * 2,
         (VMEM, VMEM, VMEM, SMEM),
-        flops=10**7,
+        flops=10**11,
         scratch_shapes=[pltpu.SMEM((3,), jnp.float32)] * 3
         + [pltpu.SMEM((VIEWS,), jnp.int32)] * 2
         + [pltpu.SemaphoreType.DMA((5,))],
-    )(light_vector, colour_gain, colour_bias, shear_step, reverse_view, own)
+    )(light_vector, colour_gain, colour_bias, shear_step, reverse_view, own, low)
 
     brick, first = kernel(
         join_kernel, "join", (array(PLANES, PADDED, COLS), array(2, PADDED, COLS)), [VMEM] * 4, (VMEM,) * 2

time: 46.9 us -> 46.4 us (0.989)
  the two profiles are of different devices: /device:TPU:6 before, /device:TPU:25 now
where the time goes in v5:
time: 46.4 us; the launch traced here: 46.2 us
  blocking collectives  23.4 us (50%)
  starting transfers between devices  10.3 us (22%)
  waiting for transfers between devices  6.93 us (15%)
  Pallas kernels  4.42 us (10%)
  local copies, waits for them, and re-layouts  0.97 us (2%)
    all_to_all x1, blocking collectives, on_device(): lax.all_to_all(merged, 'depth', 0, 0, tiled=True, axis_index_groups=chips)  21.2 us
    ppermute x1, starting transfers between devices, on_device(): lax.ppermute(own_low, 'height', [(i, i + 1) for i in range(heights - 1)])  4.42 us
    ppermute x1, starting transfers between devices, on_device(): lax.ppermute(first, 'depth', [(i + 1, i) for i in range(depths - 1)])  4.01 us
    ppermute x1, waiting for transfers between devices, on_device(): lax.ppermute(first, 'depth', [(i + 1, i) for i in range(depths - 1)])  3.86 us
    ppermute x1, waiting for transfers between devices, on_device(): lax.ppermute(own_high, 'height', [(i + 1, i) for i in range(heights - 1)])  3.07 us
    all_gather x1, blocking collectives, on_device(): gathered = lax.all_gather(given, 'depth', axis=0, axis_index_groups=cores)  2.18 us
    ppermute x1, starting transfers between devices, on_device(): lax.ppermute(own_high, 'height', [(i + 1, i) for i in range(heights - 1)])  1.92 us
    pallas_call x1, Pallas kernels, on_device(): kernel(inner_kernel, 'inner', (array(4, SLABS * TALL, COLS), array(16, CO...  1.86 us
  transfers between devices with their start and end apart: 3, of which 2 were waited for; matrix products, arithmetic and copies ran while one was open for 0% of the time, Pallas kernels for 5%

profile of v5, /device:TPU:25, one launch (start us, length us, event | category | flops | bytes accessed | tf_op | source)
XLA Modules:
  0.0 46.2 jit_solution(12545643943440023595)
XLA Ops:
  0.0 0.0 copy-start
  0.0 0.9 %copy-done = f32[8,64,128]{2,1,0:T(8,128)S(1)} copy-done((f32[8,64,128]{2,1,0:T(8,128)S(1)}, f32[8,64,128]{2,1,0:T(8,128)}, u32[]{:S(2)}) %copy-start) | copy-done | bytes 262168
  1.0 0.0 copy-start.1
  1.0 0.0 copy-start.2
  1.0 0.0 copy-start.3
  1.0 0.0 copy-start.4
  1.0 0.0 copy-start.5
  1.0 4.4 %collective-permute-start = (f32[8,128]{1,0:T(8,128)S(1)}, f32[8,128]{1,0:T(8,128)S(1)}, u32[]{:S(2)}, u32[]{:S(2)}) collective-permute-start(f32[8,128]{1,0:T(8,128)S(1)} %get-tuple-element.17), channel_id=1, source_target_pairs={{0,1},{1,2},{2,3},{3,4},{4,5},{5,6},{6,7},{7,8},{8,9},{9,10},{10,1... | collective-permute-start | bytes 12296 | tf_op jit(solution)/shard_map/ppermute | solution.py:284
  5.4 1.9 %collective-permute-start.1 = (f32[8,32,128]{2,1,0:T(8,128)S(1)}, f32[8,32,128]{2,1,0:T(8,128)S(1)}, u32[]{:S(2)}, u32[]{:S(2)}) collective-permute-start(f32[8,32,128]{2,1,0:T(8,128)S(1)} %get-tuple-element.21), channel_id=1, source_target_pairs={{1,0},{2,1},{3,2},{4,3},{5,4},{6,5},{7,6},{8,7},{9,8},{10,9},{11,1... | collective-permute-start | bytes 393224 | tf_op jit(solution)/shard_map/ppermute | solution.py:283
  7.4 0.0 collective-permute-done.refs_6_.low
  7.4 0.0 copy-done.1
  7.4 0.0 copy-done.2
  7.4 0.0 copy-done.3
  7.4 0.0 copy-done.4
  7.4 0.0 copy-done.5
  7.4 1.9 %inner.1 = (f32[4,864,128]{2,1,0:T(8,128)S(1)}, f32[16,128]{1,0:T(8,128)S(1)}, f32[5,8,128]{2,1,0:T(8,128)S(1)}, s32[64]{0:T(128)S(1)}) custom-call(f32[3]{0:T(128)S(1)} %copy-done.1, f32[3]{0:T(128)S(1)} %copy-done.2, f32[3]{0:T(128)S(1)} %copy-done.3, s32[4]{0:T(128)S(1)} %copy-done.4, s32[4]{0:T(128)S(1)} %copy-done.5, ...), custom_call_target="tpu_custom_call" | custom-call | flops 99999997952 | bytes 1048576 | tf_op jit(solution)/shard_map/inner/pallas_call | solution.py:286
  9.3 3.1 %collective-permute-done.1.high = f32[8,32,128]{2,1,0:T(8,128)S(1)} collective-permute-done((f32[8,32,128]{2,1,0:T(8,128)S(1)}, f32[8,32,128]{2,1,0:T(8,128)S(1)}, u32[]{:S(2)}, u32[]{:S(2)}) %collective-permute-start.1) | collective-permute-done | bytes 131104 | tf_op jit(solution)/shard_map/ppermute | solution.py:283
  12.4 4.0 %collective-permute-start.2 = (f32[2,112,128]{2,1,0:T(8,128)S(1)}, f32[2,112,128]{2,1,0:T(8,128)S(1)}, u32[]{:S(2)}, u32[]{:S(2)}) collective-permute-start(f32[2,112,128]{2,1,0:T(8,128)S(1)} %get-tuple-element.23), channel_id=1, source_target_pairs={{32,0},{64,32},{96,64},{128,96},{160,128},{192,160},{224,192},{256... | collective-permute-start | bytes 344072 | tf_op jit(solution)/shard_map/ppermute | solution.py:306
  16.4 0.6 %edge.1.held = f32[4,864,128]{2,1,0:T(8,128)S(1)} custom-call(f32[16,128]{1,0:T(8,128)S(1)} %get-tuple-element.19.table, f32[8,112,128]{2,1,0:T(8,128)S(1)} %get-tuple-element.22.brick, f32[4,864,128]{2,1,0:T(8,128)S(1)} %get-tuple-element.24.held), custom_call_target="tpu_custom_call", output_to_operand_aliasing={{}: (2, {})} | custom-call | flops 10000000 | bytes 1048576 | tf_op jit(solution)/shard_map/edge/pallas_call | solution.py:308
  17.0 3.9 %collective-permute-done.2.coming = f32[2,112,128]{2,1,0:T(8,128)S(1)} collective-permute-done((f32[2,112,128]{2,1,0:T(8,128)S(1)}, f32[2,112,128]{2,1,0:T(8,128)S(1)}, u32[]{:S(2)}, u32[]{:S(2)}) %collective-permute-start.2) | collective-permute-done | bytes 114720 | tf_op jit(solution)/shard_map/ppermute | solution.py:306
  20.9 1.2 %render.1 = (f32[8,4,2,8,128]{4,3,2,1,0:T(8,128)S(1)}, f32[8,4,2,8,128]{4,3,2,1,0:T(8,128)S(1)}, f32[4,864,128]{2,1,0:T(8,128)S(1)}) custom-call(f32[16,128]{1,0:T(8,128)S(1)} %get-tuple-element.19.table, f32[5,8,128]{2,1,0:T(8,128)S(1)} %get-tuple-element.18.masks, s32[64]{0:T(128)S(1)} %get-tuple-element.20.starts_in, ...), custom_call_target="tpu_custom_call", output_to_operand_aliasing={{2}: (5, {})} | custom-call | bytes 1048576 | tf_op jit(solution)/shard_map/render/pallas_call | solution.py:319
  22.1 2.2 %all-gather = f32[16,4,2,8,128]{4,3,2,1,0:T(8,128)S(1)} all-gather(f32[8,4,2,8,128]{4,3,2,1,0:T(8,128)S(1)} %get-tuple-element.26), channel_id=2, replica_groups={{0,32},{64,96},{128,160},{192,224},{256,288},{320,352},{384,416},{448,4..., dimensions={0}, use_global_device_ids=true | all-gather | bytes 786432 | tf_op jit(solution)/shard_map/all_gather | solution.py:330
  24.3 0.1 merge.1
  24.3 21.2 %all_to_all.5.slabs = f32[8,4,2,8,128]{4,3,2,1,0:T(8,128)S(1)} all-to-all(f32[8,4,2,8,128]{4,3,2,1,0:T(8,128)S(1)} %merge.1), channel_id=1, replica_groups={{0,64,128,192,256,320,384,448},{32,96,160,224,288,352,416,480},{1,65,12..., dimensions={0} | all-to-all | bytes 524288 | tf_op jit(solution)/shard_map/all_to_all | solution.py:333
  45.5 0.7 %composite.1 = f32[4,4,4,128]{3,2,1,0:T(4,128)} custom-call(f32[5,8,128]{2,1,0:T(8,128)S(1)} %get-tuple-element.18.masks, f32[8,4,2,8,128]{4,3,2,1,0:T(8,128)S(1)} %all_to_all.5.slabs), custom_call_target="tpu_custom_call" | custom-call | bytes 1048576 | tf_op jit(solution)/shard_map/composite/pallas_call | solution.py:334
  (2 shorter events, 0.1 us)
Async XLA Ops:
  0.0 0.9 %copy-start = (f32[8,64,128]{2,1,0:T(8,128)S(1)}, f32[8,64,128]{2,1,0:T(8,128)}, u32[]{:S(2)}) copy-start(f32[8,64,128]{2,1,0:T(8,128)} %density.1) | copy-start | bytes 786436
  1.0 6.4 %copy-start.1 = (f32[3]{0:T(128)S(1)}, f32[3]{0:T(128)}, u32[]{:S(2)}) copy-start(f32[3]{0:T(128)} %refs_0_.1) | copy-start | bytes 40
  1.0 6.4 %copy-start.2 = (f32[3]{0:T(128)S(1)}, f32[3]{0:T(128)}, u32[]{:S(2)}) copy-start(f32[3]{0:T(128)} %refs_1_.1) | copy-start | bytes 40
  1.0 6.5 %copy-start.3 = (f32[3]{0:T(128)S(1)}, f32[3]{0:T(128)}, u32[]{:S(2)}) copy-start(f32[3]{0:T(128)} %refs_2_.1) | copy-start | bytes 40
  1.0 6.5 %copy-start.4 = (s32[4]{0:T(128)S(1)}, s32[4]{0:T(128)}, u32[]{:S(2)}) copy-start(s32[4]{0:T(128)} %refs_3_.1) | copy-start | bytes 52
  1.0 6.5 %copy-start.5 = (s32[4]{0:T(128)S(1)}, s32[4]{0:T(128)}, u32[]{:S(2)}) copy-start(s32[4]{0:T(128)} %refs_4_.1) | copy-start | bytes 52
  1.0 6.4 %collective-permute-start = (f32[8,128]{1,0:T(8,128)S(1)}, f32[8,128]{1,0:T(8,128)S(1)}, u32[]{:S(2)}, u32[]{:S(2)}) collective-permute-start(f32[8,128]{1,0:T(8,128)S(1)} %get-tuple-element.17), channel_id=1, source_target_pairs={{0,1},{1,2},{2,3},{3,4},{4,5},{5,6},{6,7},{7,8},{8,9},{9,10},{10,1... | collective-permute-start | bytes 12296 | tf_op jit(solution)/shard_map/ppermute | solution.py:284
  5.4 6.9 %collective-permute-start.1 = (f32[8,32,128]{2,1,0:T(8,128)S(1)}, f32[8,32,128]{2,1,0:T(8,128)S(1)}, u32[]{:S(2)}, u32[]{:S(2)}) collective-permute-start(f32[8,32,128]{2,1,0:T(8,128)S(1)} %get-tuple-element.21), channel_id=1, source_target_pairs={{1,0},{2,1},{3,2},{4,3},{5,4},{6,5},{7,6},{8,7},{9,8},{10,9},{11,1... | collective-permute-start | bytes 393224 | tf_op jit(solution)/shard_map/ppermute | solution.py:283
  12.4 8.5 %collective-permute-start.2 = (f32[2,112,128]{2,1,0:T(8,128)S(1)}, f32[2,112,128]{2,1,0:T(8,128)S(1)}, u32[]{:S(2)}, u32[]{:S(2)}) collective-permute-start(f32[2,112,128]{2,1,0:T(8,128)S(1)} %get-tuple-element.23), channel_id=1, source_target_pairs={{32,0},{64,32},{96,64},{128,96},{160,128},{192,160},{224,192},{256... | collective-permute-start | bytes 344072 | tf_op jit(solution)/shard_map/ppermute | solution.py:306

commit v6 on v3

--- a/solution.py
+++ b/solution.py
@@ -11,15 +11,14 @@
 ANY = pl.BlockSpec(memory_space=pl.ANY)
 HBM = pl.BlockSpec(memory_space=pltpu.HBM)
 PLANES, ROWS, COLS, SHEAR, VIEWS, GROUPS, BRICKS = 8, 64, 128, 32, 4, 16, 32
-TOP = 8
 TALL = ROWS + SHEAR
-PADDED = TOP + TALL + 8
 SLABS = PLANES + 1
 CHIPS = GROUPS // 2
 SHARE = ROWS // GROUPS
 PARAMS = pltpu.CompilerParams(vmem_limit_bytes=8 * 2**20)
 LIGHT, GAIN, BIAS, PLAIN, BEYOND, NEXT, NEXT_BEYOND = 0, 3, 6, 9, 10, 11, 12
 FRONT, BACK, CORE = 0, 2, 4
+INNER = slice(8, ROWS - 8)
 FIRST = VIEWS * SLABS
 
 
@@ -50,13 +49,11 @@
     return [strength * tone for tone in tones] + [optical]
 
 
-def load_kernel(density, own, low, high, semaphore):
+def load_kernel(density, own, first, semaphore):
     copy = pltpu.make_async_copy(density, own, semaphore)
     copy.start()
     copy.wait()
-    high[...] = own[:, :SHEAR, :]
-    for plane in range(PLANES):
-        low[plane : plane + 1, :] = own[plane, ROWS - 1 : ROWS, :]
+    first[...] = own[:2]
 
 
 def inner_kernel(*refs):
@@ -91,90 +88,109 @@
             offset = lax.shift_right_logical((depth * PLANES + slot) * shear[view], 7)
             starts[view * SLABS + step] = slot * TALL + jnp.minimum(offset, SHEAR)
 
-    def plane_of(step, _):
-        plane = step + 1
-        inner = slice(8, ROWS - 8)
-        values = shade(
-            lambda row: values_of[row],
-            extinction,
-            own[plane, inner, :],
-            own[plane, 7 : ROWS - 9, :],
-            own[plane, 9 : ROWS - 7, :],
-            own[plane - 1, inner, :],
-            own[plane + 1, inner, :],
-        )
-        rows = pl.ds(pl.multiple_of(plane * TALL + 8, 8), ROWS - 16)
-        for kind in range(4):
-            fields[kind, rows, :] = values[kind]
+    coefficient = lambda at: values_of[at]
+
+    def plane_of(plane, _):
+        shade_inner(coefficient, extinction, own.at[plane], own[plane - 1, INNER, :], own[plane + 1, INNER, :], fields, plane)
         return 0
 
-    lax.fori_loop(0, PLANES - 2, plane_of, 0)
-
-
-def join_kernel(own, low, high, table, brick, first):
-    del table
-    for plane in range(PLANES):
-        parts = (
-            (0, jnp.broadcast_to(low[plane : plane + 1, :], (8, COLS))),
-            (TOP, own[plane]),
-            (TOP + ROWS, high[plane]),
-            (TOP + TALL, jnp.zeros((8, COLS), jnp.float32)),
-        )
-        for start, part in parts:
-            brick[plane, start : start + part.shape[0], :] = part
-            if plane < 2:
-                first[plane, start : start + part.shape[0], :] = part
-
-
-def shade_rows(table, extinction, row, count, plane, before, after, fields, slot):
-    start = row + TOP
-    values = shade(
-        lambda at: table[at : at + 1, :],
-        table[extinction : extinction + 1, :],
-        plane[start : start + count, :],
-        plane[start - 1 : start - 1 + count, :],
-        plane[start + 1 : start + 1 + count, :],
-        0.0 if before is None else before[start : start + count, :],
-        after[start : start + count, :],
-    )
-    rows = pl.ds(pl.multiple_of(slot * TALL + row, 8), count)
+    lax.fori_loop(1, PLANES - 1, plane_of, 0)
+
+    @pl.when(depth == 0)
+    def _():
+        shade_inner(coefficient, extinction, own.at[0], 0.0, own[1, INNER, :], fields, 0)
+
+
+def shade_inner(coefficient, extinction, plane, before, after, fields, slot):
+    centre = plane[INNER, :]
+    values = shade(coefficient, extinction, centre, plane[7 : ROWS - 9, :], plane[9 : ROWS - 7, :], before, after)
+    store(fields, slot, 8, values)
+
+
+def store(fields, slot, row, values):
+    rows = pl.ds(pl.multiple_of(slot * TALL + row, 8), values[0].shape[0])
     for kind in range(4):
         fields[kind, rows, :] = values[kind]
 
 
-def edge_kernel(table, brick, held, fields):
+def cut_kernel(own, coming, held, high, low):
     del held
-
-    def plane_of(step, _):
-        plane = step + 1
-        refs = (brick.at[plane], brick.at[plane - 1], brick.at[plane + 1], fields, plane)
-        shade_rows(table, PLAIN, 0, 8, *refs)
-        shade_rows(table, PLAIN, ROWS - 8, 8, *refs)
-        shade_rows(table, BEYOND, ROWS, SHEAR, *refs)
+    high[:PLANES] = own[:, :SHEAR, :]
+    high[PLANES:] = coming[:, :SHEAR, :]
+    for plane in range(PLANES):
+        low[plane : plane + 1, :] = own[plane, ROWS - 1 : ROWS, :]
+    low[PLANES:, :] = jnp.broadcast_to(coming[0, ROWS - 1 : ROWS, :], (8, COLS))
+
+
+def next_kernel(table, own, coming, held, fields):
+    del held
+    coefficient = lambda at: table[at : at + 1, :]
+    shade_inner(
+        coefficient, coefficient(PLAIN), own.at[PLANES - 1], own[PLANES - 2, INNER, :], coming[0, INNER, :], fields, PLANES - 1
+    )
+    shade_inner(
+        coefficient, coefficient(NEXT), coming.at[0], own[PLANES - 1, INNER, :], coming[1, INNER, :], fields, PLANES
+    )
+
+
+def edge_kernel(table, own, coming, high, held, fields, brick):
+    del held
+    coefficient = lambda at: table[at : at + 1, :]
+    for plane in range(PLANES + 2):
+        source = own.at[plane] if plane < PLANES else coming.at[plane - PLANES]
+        brick[plane, :16, :] = source[ROWS - 16 :, :]
+        brick[plane, 16 : 16 + SHEAR, :] = high[plane]
+        brick[plane, 16 + SHEAR :, :] = jnp.zeros((8, COLS), jnp.float32)
+
+    def rows_of(slot, before, plain, beyond):
+        for start, count, extinction in ((8, 8, plain), (16, SHEAR, beyond)):
+            values = shade(
+                coefficient,
+                coefficient(extinction),
+                brick[slot, start : start + count, :],
+                brick[slot, start - 1 : start - 1 + count, :],
+                brick[slot, start + 1 : start + 1 + count, :],
+                0.0 if before is None else brick[before, start : start + count, :],
+                brick[slot + 1, start : start + count, :],
+            )
+            store(fields, slot, ROWS - 16 + start, values)
+
+    def plane_of(plane, _):
+        rows_of(plane, plane - 1, PLAIN, BEYOND)
         return 0
 
-    lax.fori_loop(0, PLANES - 2, plane_of, 0)
-
-
-def render_kernel(table, masks, starts_in, brick, coming, held, given, kept, fields, starts, semaphore):
+    lax.fori_loop(1, PLANES, plane_of, 0)
+    rows_of(PLANES, PLANES - 1, NEXT, NEXT_BEYOND)
+
+    @pl.when(lax.axis_index("depth") == 0)
+    def _():
+        rows_of(0, None, PLAIN, BEYOND)
+
+
+def render_kernel(table, masks, starts_in, own, coming, low, held, given, kept, fields, starts, semaphore):
     del held
     copy = pltpu.make_async_copy(starts_in, starts, semaphore)
     copy.start()
-
-    def whole_plane(slot, plane, before, after, own, beyond):
-        refs = (plane, before, after, fields, slot)
-        shade_rows(table, own, 0, SHEAR, *refs)
-        shade_rows(table, own, SHEAR, SHEAR, *refs)
-        shade_rows(table, beyond, ROWS, SHEAR, *refs)
-
-    whole_plane(PLANES - 1, brick.at[PLANES - 1], brick.at[PLANES - 2], coming.at[0], PLAIN, BEYOND)
-    whole_plane(PLANES, coming.at[0], brick.at[PLANES - 1], coming.at[1], NEXT, NEXT_BEYOND)
+    coefficient = lambda at: table[at : at + 1, :]
+    top = lax.broadcasted_iota(jnp.int32, (8, COLS), 0) == 0
+
+    def first_rows(slot):
+        plane_at = lambda plane: own.at[plane] if plane < PLANES else coming.at[plane - PLANES]
+        plane = plane_at(slot)
+        centre = plane[:8, :]
+        above = jnp.where(top, low[slot : slot + 1, :], pltpu.roll(centre, 1, 0))
+        before = 0.0 if slot == 0 else plane_at(slot - 1)[:8, :]
+        extinction = coefficient(NEXT if slot == PLANES else PLAIN)
+        store(fields, slot, 0, shade(coefficient, extinction, centre, above, plane[1:9, :], before, plane_at(slot + 1)[:8, :]))
+
+    for slot in range(1, SLABS):
+        first_rows(slot)
     copy.wait()
     leading = starts[FIRST] == 0
 
     @pl.when(leading)
     def _():
-        whole_plane(0, brick.at[0], None, brick.at[1], PLAIN, BEYOND)
+        first_rows(0)
 
     def render(planes):
         upper = lax.broadcasted_iota(jnp.int32, (8, COLS), 0) < SHARE
@@ -267,27 +283,22 @@
 def on_device(density, light_vector, colour_gain, colour_bias, shear_step, reverse_view):
     heights, depths = lax.axis_size("height"), lax.axis_size("depth")
 
-    own, own_low, own_high = kernel(
+    own, first = kernel(
         load_kernel,
         "load",
-        (array(PLANES, ROWS, COLS), array(PLANES, COLS), array(PLANES, SHEAR, COLS)),
+        (array(PLANES, ROWS, COLS), array(2, ROWS, COLS)),
         [HBM],
-        (VMEM,) * 3,
+        (VMEM,) * 2,
         flops=10**9,
         scratch_shapes=[pltpu.SemaphoreType.DMA],
     )(density)
-    high = lax.ppermute(own_high, "height", [(i + 1, i) for i in range(heights - 1)])
-    low = lax.ppermute(own_low, "height", [(i, i + 1) for i in range(heights - 1)])
-
+    coming = lax.ppermute(first, "depth", [(i + 1, i) for i in range(depths - 1)])
+
+    shaded = array(4, SLABS * TALL, COLS)
     fields, table, masks, starts = kernel(
         inner_kernel,
         "inner",
-        (
-            array(4, SLABS * TALL, COLS),
-            array(16, COLS),
-            array(5, 8, COLS),
-            jax.ShapeDtypeStruct((64,), jnp.int32),
-        ),
+        (shaded, array(16, COLS), array(5, 8, COLS), jax.ShapeDtypeStruct((64,), jnp.int32)),
         [HBM] * 5 + [VMEM],
         (VMEM, VMEM, VMEM, SMEM),
         flops=10**7,
@@ -296,31 +307,35 @@
         + [pltpu.SemaphoreType.DMA((5,))],
     )(light_vector, colour_gain, colour_bias, shear_step, reverse_view, own)
 
-    brick, first = kernel(
-        join_kernel, "join", (array(PLANES, PADDED, COLS), array(2, PADDED, COLS)), [VMEM] * 4, (VMEM,) * 2
-    )(own, low, high, table)
-    coming = lax.ppermute(first, "depth", [(i + 1, i) for i in range(depths - 1)])
-
+    own_high, own_low = kernel(
+        cut_kernel, "cut", (array(PLANES + 2, SHEAR, COLS), array(PLANES + 8, COLS)), [VMEM] * 3, (VMEM,) * 2
+    )(own, coming, fields)
+    high = lax.ppermute(own_high, "height", [(i + 1, i) for i in range(heights - 1)])
+    low = lax.ppermute(own_low, "height", [(i, i + 1) for i in range(heights - 1)])
+    fields = kernel(
+        next_kernel, "next", shaded, [VMEM] * 4, VMEM, flops=10**7, input_output_aliases={3: 0}
+    )(table, own, coming, fields)
     fields = kernel(
         edge_kernel,
         "edge",
-        array(4, SLABS * TALL, COLS),
-        [VMEM] * 3,
+        shaded,
+        [VMEM] * 5,
         VMEM,
         flops=10**7,
-        input_output_aliases={2: 0},
-    )(table, brick, fields)
+        input_output_aliases={4: 0},
+        scratch_shapes=[pltpu.VMEM((PLANES + 2, 24 + SHEAR, COLS), jnp.float32)],
+    )(table, own, coming, high, fields)
 
     part = array(CHIPS, 4, VIEWS // 2, 8, COLS)
     given, kept, _ = kernel(
         render_kernel,
         "render",
-        (part, part, array(4, SLABS * TALL, COLS)),
-        [VMEM, VMEM, ANY, VMEM, VMEM, VMEM],
+        (part, part, shaded),
+        [VMEM, VMEM, ANY, VMEM, VMEM, VMEM, VMEM],
         (VMEM,) * 3,
-        input_output_aliases={5: 2},
+        input_output_aliases={6: 2},
         scratch_shapes=[pltpu.SMEM((64,), jnp.int32), pltpu.SemaphoreType.DMA],
-    )(table, masks, starts, brick, coming, fields)
+    )(table, masks, starts, own, coming, low, fields)
 
     cores = [[2 * chip, 2 * chip + 1] for chip in range(CHIPS)]
     gathered = lax.all_gather(given, "depth", axis=0, axis_index_groups=cores)

time: 46.9 us -> 44.9 us (0.957)
  blocking collectives: 26.9 us -> 24.9 us
  Pallas kernels: 4.59 us -> 5.13 us
    all_gather x1, blocking collectives: 5.27 us -> 3.17 us  [on_device(): gathered = lax.all_gather(given, 'depth', axis=0, axis_index_groups=cores)]
    ppermute x1, waiting for transfers between devices: 1.33 us -> 0.01 us  [on_device(): lax.ppermute(first, 'depth', [(i + 1, i) for i in range(depths - 1)])]
    ppermute x1, waiting for transfers between devices: 0.01 us -> 0.75 us  [on_device(): lax.ppermute(own_high, 'height', [(i + 1, i) for i in range(heights - 1)])]
    pallas_call x5 -> x6, Pallas kernels: 3.87 us -> 4.41 us  [the longest x1 2.04 us: on_device(): kernel(inner_kernel, 'inner', (shaded, array(16, COLS), array(5, 8, COLS)...]
  transfers between devices with their start and end apart: 3 -> 3, of which waited for: 2 -> 2; matrix products, arithmetic and copies ran while one was open for 0% -> 0% of each run, Pallas kernels for 5% -> 7%
where the time goes in v6:
time: 44.9 us; the launch traced here: 44.7 us
  blocking collectives  24.9 us (55%)
  starting transfers between devices  8.86 us (20%)
  Pallas kernels  5.13 us (11%)
  waiting for transfers between devices  4.72 us (11%)
  local copies, waits for them, and re-layouts  1.01 us (2%)
    all_to_all x1, blocking collectives, on_device(): lax.all_to_all(merged, 'depth', 0, 0, tiled=True, axis_index_groups=chips)  21.7 us
    ppermute x1, starting transfers between devices, on_device(): lax.ppermute(own_high, 'height', [(i + 1, i) for i in range(heights - 1)])  5.64 us
    ppermute x1, waiting for transfers between devices, on_device(): lax.ppermute(own_low, 'height', [(i, i + 1) for i in range(heights - 1)])  3.97 us
    all_gather x1, blocking collectives, on_device(): gathered = lax.all_gather(given, 'depth', axis=0, axis_index_groups=cores)  3.17 us
    pallas_call x1, Pallas kernels, on_device(): kernel(inner_kernel, 'inner', (shaded, array(16, COLS), array(5, 8, COLS)...  2.04 us
    ppermute x1, starting transfers between devices, on_device(): lax.ppermute(own_low, 'height', [(i, i + 1) for i in range(heights - 1)])  1.92 us
    pallas_call x1, Pallas kernels, on_device(): kernel(render_kernel, 'render', (part, part, shaded), [VMEM, VMEM, ANY, V...  1.33 us
    ppermute x1, starting transfers between devices, on_device(): lax.ppermute(first, 'depth', [(i + 1, i) for i in range(depths - 1)])  1.29 us
  transfers between devices with their start and end apart: 3, of which 2 were waited for; matrix products, arithmetic and copies ran while one was open for 0% of the time, Pallas kernels for 7%

profile of v6, /device:TPU:6, one launch (start us, length us, event | category | flops | bytes accessed | tf_op | source)
XLA Modules:
  0.0 44.7 jit_solution(10847755490169259073)
XLA Ops:
  0.0 0.0 copy-start.4
  0.0 0.0 copy-start.3
  0.0 0.0 copy-start.2
  0.0 0.0 copy-start.1
  0.0 0.0 copy-start.5
  0.0 1.0 %copy-done.5 = f32[8,64,128]{2,1,0:T(8,128)S(1)} copy-done((f32[8,64,128]{2,1,0:T(8,128)S(1)}, f32[8,64,128]{2,1,0:T(8,128)}, u32[]{:S(2)}) %copy-start.5) | copy-done | bytes 262168
  1.0 0.0 copy-start
  1.1 1.3 %collective-permute-start = (f32[2,64,128]{2,1,0:T(8,128)S(1)}, f32[2,64,128]{2,1,0:T(8,128)S(1)}, u32[]{:S(2)}, u32[]{:S(2)}) collective-permute-start(f32[2,64,128]{2,1,0:T(8,128)S(1)} %get-tuple-element.19), channel_id=1, source_target_pairs={{32,0},{64,32},{96,64},{128,96},{160,128},{192,160},{224,192},{256... | collective-permute-start | bytes 196616 | tf_op jit(solution)/shard_map/ppermute | solution.py:295
  2.4 0.0 copy-done.4
  2.4 0.0 copy-done.3
  2.4 0.0 copy-done.2
  2.4 0.0 copy-done.1
  2.4 0.0 copy-done
  2.4 2.0 %inner.1 = (f32[4,864,128]{2,1,0:T(8,128)S(1)}, f32[16,128]{1,0:T(8,128)S(1)}, f32[5,8,128]{2,1,0:T(8,128)S(1)}, s32[64]{0:T(128)S(1)}) custom-call(f32[3]{0:T(128)S(1)} %copy-done, f32[3]{0:T(128)S(1)} %copy-done.1, f32[3]{0:T(128)S(1)} %copy-done.2, s32[4]{0:T(128)S(1)} %copy-done.3, s32[4]{0:T(128)S(1)} %copy-done.4, ...), custom_call_target="tpu_custom_call" | custom-call | flops 10000000 | bytes 1048576 | tf_op jit(solution)/shard_map/inner/pallas_call | solution.py:298
  4.5 0.0 collective-permute-done.coming
  4.5 5.6 %collective-permute-start.2 = (f32[10,32,128]{2,1,0:T(8,128)S(1)}, f32[10,32,128]{2,1,0:T(8,128)S(1)}, u32[]{:S(2)}, u32[]{:S(2)}) collective-permute-start(f32[10,32,128]{2,1,0:T(8,128)S(1)} %get-tuple-element.22), channel_id=1, source_target_pairs={{1,0},{2,1},{3,2},{4,3},{5,4},{6,5},{7,6},{8,7},{9,8},{10,9},{11,1... | collective-permute-start | bytes 491528 | tf_op jit(solution)/shard_map/ppermute | solution.py:313
  10.1 1.9 %collective-permute-start.1 = (f32[16,128]{1,0:T(8,128)S(1)}, f32[16,128]{1,0:T(8,128)S(1)}, u32[]{:S(2)}, u32[]{:S(2)}) collective-permute-start(f32[16,128]{1,0:T(8,128)S(1)} %get-tuple-element.21), channel_id=1, source_target_pairs={{0,1},{1,2},{2,3},{3,4},{4,5},{5,6},{6,7},{7,8},{8,9},{9,10},{10,1... | collective-permute-start | bytes 24584 | tf_op jit(solution)/shard_map/ppermute | solution.py:314
  12.1 0.1 next.1.held
  12.2 0.8 %collective-permute-done.2.high = f32[10,32,128]{2,1,0:T(8,128)S(1)} collective-permute-done((f32[10,32,128]{2,1,0:T(8,128)S(1)}, f32[10,32,128]{2,1,0:T(8,128)S(1)}, u32[]{:S(2)}, u32[]{:S(2)}) %collective-permute-start.2) | collective-permute-done | bytes 163872 | tf_op jit(solution)/shard_map/ppermute | solution.py:313
  13.0 0.9 %edge.1.held = f32[4,864,128]{2,1,0:T(8,128)S(1)} custom-call(f32[16,128]{1,0:T(8,128)S(1)} %get-tuple-element.17.table, f32[8,64,128]{2,1,0:T(8,128)S(1)} %get-tuple-element.15.refs_5_.own, f32[2,64,128]{2,1,0:T(8,128)S(1)} %collective-permute-done.coming, f32[10,32,128]{2,1,0:T(8,128)S(1)} %collective-permute-done.2.high, ...), custom_call_target="tpu_custom_call", output_to_operand_aliasing={{}: (4, {})} | custom-call | flops 10000000 | bytes 1048576 | tf_op jit(solution)/shard_map/edge/pallas_call | solution.py:318
  13.8 4.0 %collective-permute-done.1.low = f32[16,128]{1,0:T(8,128)S(1)} collective-permute-done((f32[16,128]{1,0:T(8,128)S(1)}, f32[16,128]{1,0:T(8,128)S(1)}, u32[]{:S(2)}, u32[]{:S(2)}) %collective-permute-start.1) | collective-permute-done | bytes 8224 | tf_op jit(solution)/shard_map/ppermute | solution.py:314
  17.8 1.3 %render.1 = (f32[8,4,2,8,128]{4,3,2,1,0:T(8,128)S(1)}, f32[8,4,2,8,128]{4,3,2,1,0:T(8,128)S(1)}, f32[4,864,128]{2,1,0:T(8,128)S(1)}) custom-call(f32[16,128]{1,0:T(8,128)S(1)} %get-tuple-element.17.table, f32[5,8,128]{2,1,0:T(8,128)S(1)} %get-tuple-element.16.masks, s32[64]{0:T(128)S(1)} %get-tuple-element.18.starts_in, ...), custom_call_target="tpu_custom_call", output_to_operand_aliasing={{2}: (6, {})} | custom-call | bytes 1048576 | tf_op jit(solution)/shard_map/render/pallas_call | solution.py:330
  19.1 3.2 %all-gather = f32[16,4,2,8,128]{4,3,2,1,0:T(8,128)S(1)} all-gather(f32[8,4,2,8,128]{4,3,2,1,0:T(8,128)S(1)} %get-tuple-element.24), channel_id=2, replica_groups={{0,32},{64,96},{128,160},{192,224},{256,288},{320,352},{384,416},{448,4..., dimensions={0}, use_global_device_ids=true | all-gather | bytes 786432 | tf_op jit(solution)/shard_map/all_gather | solution.py:341
  22.3 0.1 merge.1
  22.4 21.7 %all_to_all.5.slabs = f32[8,4,2,8,128]{4,3,2,1,0:T(8,128)S(1)} all-to-all(f32[8,4,2,8,128]{4,3,2,1,0:T(8,128)S(1)} %merge.1), channel_id=1, replica_groups={{0,64,128,192,256,320,384,448},{32,96,160,224,288,352,416,480},{1,65,12..., dimensions={0} | all-to-all | bytes 524288 | tf_op jit(solution)/shard_map/all_to_all | solution.py:344
  44.1 0.7 %composite.1 = f32[4,4,4,128]{3,2,1,0:T(4,128)} custom-call(f32[5,8,128]{2,1,0:T(8,128)S(1)} %get-tuple-element.16.masks, f32[8,4,2,8,128]{4,3,2,1,0:T(8,128)S(1)} %all_to_all.5.slabs), custom_call_target="tpu_custom_call" | custom-call | bytes 1048576 | tf_op jit(solution)/shard_map/composite/pallas_call | solution.py:345
  (2 shorter events, 0.1 us)
Async XLA Ops:
  0.0 2.4 %copy-start.4 = (s32[4]{0:T(128)S(1)}, s32[4]{0:T(128)}, u32[]{:S(2)}) copy-start(s32[4]{0:T(128)} %refs_4_.1) | copy-start | bytes 52
  0.0 2.4 %copy-start.3 = (s32[4]{0:T(128)S(1)}, s32[4]{0:T(128)}, u32[]{:S(2)}) copy-start(s32[4]{0:T(128)} %refs_3_.1) | copy-start | bytes 52
  0.0 2.4 %copy-start.2 = (f32[3]{0:T(128)S(1)}, f32[3]{0:T(128)}, u32[]{:S(2)}) copy-start(f32[3]{0:T(128)} %refs_2_.1) | copy-start | bytes 40
  0.0 2.4 %copy-start.1 = (f32[3]{0:T(128)S(1)}, f32[3]{0:T(128)}, u32[]{:S(2)}) copy-start(f32[3]{0:T(128)} %refs_1_.1) | copy-start | bytes 40
  0.0 1.0 %copy-start.5 = (f32[8,64,128]{2,1,0:T(8,128)S(1)}, f32[8,64,128]{2,1,0:T(8,128)}, u32[]{:S(2)}) copy-start(f32[8,64,128]{2,1,0:T(8,128)} %density.1) | copy-start | bytes 786436
  1.0 1.4 %copy-start = (f32[3]{0:T(128)S(1)}, f32[3]{0:T(128)}, u32[]{:S(2)}) copy-start(f32[3]{0:T(128)} %refs_0_.1) | copy-start | bytes 40
  1.1 3.4 %collective-permute-start = (f32[2,64,128]{2,1,0:T(8,128)S(1)}, f32[2,64,128]{2,1,0:T(8,128)S(1)}, u32[]{:S(2)}, u32[]{:S(2)}) collective-permute-start(f32[2,64,128]{2,1,0:T(8,128)S(1)} %get-tuple-element.19), channel_id=1, source_target_pairs={{32,0},{64,32},{96,64},{128,96},{160,128},{192,160},{224,192},{256... | collective-permute-start | bytes 196616 | tf_op jit(solution)/shard_map/ppermute | solution.py:295
  4.5 8.5 %collective-permute-start.2 = (f32[10,32,128]{2,1,0:T(8,128)S(1)}, f32[10,32,128]{2,1,0:T(8,128)S(1)}, u32[]{:S(2)}, u32[]{:S(2)}) collective-permute-start(f32[10,32,128]{2,1,0:T(8,128)S(1)} %get-tuple-element.22), channel_id=1, source_target_pairs={{1,0},{2,1},{3,2},{4,3},{5,4},{6,5},{7,6},{8,7},{9,8},{10,9},{11,1... | collective-permute-start | bytes 491528 | tf_op jit(solution)/shard_map/ppermute | solution.py:313
  10.1 7.7 %collective-permute-start.1 = (f32[16,128]{1,0:T(8,128)S(1)}, f32[16,128]{1,0:T(8,128)S(1)}, u32[]{:S(2)}, u32[]{:S(2)}) collective-permute-start(f32[16,128]{1,0:T(8,128)S(1)} %get-tuple-element.21), channel_id=1, source_target_pairs={{0,1},{1,2},{2,3},{3,4},{4,5},{5,6},{6,7},{7,8},{8,9},{9,10},{10,1... | collective-permute-start | bytes 24584 | tf_op jit(solution)/shard_map/ppermute | solution.py:314

commit v7 on v6

--- a/solution.py
+++ b/solution.py
@@ -57,7 +57,7 @@
 
 
 def inner_kernel(*refs):
-    arguments, (own, fields, table, masks, starts), scalars, semaphores = refs[:5], refs[5:10], refs[10:15], refs[15]
+    arguments, (own, coming, _, fields, table, masks, starts), scalars, semaphores = refs[:5], refs[5:12], refs[12:17], refs[17]
     copies = [pltpu.make_async_copy(arguments[i], scalars[i], semaphores.at[i]) for i in range(5)]
     for copy in copies:
         copy.start()
@@ -95,6 +95,9 @@
         return 0
 
     lax.fori_loop(1, PLANES - 1, plane_of, 0)
+    last = own.at[PLANES - 1]
+    shade_inner(coefficient, extinction, last, own[PLANES - 2, INNER, :], coming[0, INNER, :], fields, PLANES - 1)
+    shade_inner(coefficient, following, coming.at[0], last[INNER, :], coming[1, INNER, :], fields, PLANES)
 
     @pl.when(depth == 0)
     def _():
@@ -113,24 +116,12 @@
         fields[kind, rows, :] = values[kind]
 
 
-def cut_kernel(own, coming, held, high, low):
-    del held
+def cut_kernel(own, coming, high, low):
     high[:PLANES] = own[:, :SHEAR, :]
     high[PLANES:] = coming[:, :SHEAR, :]
     for plane in range(PLANES):
         low[plane : plane + 1, :] = own[plane, ROWS - 1 : ROWS, :]
     low[PLANES:, :] = jnp.broadcast_to(coming[0, ROWS - 1 : ROWS, :], (8, COLS))
-
-
-def next_kernel(table, own, coming, held, fields):
-    del held
-    coefficient = lambda at: table[at : at + 1, :]
-    shade_inner(
-        coefficient, coefficient(PLAIN), own.at[PLANES - 1], own[PLANES - 2, INNER, :], coming[0, INNER, :], fields, PLANES - 1
-    )
-    shade_inner(
-        coefficient, coefficient(NEXT), coming.at[0], own[PLANES - 1, INNER, :], coming[1, INNER, :], fields, PLANES
-    )
 
 
 def edge_kernel(table, own, coming, high, held, fields, brick):
@@ -167,8 +158,16 @@
         rows_of(0, None, PLAIN, BEYOND)
 
 
-def render_kernel(table, masks, starts_in, own, coming, low, held, given, kept, fields, starts, semaphore):
+def render_kernel(masks, starts_in, fields, given, kept, starts, semaphore):
+    copy = pltpu.make_async_copy(starts_in, starts, semaphore)
+    copy.start()
+    copy.wait()
+    render(masks, starts, fields, given, kept, 1, ROWS // 8)
+
+
+def first_kernel(table, masks, starts_in, own, coming, low, held, *refs):
     del held
+    given, kept, fields, starts, semaphore = refs[2:]
     copy = pltpu.make_async_copy(starts_in, starts, semaphore)
     copy.start()
     coefficient = lambda at: table[at : at + 1, :]
@@ -185,17 +184,20 @@
 
     for slot in range(1, SLABS):
         first_rows(slot)
+
+    @pl.when(lax.axis_index("depth") == 0)
+    def _():
+        first_rows(0)
+
     copy.wait()
-    leading = starts[FIRST] == 0
-
-    @pl.when(leading)
-    def _():
-        first_rows(0)
-
-    def render(planes):
-        upper = lax.broadcasted_iota(jnp.int32, (8, COLS), 0) < SHARE
-        odd = masks[CORE] > 0.5
-
+    render(masks, starts, fields, given, kept, 0, 1)
+
+
+def render(masks, starts, fields, given, kept, tile, tiles):
+    upper = lax.broadcasted_iota(jnp.int32, (8, COLS), 0) < SHARE
+    odd = masks[CORE] > 0.5
+
+    def of(planes):
         def tile_of(tile, _):
             for pair in range(VIEWS // 2):
                 sums = []
@@ -217,15 +219,17 @@
                     given[tile, kind, pair] = jnp.where(odd, even_rows, odd_rows)
             return 0
 
-        lax.fori_loop(0, ROWS // 8, tile_of, 0)
+        lax.fori_loop(tile, tiles, tile_of, 0)
+
+    leading = starts[FIRST] == 0
 
     @pl.when(leading)
     def _():
-        render(SLABS)
+        of(SLABS)
 
     @pl.when(jnp.logical_not(leading))
     def _():
-        render(PLANES)
+        of(PLANES)
 
 
 def merge_kernel(masks, kept, gathered, out):
@@ -294,27 +298,24 @@
     )(density)
     coming = lax.ppermute(first, "depth", [(i + 1, i) for i in range(depths - 1)])
 
+    own_high, own_low = kernel(
+        cut_kernel, "cut", (array(PLANES + 2, SHEAR, COLS), array(PLANES + 8, COLS)), [VMEM] * 2, (VMEM,) * 2
+    )(own, coming)
+    high = lax.ppermute(own_high, "height", [(i + 1, i) for i in range(heights - 1)])
+    low = lax.ppermute(own_low, "height", [(i, i + 1) for i in range(heights - 1)])
+
     shaded = array(4, SLABS * TALL, COLS)
     fields, table, masks, starts = kernel(
         inner_kernel,
         "inner",
         (shaded, array(16, COLS), array(5, 8, COLS), jax.ShapeDtypeStruct((64,), jnp.int32)),
-        [HBM] * 5 + [VMEM],
+        [HBM] * 5 + [VMEM] * 3,
         (VMEM, VMEM, VMEM, SMEM),
         flops=10**7,
         scratch_shapes=[pltpu.SMEM((3,), jnp.float32)] * 3
         + [pltpu.SMEM((VIEWS,), jnp.int32)] * 2
         + [pltpu.SemaphoreType.DMA((5,))],
-    )(light_vector, colour_gain, colour_bias, shear_step, reverse_view, own)
-
-    own_high, own_low = kernel(
-        cut_kernel, "cut", (array(PLANES + 2, SHEAR, COLS), array(PLANES + 8, COLS)), [VMEM] * 3, (VMEM,) * 2
-    )(own, coming, fields)
-    high = lax.ppermute(own_high, "height", [(i + 1, i) for i in range(heights - 1)])
-    low = lax.ppermute(own_low, "height", [(i, i + 1) for i in range(heights - 1)])
-    fields = kernel(
-        next_kernel, "next", shaded, [VMEM] * 4, VMEM, flops=10**7, input_output_aliases={3: 0}
-    )(table, own, coming, fields)
+    )(light_vector, colour_gain, colour_bias, shear_step, reverse_view, own, coming, own_low)
     fields = kernel(
         edge_kernel,
         "edge",
@@ -327,15 +328,19 @@
     )(table, own, coming, high, fields)
 
     part = array(CHIPS, 4, VIEWS // 2, 8, COLS)
+    memory = [pltpu.SMEM((64,), jnp.int32), pltpu.SemaphoreType.DMA]
+    given, kept = kernel(
+        render_kernel, "render", (part, part), [VMEM, ANY, VMEM], (VMEM,) * 2, flops=10**7, scratch_shapes=memory
+    )(masks, starts, fields)
     given, kept, _ = kernel(
-        render_kernel,
-        "render",
+        first_kernel,
+        "first",
         (part, part, shaded),
-        [VMEM, VMEM, ANY, VMEM, VMEM, VMEM, VMEM],
+        [VMEM, VMEM, ANY] + [VMEM] * 6,
         (VMEM,) * 3,
-        input_output_aliases={6: 2},
-        scratch_shapes=[pltpu.SMEM((64,), jnp.int32), pltpu.SemaphoreType.DMA],
-    )(table, masks, starts, own, coming, low, fields)
+        input_output_aliases={6: 2, 7: 0, 8: 1},
+        scratch_shapes=memory,
+    )(table, masks, starts, own, coming, low, fields, given, kept)
 
     cores = [[2 * chip, 2 * chip + 1] for chip in range(CHIPS)]
     gathered = lax.all_gather(given, "depth", axis=0, axis_index_groups=cores)

time: 44.9 us -> 44.3 us (0.987)
  waiting for transfers between devices: 4.72 us -> 3.3 us
  Pallas kernels: 5.13 us -> 5.62 us
    ppermute x1, waiting for transfers between devices: 3.97 us -> 1.45 us  [on_device(): lax.ppermute(own_low, 'height', [(i, i + 1) for i in range(heights - 1)])]
    ppermute x1, waiting for transfers between devices: 0.01 us -> 1.85 us  [on_device(): lax.ppermute(first, 'depth', [(i + 1, i) for i in range(depths - 1)])]
    ppermute x1, waiting for transfers between devices: 0.75 us -> 0.01 us  [on_device(): lax.ppermute(own_high, 'height', [(i + 1, i) for i in range(heights - 1)])]
  transfers between devices with their start and end apart: 3 -> 3, of which waited for: 2 -> 2; matrix products, arithmetic and copies ran while one was open for 0% -> 0% of each run, Pallas kernels for 7% -> 10%
where the time goes in v7:
time: 44.3 us; the launch traced here: 44.1 us
  blocking collectives  25.2 us (57%)
  starting transfers between devices  8.86 us (20%)
  Pallas kernels  5.62 us (13%)
  waiting for transfers between devices  3.3 us (7%)
  local copies, waits for them, and re-layouts  1.01 us (2%)
    all_to_all x1, blocking collectives, on_device(): lax.all_to_all(merged, 'depth', 0, 0, tiled=True, axis_index_groups=chips)  21.6 us
    ppermute x1, starting transfers between devices, on_device(): lax.ppermute(own_high, 'height', [(i + 1, i) for i in range(heights - 1)])  5.64 us
    all_gather x1, blocking collectives, on_device(): gathered = lax.all_gather(given, 'depth', axis=0, axis_index_groups=cores)  3.56 us
    pallas_call x1, Pallas kernels, on_device(): kernel(inner_kernel, 'inner', (shaded, array(16, COLS), array(5, 8, COLS)...  2.16 us
    ppermute x1, starting transfers between devices, on_device(): lax.ppermute(own_low, 'height', [(i, i + 1) for i in range(heights - 1)])  1.92 us
    ppermute x1, waiting for transfers between devices, on_device(): lax.ppermute(first, 'depth', [(i + 1, i) for i in range(depths - 1)])  1.85 us
    ppermute x1, waiting for transfers between devices, on_device(): lax.ppermute(own_low, 'height', [(i, i + 1) for i in range(heights - 1)])  1.45 us
    ppermute x1, starting transfers between devices, on_device(): lax.ppermute(first, 'depth', [(i + 1, i) for i in range(depths - 1)])  1.29 us
  transfers between devices with their start and end apart: 3, of which 2 were waited for; matrix products, arithmetic and copies ran while one was open for 0% of the time, Pallas kernels for 10%

profile of v7, /device:TPU:6, one launch (start us, length us, event | category | flops | bytes accessed | tf_op | source)
XLA Modules:
  0.0 44.1 jit_solution(3858806853565244963)
XLA Ops:
  0.0 0.0 copy-start.4
  0.0 0.0 copy-start.3
  0.0 0.0 copy-start.2
  0.0 0.0 copy-start.1
  0.0 0.0 copy-start.5
  0.0 1.0 %copy-done.5 = f32[8,64,128]{2,1,0:T(8,128)S(1)} copy-done((f32[8,64,128]{2,1,0:T(8,128)S(1)}, f32[8,64,128]{2,1,0:T(8,128)}, u32[]{:S(2)}) %copy-start.5) | copy-done | bytes 262168
  1.0 0.0 copy-start
  1.1 1.3 %collective-permute-start = (f32[2,64,128]{2,1,0:T(8,128)S(1)}, f32[2,64,128]{2,1,0:T(8,128)S(1)}, u32[]{:S(2)}, u32[]{:S(2)}) collective-permute-start(f32[2,64,128]{2,1,0:T(8,128)S(1)} %get-tuple-element.18), channel_id=1, source_target_pairs={{32,0},{64,32},{96,64},{128,96},{160,128},{192,160},{224,192},{256... | collective-permute-start | bytes 196616 | tf_op jit(solution)/shard_map/ppermute | solution.py:299
  2.4 1.8 %collective-permute-done.coming.refs_6_ = f32[2,64,128]{2,1,0:T(8,128)S(1)} collective-permute-done((f32[2,64,128]{2,1,0:T(8,128)S(1)}, f32[2,64,128]{2,1,0:T(8,128)S(1)}, u32[]{:S(2)}, u32[]{:S(2)}) %collective-permute-start) | collective-permute-done | bytes 65568 | tf_op jit(solution)/shard_map/ppermute | solution.py:299
  4.2 5.6 %collective-permute-start.2 = (f32[10,32,128]{2,1,0:T(8,128)S(1)}, f32[10,32,128]{2,1,0:T(8,128)S(1)}, u32[]{:S(2)}, u32[]{:S(2)}) collective-permute-start(f32[10,32,128]{2,1,0:T(8,128)S(1)} %get-tuple-element.23), channel_id=1, source_target_pairs={{1,0},{2,1},{3,2},{4,3},{5,4},{6,5},{7,6},{8,7},{9,8},{10,9},{11,1... | collective-permute-start | bytes 491528 | tf_op jit(solution)/shard_map/ppermute | solution.py:304
  9.9 1.9 %collective-permute-start.1 = (f32[16,128]{1,0:T(8,128)S(1)}, f32[16,128]{1,0:T(8,128)S(1)}, u32[]{:S(2)}, u32[]{:S(2)}) collective-permute-start(f32[16,128]{1,0:T(8,128)S(1)} %get-tuple-element.19.refs_7_), channel_id=1, source_target_pairs={{0,1},{1,2},{2,3},{3,4},{4,5},{5,6},{6,7},{7,8},{8,9},{9,10},{10,1... | collective-permute-start | bytes 24584 | tf_op jit(solution)/shard_map/ppermute | solution.py:305
  11.8 0.0 copy-done.4
  11.8 0.0 copy-done.3
  11.8 0.0 copy-done.2
  11.8 0.0 copy-done.1
  11.8 0.0 copy-done
  11.9 2.2 %inner.1 = (f32[4,864,128]{2,1,0:T(8,128)S(1)}, f32[16,128]{1,0:T(8,128)S(1)}, f32[5,8,128]{2,1,0:T(8,128)S(1)}, s32[64]{0:T(128)S(1)}) custom-call(f32[3]{0:T(128)S(1)} %copy-done, f32[3]{0:T(128)S(1)} %copy-done.1, f32[3]{0:T(128)S(1)} %copy-done.2, s32[4]{0:T(128)S(1)} %copy-done.3, s32[4]{0:T(128)S(1)} %copy-done.4, ...), custom_call_target="tpu_custom_call" | custom-call | flops 10000000 | bytes 1048576 | tf_op jit(solution)/shard_map/inner/pallas_call | solution.py:308
  14.0 0.0 collective-permute-done.2.high
  14.0 0.9 %edge.1.fields.held = f32[4,864,128]{2,1,0:T(8,128)S(1)} custom-call(f32[16,128]{1,0:T(8,128)S(1)} %get-tuple-element.21.table, f32[8,64,128]{2,1,0:T(8,128)S(1)} %get-tuple-element.17.own.refs_5_, f32[2,64,128]{2,1,0:T(8,128)S(1)} %collective-permute-done.coming.refs_6_, ...), custom_call_target="tpu_custom_call", output_to_operand_aliasing={{}: (4, {})} | custom-call | flops 10000000 | bytes 1048576 | tf_op jit(solution)/shard_map/edge/pallas_call | solution.py:319
  14.9 1.2 %render.1 = (f32[8,4,2,8,128]{4,3,2,1,0:T(8,128)S(1)}, f32[8,4,2,8,128]{4,3,2,1,0:T(8,128)S(1)}) custom-call(f32[5,8,128]{2,1,0:T(8,128)S(1)} %get-tuple-element.20.masks, s32[64]{0:T(128)S(1)} %get-tuple-element.22.starts_in, f32[4,864,128]{2,1,0:T(8,128)S(1)} %edge.1.fields.held), custom_call_target="tpu_custom_call" | custom-call | flops 10000000 | bytes 1048576 | tf_op jit(solution)/shard_map/render/pallas_call | solution.py:332
  16.1 1.4 %collective-permute-done.1.low = f32[16,128]{1,0:T(8,128)S(1)} collective-permute-done((f32[16,128]{1,0:T(8,128)S(1)}, f32[16,128]{1,0:T(8,128)S(1)}, u32[]{:S(2)}, u32[]{:S(2)}) %collective-permute-start.1) | collective-permute-done | bytes 8224 | tf_op jit(solution)/shard_map/ppermute | solution.py:305
  17.5 0.7 %first.1 = (f32[8,4,2,8,128]{4,3,2,1,0:T(8,128)S(1)}, f32[8,4,2,8,128]{4,3,2,1,0:T(8,128)S(1)}, f32[4,864,128]{2,1,0:T(8,128)S(1)}) custom-call(f32[16,128]{1,0:T(8,128)S(1)} %get-tuple-element.21.table, f32[5,8,128]{2,1,0:T(8,128)S(1)} %get-tuple-element.20.masks, ...), custom_call_target="tpu_custom_call", output_to_operand_aliasing={{2}: (6, {}), {0}: (7, {}), {1}: (8, {})} | custom-call | bytes 1048576 | tf_op jit(solution)/shard_map/first/pallas_call | solution.py:335
  18.2 3.6 %all-gather = f32[16,4,2,8,128]{4,3,2,1,0:T(8,128)S(1)} all-gather(f32[8,4,2,8,128]{4,3,2,1,0:T(8,128)S(1)} %get-tuple-element.28), channel_id=2, replica_groups={{0,32},{64,96},{128,160},{192,224},{256,288},{320,352},{384,416},{448,4..., dimensions={0}, use_global_device_ids=true | all-gather | bytes 786432 | tf_op jit(solution)/shard_map/all_gather | solution.py:346
  21.8 0.1 merge.1
  21.8 21.6 %all_to_all.5.slabs = f32[8,4,2,8,128]{4,3,2,1,0:T(8,128)S(1)} all-to-all(f32[8,4,2,8,128]{4,3,2,1,0:T(8,128)S(1)} %merge.1), channel_id=1, replica_groups={{0,64,128,192,256,320,384,448},{32,96,160,224,288,352,416,480},{1,65,12..., dimensions={0} | all-to-all | bytes 524288 | tf_op jit(solution)/shard_map/all_to_all | solution.py:349
  43.4 0.7 %composite.1 = f32[4,4,4,128]{3,2,1,0:T(4,128)} custom-call(f32[5,8,128]{2,1,0:T(8,128)S(1)} %get-tuple-element.20.masks, f32[8,4,2,8,128]{4,3,2,1,0:T(8,128)S(1)} %all_to_all.5.slabs), custom_call_target="tpu_custom_call" | custom-call | bytes 1048576 | tf_op jit(solution)/shard_map/composite/pallas_call | solution.py:350
  (2 shorter events, 0.0 us)
Async XLA Ops:
  0.0 11.8 %copy-start.4 = (s32[4]{0:T(128)S(1)}, s32[4]{0:T(128)}, u32[]{:S(2)}) copy-start(s32[4]{0:T(128)} %refs_4_.1) | copy-start | bytes 52
  0.0 11.8 %copy-start.3 = (s32[4]{0:T(128)S(1)}, s32[4]{0:T(128)}, u32[]{:S(2)}) copy-start(s32[4]{0:T(128)} %refs_3_.1) | copy-start | bytes 52
  0.0 11.8 %copy-start.2 = (f32[3]{0:T(128)S(1)}, f32[3]{0:T(128)}, u32[]{:S(2)}) copy-start(f32[3]{0:T(128)} %refs_2_.1) | copy-start | bytes 40
  0.0 11.8 %copy-start.1 = (f32[3]{0:T(128)S(1)}, f32[3]{0:T(128)}, u32[]{:S(2)}) copy-start(f32[3]{0:T(128)} %refs_1_.1) | copy-start | bytes 40
  0.0 1.0 %copy-start.5 = (f32[8,64,128]{2,1,0:T(8,128)S(1)}, f32[8,64,128]{2,1,0:T(8,128)}, u32[]{:S(2)}) copy-start(f32[8,64,128]{2,1,0:T(8,128)} %density.1) | copy-start | bytes 786436
  1.0 10.8 %copy-start = (f32[3]{0:T(128)S(1)}, f32[3]{0:T(128)}, u32[]{:S(2)}) copy-start(f32[3]{0:T(128)} %refs_0_.1) | copy-start | bytes 40
  1.1 3.1 %collective-permute-start = (f32[2,64,128]{2,1,0:T(8,128)S(1)}, f32[2,64,128]{2,1,0:T(8,128)S(1)}, u32[]{:S(2)}, u32[]{:S(2)}) collective-permute-start(f32[2,64,128]{2,1,0:T(8,128)S(1)} %get-tuple-element.18), channel_id=1, source_target_pairs={{32,0},{64,32},{96,64},{128,96},{160,128},{192,160},{224,192},{256... | collective-permute-start | bytes 196616 | tf_op jit(solution)/shard_map/ppermute | solution.py:299
  4.2 9.8 %collective-permute-start.2 = (f32[10,32,128]{2,1,0:T(8,128)S(1)}, f32[10,32,128]{2,1,0:T(8,128)S(1)}, u32[]{:S(2)}, u32[]{:S(2)}) collective-permute-start(f32[10,32,128]{2,1,0:T(8,128)S(1)} %get-tuple-element.23), channel_id=1, source_target_pairs={{1,0},{2,1},{3,2},{4,3},{5,4},{6,5},{7,6},{8,7},{9,8},{10,9},{11,1... | collective-permute-start | bytes 491528 | tf_op jit(solution)/shard_map/ppermute | solution.py:304
  9.9 7.7 %collective-permute-start.1 = (f32[16,128]{1,0:T(8,128)S(1)}, f32[16,128]{1,0:T(8,128)S(1)}, u32[]{:S(2)}, u32[]{:S(2)}) collective-permute-start(f32[16,128]{1,0:T(8,128)S(1)} %get-tuple-element.19.refs_7_), channel_id=1, source_target_pairs={{0,1},{1,2},{2,3},{3,4},{4,5},{5,6},{6,7},{7,8},{8,9},{9,10},{10,1... | collective-permute-start | bytes 24584 | tf_op jit(solution)/shard_map/ppermute | solution.py:305

commit v8 on v3

--- a/solution.py
+++ b/solution.py
@@ -12,6 +12,7 @@
 HBM = pl.BlockSpec(memory_space=pltpu.HBM)
 PLANES, ROWS, COLS, SHEAR, VIEWS, GROUPS, BRICKS = 8, 64, 128, 32, 4, 16, 32
 TOP = 8
+HALF = ROWS // 2
 TALL = ROWS + SHEAR
 PADDED = TOP + TALL + 8
 SLABS = PLANES + 1
@@ -50,13 +51,13 @@
     return [strength * tone for tone in tones] + [optical]
 
 
-def load_kernel(density, own, low, high, semaphore):
+def load_kernel(density, own, one, two, semaphore):
     copy = pltpu.make_async_copy(density, own, semaphore)
     copy.start()
+    odd = lax.axis_index("height") % 2
     copy.wait()
-    high[...] = own[:, :SHEAR, :]
-    for plane in range(PLANES):
-        low[plane : plane + 1, :] = own[plane, ROWS - 1 : ROWS, :]
+    one[...] = own[:, pl.ds(pl.multiple_of(odd * HALF, HALF), HALF), :]
+    two[...] = own[:, pl.ds(pl.multiple_of((1 - odd) * HALF, HALF), HALF), :]
 
 
 def inner_kernel(*refs):
@@ -111,13 +112,15 @@
     lax.fori_loop(0, PLANES - 2, plane_of, 0)
 
 
-def join_kernel(own, low, high, table, brick, first):
+def join_kernel(own, one, two, table, brick, first):
     del table
+    odd = lax.axis_index("height") % 2 == 1
     for plane in range(PLANES):
+        low = jnp.where(odd, two[plane, HALF - 1 : HALF, :], one[plane, HALF - 1 : HALF, :])
         parts = (
-            (0, jnp.broadcast_to(low[plane : plane + 1, :], (8, COLS))),
+            (0, jnp.broadcast_to(low, (8, COLS))),
             (TOP, own[plane]),
-            (TOP + ROWS, high[plane]),
+            (TOP + ROWS, jnp.where(odd, one[plane, :SHEAR, :], two[plane, :SHEAR, :])),
             (TOP + TALL, jnp.zeros((8, COLS), jnp.float32)),
         )
         for start, part in parts:
@@ -267,17 +270,21 @@
 def on_device(density, light_vector, colour_gain, colour_bias, shear_step, reverse_view):
     heights, depths = lax.axis_size("height"), lax.axis_size("depth")
 
-    own, own_low, own_high = kernel(
+    half = array(PLANES, HALF, COLS)
+    own, own_one, own_two = kernel(
         load_kernel,
         "load",
-        (array(PLANES, ROWS, COLS), array(PLANES, COLS), array(PLANES, SHEAR, COLS)),
+        (array(PLANES, ROWS, COLS), half, half),
         [HBM],
         (VMEM,) * 3,
         flops=10**9,
         scratch_shapes=[pltpu.SemaphoreType.DMA],
     )(density)
-    high = lax.ppermute(own_high, "height", [(i + 1, i) for i in range(heights - 1)])
-    low = lax.ppermute(own_low, "height", [(i, i + 1) for i in range(heights - 1)])
+    swaps = [[(i, i + 1) for i in range(start, heights - 1, 2)] for start in (1, 0)]
+    one, two = [
+        lax.ppermute(mine, "height", pairs + [(j, i) for i, j in pairs])
+        for mine, pairs in zip((own_one, own_two), swaps)
+    ]
 
     fields, table, masks, starts = kernel(
         inner_kernel,
@@ -298,7 +305,7 @@
 
     brick, first = kernel(
         join_kernel, "join", (array(PLANES, PADDED, COLS), array(2, PADDED, COLS)), [VMEM] * 4, (VMEM,) * 2
-    )(own, low, high, table)
+    )(own, one, two, table)
     coming = lax.ppermute(first, "depth", [(i + 1, i) for i in range(depths - 1)])
 
     fields = kernel(

time: 46.9 us -> 46.2 us (0.985)
  waiting for transfers between devices: 5.12 us -> 4.36 us
    ppermute x2, waiting for transfers between devices: 3.79 us -> 3.03 us  [on_device(): lax.ppermute(mine, 'height', pairs + [(j, i) for i, j in pairs])]
where the time goes in v8:
time: 46.2 us; the launch traced here: 45.9 us
  blocking collectives  26.9 us (58%)
  starting transfers between devices  8.86 us (19%)
  Pallas kernels  4.61 us (10%)
  waiting for transfers between devices  4.36 us (9%)
  local copies, waits for them, and re-layouts  1.01 us (2%)
    all_to_all x1, blocking collectives, on_device(): lax.all_to_all(merged, 'depth', 0, 0, tiled=True, axis_index_groups=chips)  21.6 us
    ppermute x2, starting transfers between devices, on_device(): lax.ppermute(mine, 'height', pairs + [(j, i) for i, j in pairs])  7.56 us
    all_gather x1, blocking collectives, on_device(): gathered = lax.all_gather(given, 'depth', axis=0, axis_index_groups=cores)  5.27 us
    ppermute x2, waiting for transfers between devices, on_device(): lax.ppermute(mine, 'height', pairs + [(j, i) for i, j in pairs])  3.03 us
    pallas_call x1, Pallas kernels, on_device(): kernel(inner_kernel, 'inner', (array(4, SLABS * TALL, COLS), array(16, CO...  1.84 us
    pallas_call x1, Pallas kernels, on_device(): kernel(render_kernel, 'render', (part, part, array(4, SLABS * TALL, COLS)...  1.38 us
    ppermute x1, waiting for transfers between devices, on_device(): lax.ppermute(first, 'depth', [(i + 1, i) for i in range(depths - 1)])  1.33 us
    ppermute x1, starting transfers between devices, on_device(): lax.ppermute(first, 'depth', [(i + 1, i) for i in range(depths - 1)])  1.29 us
  transfers between devices with their start and end apart: 3, of which 2 were waited for; matrix products, arithmetic and copies ran while one was open for 0% of the time, Pallas kernels for 5%

profile of v8, /device:TPU:6, one launch (start us, length us, event | category | flops | bytes accessed | tf_op | source)
XLA Modules:
  0.0 45.9 jit_solution(16133410695236686463)
XLA Ops:
  0.0 0.0 copy-start.4
  0.0 0.0 copy-start.3
  0.0 0.0 copy-start.2
  0.0 0.0 copy-start.1
  0.0 0.0 copy-start.5
  0.0 1.0 %copy-done.5 = f32[8,64,128]{2,1,0:T(8,128)S(1)} copy-done((f32[8,64,128]{2,1,0:T(8,128)S(1)}, f32[8,64,128]{2,1,0:T(8,128)}, u32[]{:S(2)}) %copy-start.5) | copy-done | bytes 262168
  1.0 0.0 copy-start
  1.0 0.1 load.1
  1.1 5.6 %collective-permute-start = (f32[8,32,128]{2,1,0:T(8,128)S(1)}, f32[8,32,128]{2,1,0:T(8,128)S(1)}, u32[]{:S(2)}, u32[]{:S(2)}) collective-permute-start(f32[8,32,128]{2,1,0:T(8,128)S(1)} %get-tuple-element.20), channel_id=1, source_target_pairs={{1,2},{3,4},{5,6},{7,8},{9,10},{11,12},{13,14},{15,16},{17,18},{19... | collective-permute-start | bytes 393224 | tf_op jit(solution)/shard_map/ppermute | solution.py:285
  6.7 1.9 %collective-permute-start.1 = (f32[8,32,128]{2,1,0:T(8,128)S(1)}, f32[8,32,128]{2,1,0:T(8,128)S(1)}, u32[]{:S(2)}, u32[]{:S(2)}) collective-permute-start(f32[8,32,128]{2,1,0:T(8,128)S(1)} %get-tuple-element.21), channel_id=1, source_target_pairs={{0,1},{2,3},{4,5},{6,7},{8,9},{10,11},{12,13},{14,15},{16,17},{18,... | collective-permute-start | bytes 393224 | tf_op jit(solution)/shard_map/ppermute | solution.py:285
  8.7 0.0 copy-done.4
  8.7 0.0 copy-done.3
  8.7 0.0 copy-done.2
  8.7 0.0 copy-done.1
  8.7 0.0 copy-done
  8.7 1.8 %inner.1 = (f32[4,864,128]{2,1,0:T(8,128)S(1)}, f32[16,128]{1,0:T(8,128)S(1)}, f32[5,8,128]{2,1,0:T(8,128)S(1)}, s32[64]{0:T(128)S(1)}) custom-call(f32[3]{0:T(128)S(1)} %copy-done, f32[3]{0:T(128)S(1)} %copy-done.1, f32[3]{0:T(128)S(1)} %copy-done.2, s32[4]{0:T(128)S(1)} %copy-done.3, s32[4]{0:T(128)S(1)} %copy-done.4, ...), custom_call_target="tpu_custom_call" | custom-call | flops 10000000 | bytes 1048576 | tf_op jit(solution)/shard_map/inner/pallas_call | solution.py:289
  10.5 0.0 collective-permute-done.one
  10.6 3.0 %collective-permute-done.1.two = f32[8,32,128]{2,1,0:T(8,128)S(1)} collective-permute-done((f32[8,32,128]{2,1,0:T(8,128)S(1)}, f32[8,32,128]{2,1,0:T(8,128)S(1)}, u32[]{:S(2)}, u32[]{:S(2)}) %collective-permute-start.1) | collective-permute-done | bytes 131104 | tf_op jit(solution)/shard_map/ppermute | solution.py:285
  13.6 1.3 %collective-permute-start.2 = (f32[2,112,128]{2,1,0:T(8,128)S(1)}, f32[2,112,128]{2,1,0:T(8,128)S(1)}, u32[]{:S(2)}, u32[]{:S(2)}) collective-permute-start(f32[2,112,128]{2,1,0:T(8,128)S(1)} %get-tuple-element.23), channel_id=1, source_target_pairs={{32,0},{64,32},{96,64},{128,96},{160,128},{192,160},{224,192},{256... | collective-permute-start | bytes 344072 | tf_op jit(solution)/shard_map/ppermute | solution.py:309
  14.9 0.6 %edge.1.held = f32[4,864,128]{2,1,0:T(8,128)S(1)} custom-call(f32[16,128]{1,0:T(8,128)S(1)} %get-tuple-element.18.table, f32[8,112,128]{2,1,0:T(8,128)S(1)} %get-tuple-element.22.brick, f32[4,864,128]{2,1,0:T(8,128)S(1)} %get-tuple-element.24.held), custom_call_target="tpu_custom_call", output_to_operand_aliasing={{}: (2, {})} | custom-call | flops 10000000 | bytes 1048576 | tf_op jit(solution)/shard_map/edge/pallas_call | solution.py:311
  15.5 1.3 %collective-permute-done.2.coming = f32[2,112,128]{2,1,0:T(8,128)S(1)} collective-permute-done((f32[2,112,128]{2,1,0:T(8,128)S(1)}, f32[2,112,128]{2,1,0:T(8,128)S(1)}, u32[]{:S(2)}, u32[]{:S(2)}) %collective-permute-start.2) | collective-permute-done | bytes 114720 | tf_op jit(solution)/shard_map/ppermute | solution.py:309
  16.9 1.4 %render.1 = (f32[8,4,2,8,128]{4,3,2,1,0:T(8,128)S(1)}, f32[8,4,2,8,128]{4,3,2,1,0:T(8,128)S(1)}, f32[4,864,128]{2,1,0:T(8,128)S(1)}) custom-call(f32[16,128]{1,0:T(8,128)S(1)} %get-tuple-element.18.table, f32[5,8,128]{2,1,0:T(8,128)S(1)} %get-tuple-element.17.masks, s32[64]{0:T(128)S(1)} %get-tuple-element.19.starts_in, ...), custom_call_target="tpu_custom_call", output_to_operand_aliasing={{2}: (5, {})} | custom-call | bytes 1048576 | tf_op jit(solution)/shard_map/render/pallas_call | solution.py:322
  18.2 5.3 %all-gather = f32[16,4,2,8,128]{4,3,2,1,0:T(8,128)S(1)} all-gather(f32[8,4,2,8,128]{4,3,2,1,0:T(8,128)S(1)} %get-tuple-element.26), channel_id=2, replica_groups={{0,32},{64,96},{128,160},{192,224},{256,288},{320,352},{384,416},{448,4..., dimensions={0}, use_global_device_ids=true | all-gather | bytes 786432 | tf_op jit(solution)/shard_map/all_gather | solution.py:333
  23.5 0.1 merge.1
  23.6 21.6 %all_to_all.5.slabs = f32[8,4,2,8,128]{4,3,2,1,0:T(8,128)S(1)} all-to-all(f32[8,4,2,8,128]{4,3,2,1,0:T(8,128)S(1)} %merge.1), channel_id=1, replica_groups={{0,64,128,192,256,320,384,448},{32,96,160,224,288,352,416,480},{1,65,12..., dimensions={0} | all-to-all | bytes 524288 | tf_op jit(solution)/shard_map/all_to_all | solution.py:336
  45.2 0.7 %composite.1 = f32[4,4,4,128]{3,2,1,0:T(4,128)} custom-call(f32[5,8,128]{2,1,0:T(8,128)S(1)} %get-tuple-element.17.masks, f32[8,4,2,8,128]{4,3,2,1,0:T(8,128)S(1)} %all_to_all.5.slabs), custom_call_target="tpu_custom_call" | custom-call | bytes 1048576 | tf_op jit(solution)/shard_map/composite/pallas_call | solution.py:337
  (1 shorter events, 0.0 us)
Async XLA Ops:
  0.0 8.7 %copy-start.4 = (s32[4]{0:T(128)S(1)}, s32[4]{0:T(128)}, u32[]{:S(2)}) copy-start(s32[4]{0:T(128)} %refs_4_.1) | copy-start | bytes 52
  0.0 8.7 %copy-start.3 = (s32[4]{0:T(128)S(1)}, s32[4]{0:T(128)}, u32[]{:S(2)}) copy-start(s32[4]{0:T(128)} %refs_3_.1) | copy-start | bytes 52
  0.0 8.7 %copy-start.2 = (f32[3]{0:T(128)S(1)}, f32[3]{0:T(128)}, u32[]{:S(2)}) copy-start(f32[3]{0:T(128)} %refs_2_.1) | copy-start | bytes 40
  0.0 8.7 %copy-start.1 = (f32[3]{0:T(128)S(1)}, f32[3]{0:T(128)}, u32[]{:S(2)}) copy-start(f32[3]{0:T(128)} %refs_1_.1) | copy-start | bytes 40
  0.0 1.0 %copy-start.5 = (f32[8,64,128]{2,1,0:T(8,128)S(1)}, f32[8,64,128]{2,1,0:T(8,128)}, u32[]{:S(2)}) copy-start(f32[8,64,128]{2,1,0:T(8,128)} %density.1) | copy-start | bytes 786436
  1.0 7.7 %copy-start = (f32[3]{0:T(128)S(1)}, f32[3]{0:T(128)}, u32[]{:S(2)}) copy-start(f32[3]{0:T(128)} %refs_0_.1) | copy-start | bytes 40
  1.1 9.5 %collective-permute-start = (f32[8,32,128]{2,1,0:T(8,128)S(1)}, f32[8,32,128]{2,1,0:T(8,128)S(1)}, u32[]{:S(2)}, u32[]{:S(2)}) collective-permute-start(f32[8,32,128]{2,1,0:T(8,128)S(1)} %get-tuple-element.20), channel_id=1, source_target_pairs={{1,2},{3,4},{5,6},{7,8},{9,10},{11,12},{13,14},{15,16},{17,18},{19... | collective-permute-start | bytes 393224 | tf_op jit(solution)/shard_map/ppermute | solution.py:285
  6.7 6.9 %collective-permute-start.1 = (f32[8,32,128]{2,1,0:T(8,128)S(1)}, f32[8,32,128]{2,1,0:T(8,128)S(1)}, u32[]{:S(2)}, u32[]{:S(2)}) collective-permute-start(f32[8,32,128]{2,1,0:T(8,128)S(1)} %get-tuple-element.21), channel_id=1, source_target_pairs={{0,1},{2,3},{4,5},{6,7},{8,9},{10,11},{12,13},{14,15},{16,17},{18,... | collective-permute-start | bytes 393224 | tf_op jit(solution)/shard_map/ppermute | solution.py:285
  13.6 3.2 %collective-permute-start.2 = (f32[2,112,128]{2,1,0:T(8,128)S(1)}, f32[2,112,128]{2,1,0:T(8,128)S(1)}, u32[]{:S(2)}, u32[]{:S(2)}) collective-permute-start(f32[2,112,128]{2,1,0:T(8,128)S(1)} %get-tuple-element.23), channel_id=1, source_target_pairs={{32,0},{64,32},{96,64},{128,96},{160,128},{192,160},{224,192},{256... | collective-permute-start | bytes 344072 | tf_op jit(solution)/shard_map/ppermute | solution.py:309

commit v9 on v7

--- a/solution.py
+++ b/solution.py
@@ -116,7 +116,9 @@
         fields[kind, rows, :] = values[kind]
 
 
-def cut_kernel(own, coming, high, low):
+def cut_kernel(own, pair, across, coming, high, low):
+    odd = lax.axis_index("depth") % 2 == 1
+    coming[...] = jnp.where(odd, across[...], pair[1])
     high[:PLANES] = own[:, :SHEAR, :]
     high[PLANES:] = coming[:, :SHEAR, :]
     for plane in range(PLANES):
@@ -124,8 +126,12 @@
     low[PLANES:, :] = jnp.broadcast_to(coming[0, ROWS - 1 : ROWS, :], (8, COLS))
 
 
-def edge_kernel(table, own, coming, high, held, fields, brick):
+def render_kernel(
+    table, masks, starts_in, own, coming, high, held, given, kept, fields, brick, starts, semaphore
+):
     del held
+    copy = pltpu.make_async_copy(starts_in, starts, semaphore)
+    copy.start()
     coefficient = lambda at: table[at : at + 1, :]
     for plane in range(PLANES + 2):
         source = own.at[plane] if plane < PLANES else coming.at[plane - PLANES]
@@ -157,10 +163,6 @@
     def _():
         rows_of(0, None, PLAIN, BEYOND)
 
-
-def render_kernel(masks, starts_in, fields, given, kept, starts, semaphore):
-    copy = pltpu.make_async_copy(starts_in, starts, semaphore)
-    copy.start()
     copy.wait()
     render(masks, starts, fields, given, kept, 1, ROWS // 8)
 
@@ -296,11 +298,17 @@
         flops=10**9,
         scratch_shapes=[pltpu.SemaphoreType.DMA],
     )(density)
-    coming = lax.ppermute(first, "depth", [(i + 1, i) for i in range(depths - 1)])
-
-    own_high, own_low = kernel(
-        cut_kernel, "cut", (array(PLANES + 2, SHEAR, COLS), array(PLANES + 8, COLS)), [VMEM] * 2, (VMEM,) * 2
-    )(own, coming)
+    cores = [[2 * chip, 2 * chip + 1] for chip in range(CHIPS)]
+    across = lax.ppermute(first, "depth", [(i + 1, i) for i in range(1, depths - 1, 2)])
+    pair = lax.all_gather(first, "depth", axis=0, axis_index_groups=cores)
+
+    coming, own_high, own_low = kernel(
+        cut_kernel,
+        "cut",
+        (array(2, ROWS, COLS), array(PLANES + 2, SHEAR, COLS), array(PLANES + 8, COLS)),
+        [VMEM] * 3,
+        (VMEM,) * 3,
+    )(own, pair, across)
     high = lax.ppermute(own_high, "height", [(i + 1, i) for i in range(heights - 1)])
     low = lax.ppermute(own_low, "height", [(i, i + 1) for i in range(heights - 1)])
 
@@ -316,22 +324,18 @@
         + [pltpu.SMEM((VIEWS,), jnp.int32)] * 2
         + [pltpu.SemaphoreType.DMA((5,))],
     )(light_vector, colour_gain, colour_bias, shear_step, reverse_view, own, coming, own_low)
-    fields = kernel(
-        edge_kernel,
-        "edge",
-        shaded,
-        [VMEM] * 5,
-        VMEM,
-        flops=10**7,
-        input_output_aliases={4: 0},
-        scratch_shapes=[pltpu.VMEM((PLANES + 2, 24 + SHEAR, COLS), jnp.float32)],
-    )(table, own, coming, high, fields)
-
     part = array(CHIPS, 4, VIEWS // 2, 8, COLS)
     memory = [pltpu.SMEM((64,), jnp.int32), pltpu.SemaphoreType.DMA]
-    given, kept = kernel(
-        render_kernel, "render", (part, part), [VMEM, ANY, VMEM], (VMEM,) * 2, flops=10**7, scratch_shapes=memory
-    )(masks, starts, fields)
+    given, kept, fields = kernel(
+        render_kernel,
+        "render",
+        (part, part, shaded),
+        [VMEM, VMEM, ANY] + [VMEM] * 4,
+        (VMEM,) * 3,
+        flops=10**7,
+        input_output_aliases={6: 2},
+        scratch_shapes=[pltpu.VMEM((PLANES + 2, 24 + SHEAR, COLS), jnp.float32), *memory],
+    )(table, masks, starts, own, coming, high, fields)
     given, kept, _ = kernel(
         first_kernel,
         "first",
@@ -342,7 +346,6 @@
         scratch_shapes=memory,
     )(table, masks, starts, own, coming, low, fields, given, kept)
 
-    cores = [[2 * chip, 2 * chip + 1] for chip in range(CHIPS)]
     gathered = lax.all_gather(given, "depth", axis=0, axis_index_groups=cores)
     merged = kernel(merge_kernel, "merge", part, [VMEM] * 3, VMEM)(masks, kept, gathered)
     chips = [[core + 2 * chip for chip in range(CHIPS)] for core in range(2)]

time: 44.3 us -> 44.3 us (level)
  blocking collectives: 25.2 us -> 27.6 us
  waiting for transfers between devices: 3.3 us -> 1.99 us
  starting transfers between devices: 8.86 us -> 8.23 us
  Pallas kernels: 5.62 us -> 5.1 us
    all_gather x0 -> x1, blocking collectives: none -> 2.01 us  [on_device(): pair = lax.all_gather(first, 'depth', axis=0, axis_index_groups=cores)]
    ppermute x1, waiting for transfers between devices: 1.85 us -> 0.01 us  [on_device(): lax.ppermute(first, 'depth', [(i + 1, i) for i in range(1, depths - 1, 2)])]
    ppermute x1, starting transfers between devices: 1.29 us -> 0.66 us  [on_device(): lax.ppermute(first, 'depth', [(i + 1, i) for i in range(1, depths - 1, 2)])]
    all_to_all x1, blocking collectives: 21.6 us -> 22.2 us  [on_device(): lax.all_to_all(merged, 'depth', 0, 0, tiled=True, axis_index_groups=chips)]
    ppermute x1, waiting for transfers between devices: 1.45 us -> 1.98 us  [on_device(): lax.ppermute(own_low, 'height', [(i, i + 1) for i in range(heights - 1)])]
    pallas_call x3 -> x2, Pallas kernels: 2.05 us -> 1.53 us  [the longest x1 1.5 us: on_device(): kernel(render_kernel, 'render', (part, part, shaded), [VMEM, VMEM, ANY] +...]
  transfers between devices with their start and end apart: 3 -> 3, of which waited for: 2 -> 1; matrix products, arithmetic and copies ran while one was open for 0% -> 0% of each run, Pallas kernels for 10% -> 8%
where the time goes in v9:
time: 44.3 us; the launch traced here: 44.1 us
  blocking collectives  27.6 us (62%)
  starting transfers between devices  8.23 us (19%)
  Pallas kernels  5.1 us (12%)
  waiting for transfers between devices  1.99 us (4%)
  local copies, waits for them, and re-layouts  1.01 us (2%)
    all_to_all x1, blocking collectives, on_device(): lax.all_to_all(merged, 'depth', 0, 0, tiled=True, axis_index_groups=chips)  22.2 us
    ppermute x1, starting transfers between devices, on_device(): lax.ppermute(own_high, 'height', [(i + 1, i) for i in range(heights - 1)])  5.64 us
    all_gather x1, blocking collectives, on_device(): gathered = lax.all_gather(given, 'depth', axis=0, axis_index_groups=cores)  3.4 us
    pallas_call x1, Pallas kernels, on_device(): kernel(inner_kernel, 'inner', (shaded, array(16, COLS), array(5, 8, COLS)...  2.16 us
    all_gather x1, blocking collectives, on_device(): pair = lax.all_gather(first, 'depth', axis=0, axis_index_groups=cores)  2.01 us
    ppermute x1, waiting for transfers between devices, on_device(): lax.ppermute(own_low, 'height', [(i, i + 1) for i in range(heights - 1)])  1.98 us
    ppermute x1, starting transfers between devices, on_device(): lax.ppermute(own_low, 'height', [(i, i + 1) for i in range(heights - 1)])  1.92 us
    pallas_call x1, Pallas kernels, on_device(): kernel(render_kernel, 'render', (part, part, shaded), [VMEM, VMEM, ANY] +...  1.5 us
  transfers between devices with their start and end apart: 3, of which 1 were waited for; matrix products, arithmetic and copies ran while one was open for 0% of the time, Pallas kernels for 8%

profile of v9, /device:TPU:6, one launch (start us, length us, event | category | flops | bytes accessed | tf_op | source)
XLA Modules:
  0.0 44.1 jit_solution(11164383185544057184)
XLA Ops:
  0.0 0.0 copy-start.4
  0.0 0.0 copy-start.3
  0.0 0.0 copy-start.2
  0.0 0.0 copy-start.1
  0.0 0.0 copy-start.5
  0.0 1.0 %copy-done.5 = f32[8,64,128]{2,1,0:T(8,128)S(1)} copy-done((f32[8,64,128]{2,1,0:T(8,128)S(1)}, f32[8,64,128]{2,1,0:T(8,128)}, u32[]{:S(2)}) %copy-start.5) | copy-done | bytes 262168
  1.0 0.0 copy-start
  1.1 0.7 %collective-permute-start = (f32[2,64,128]{2,1,0:T(8,128)S(1)}, f32[2,64,128]{2,1,0:T(8,128)S(1)}, u32[]{:S(2)}, u32[]{:S(2)}) collective-permute-start(f32[2,64,128]{2,1,0:T(8,128)S(1)} %get-tuple-element.20), channel_id=1, source_target_pairs={{64,32},{128,96},{192,160},{256,224},{320,288},{384,352},{448,416}... | collective-permute-start | bytes 196616 | tf_op jit(solution)/shard_map/ppermute | solution.py:302
  1.7 2.0 %all-gather = f32[4,64,128]{2,1,0:T(8,128)S(1)} all-gather(f32[2,64,128]{2,1,0:T(8,128)S(1)} %get-tuple-element.20), channel_id=2, replica_groups={{0,32},{64,96},{128,160},{192,224},{256,288},{320,352},{384,416},{448,4..., dimensions={0}, use_global_device_ids=true | all-gather | bytes 196608 | tf_op jit(solution)/shard_map/all_gather | solution.py:303
  3.7 0.0 collective-permute-done.across
  3.8 5.6 %collective-permute-start.2 = (f32[10,32,128]{2,1,0:T(8,128)S(1)}, f32[10,32,128]{2,1,0:T(8,128)S(1)}, u32[]{:S(2)}, u32[]{:S(2)}) collective-permute-start(f32[10,32,128]{2,1,0:T(8,128)S(1)} %get-tuple-element.26), channel_id=1, source_target_pairs={{1,0},{2,1},{3,2},{4,3},{5,4},{6,5},{7,6},{8,7},{9,8},{10,9},{11,1... | collective-permute-start | bytes 491528 | tf_op jit(solution)/shard_map/ppermute | solution.py:312
  9.4 1.9 %collective-permute-start.1 = (f32[16,128]{1,0:T(8,128)S(1)}, f32[16,128]{1,0:T(8,128)S(1)}, u32[]{:S(2)}, u32[]{:S(2)}) collective-permute-start(f32[16,128]{1,0:T(8,128)S(1)} %get-tuple-element.22.refs_7_), channel_id=1, source_target_pairs={{0,1},{1,2},{2,3},{3,4},{4,5},{5,6},{6,7},{7,8},{8,9},{9,10},{10,1... | collective-permute-start | bytes 24584 | tf_op jit(solution)/shard_map/ppermute | solution.py:313
  11.4 0.0 copy-done.4
  11.4 0.0 copy-done.3
  11.4 0.0 copy-done.2
  11.4 0.0 copy-done.1
  11.4 0.0 copy-done
  11.4 2.2 %inner.1 = (f32[4,864,128]{2,1,0:T(8,128)S(1)}, f32[16,128]{1,0:T(8,128)S(1)}, f32[5,8,128]{2,1,0:T(8,128)S(1)}, s32[64]{0:T(128)S(1)}) custom-call(f32[3]{0:T(128)S(1)} %copy-done, f32[3]{0:T(128)S(1)} %copy-done.1, f32[3]{0:T(128)S(1)} %copy-done.2, s32[4]{0:T(128)S(1)} %copy-done.3, s32[4]{0:T(128)S(1)} %copy-done.4, ...), custom_call_target="tpu_custom_call" | custom-call | flops 10000000 | bytes 1048576 | tf_op jit(solution)/shard_map/inner/pallas_call | solution.py:316
  13.6 0.0 collective-permute-done.2.high
  13.6 1.5 %render.1 = (f32[8,4,2,8,128]{4,3,2,1,0:T(8,128)S(1)}, f32[8,4,2,8,128]{4,3,2,1,0:T(8,128)S(1)}, f32[4,864,128]{2,1,0:T(8,128)S(1)}) custom-call(f32[16,128]{1,0:T(8,128)S(1)} %get-tuple-element.24.table, f32[5,8,128]{2,1,0:T(8,128)S(1)} %get-tuple-element.23.masks, s32[64]{0:T(128)S(1)} %get-tuple-element.25.starts_in, ...), custom_call_target="tpu_custom_call", output_to_operand_aliasing={{2}: (6, {})} | custom-call | flops 10000000 | bytes 1048576 | tf_op jit(solution)/shard_map/render/pallas_call | solution.py:329
  15.1 2.0 %collective-permute-done.1.low = f32[16,128]{1,0:T(8,128)S(1)} collective-permute-done((f32[16,128]{1,0:T(8,128)S(1)}, f32[16,128]{1,0:T(8,128)S(1)}, u32[]{:S(2)}, u32[]{:S(2)}) %collective-permute-start.1) | collective-permute-done | bytes 8224 | tf_op jit(solution)/shard_map/ppermute | solution.py:313
  17.1 0.7 %first.1 = (f32[8,4,2,8,128]{4,3,2,1,0:T(8,128)S(1)}, f32[8,4,2,8,128]{4,3,2,1,0:T(8,128)S(1)}, f32[4,864,128]{2,1,0:T(8,128)S(1)}) custom-call(f32[16,128]{1,0:T(8,128)S(1)} %get-tuple-element.24.table, f32[5,8,128]{2,1,0:T(8,128)S(1)} %get-tuple-element.23.masks, ...), custom_call_target="tpu_custom_call", output_to_operand_aliasing={{2}: (6, {}), {0}: (7, {}), {1}: (8, {})} | custom-call | bytes 1048576 | tf_op jit(solution)/shard_map/first/pallas_call | solution.py:339
  17.7 3.4 %all-gather.1 = f32[16,4,2,8,128]{4,3,2,1,0:T(8,128)S(1)} all-gather(f32[8,4,2,8,128]{4,3,2,1,0:T(8,128)S(1)} %get-tuple-element.32), channel_id=3, replica_groups={{0,32},{64,96},{128,160},{192,224},{256,288},{320,352},{384,416},{448,4..., dimensions={0}, use_global_device_ids=true | all-gather | bytes 786432 | tf_op jit(solution)/shard_map/all_gather | solution.py:349
  21.1 0.1 merge.1
  21.2 22.2 %all_to_all.5.slabs = f32[8,4,2,8,128]{4,3,2,1,0:T(8,128)S(1)} all-to-all(f32[8,4,2,8,128]{4,3,2,1,0:T(8,128)S(1)} %merge.1), channel_id=1, replica_groups={{0,64,128,192,256,320,384,448},{32,96,160,224,288,352,416,480},{1,65,12..., dimensions={0} | all-to-all | bytes 524288 | tf_op jit(solution)/shard_map/all_to_all | solution.py:352
  43.4 0.7 %composite.1 = f32[4,4,4,128]{3,2,1,0:T(4,128)} custom-call(f32[5,8,128]{2,1,0:T(8,128)S(1)} %get-tuple-element.23.masks, f32[8,4,2,8,128]{4,3,2,1,0:T(8,128)S(1)} %all_to_all.5.slabs), custom_call_target="tpu_custom_call" | custom-call | bytes 1048576 | tf_op jit(solution)/shard_map/composite/pallas_call | solution.py:353
  (2 shorter events, 0.1 us)
Async XLA Ops:
  0.0 11.4 %copy-start.4 = (s32[4]{0:T(128)S(1)}, s32[4]{0:T(128)}, u32[]{:S(2)}) copy-start(s32[4]{0:T(128)} %refs_4_.1) | copy-start | bytes 52
  0.0 11.4 %copy-start.3 = (s32[4]{0:T(128)S(1)}, s32[4]{0:T(128)}, u32[]{:S(2)}) copy-start(s32[4]{0:T(128)} %refs_3_.1) | copy-start | bytes 52
  0.0 11.4 %copy-start.2 = (f32[3]{0:T(128)S(1)}, f32[3]{0:T(128)}, u32[]{:S(2)}) copy-start(f32[3]{0:T(128)} %refs_2_.1) | copy-start | bytes 40
  0.0 11.4 %copy-start.1 = (f32[3]{0:T(128)S(1)}, f32[3]{0:T(128)}, u32[]{:S(2)}) copy-start(f32[3]{0:T(128)} %refs_1_.1) | copy-start | bytes 40
  0.0 1.0 %copy-start.5 = (f32[8,64,128]{2,1,0:T(8,128)S(1)}, f32[8,64,128]{2,1,0:T(8,128)}, u32[]{:S(2)}) copy-start(f32[8,64,128]{2,1,0:T(8,128)} %density.1) | copy-start | bytes 786436
  1.0 10.4 %copy-start = (f32[3]{0:T(128)S(1)}, f32[3]{0:T(128)}, u32[]{:S(2)}) copy-start(f32[3]{0:T(128)} %refs_0_.1) | copy-start | bytes 40
  1.1 2.7 %collective-permute-start = (f32[2,64,128]{2,1,0:T(8,128)S(1)}, f32[2,64,128]{2,1,0:T(8,128)S(1)}, u32[]{:S(2)}, u32[]{:S(2)}) collective-permute-start(f32[2,64,128]{2,1,0:T(8,128)S(1)} %get-tuple-element.20), channel_id=1, source_target_pairs={{64,32},{128,96},{192,160},{256,224},{320,288},{384,352},{448,416}... | collective-permute-start | bytes 196616 | tf_op jit(solution)/shard_map/ppermute | solution.py:302
  3.8 9.8 %collective-permute-start.2 = (f32[10,32,128]{2,1,0:T(8,128)S(1)}, f32[10,32,128]{2,1,0:T(8,128)S(1)}, u32[]{:S(2)}, u32[]{:S(2)}) collective-permute-start(f32[10,32,128]{2,1,0:T(8,128)S(1)} %get-tuple-element.26), channel_id=1, source_target_pairs={{1,0},{2,1},{3,2},{4,3},{5,4},{6,5},{7,6},{8,7},{9,8},{10,9},{11,1... | collective-permute-start | bytes 491528 | tf_op jit(solution)/shard_map/ppermute | solution.py:312
  9.4 7.7 %collective-permute-start.1 = (f32[16,128]{1,0:T(8,128)S(1)}, f32[16,128]{1,0:T(8,128)S(1)}, u32[]{:S(2)}, u32[]{:S(2)}) collective-permute-start(f32[16,128]{1,0:T(8,128)S(1)} %get-tuple-element.22.refs_7_), channel_id=1, source_target_pairs={{0,1},{1,2},{2,3},{3,4},{4,5},{5,6},{6,7},{7,8},{8,9},{9,10},{10,1... | collective-permute-start | bytes 24584 | tf_op jit(solution)/shard_map/ppermute | solution.py:313

commit v10 on v9

--- a/solution.py
+++ b/solution.py
@@ -74,7 +74,7 @@
         table[row : row + 1, :] = jnp.full((1, COLS), scalar, jnp.float32)
     upper = lax.broadcasted_iota(jnp.int32, (8, COLS), 0) < SHARE
     core = depth % 2
-    for base, digit in ((FRONT, core), (BACK, 1)):
+    for base, digit in ((FRONT, core), (BACK, 1 - core)):
         for pair in range(VIEWS // 2):
             first = jnp.where(reverse[2 * pair] == digit, 1.0, 0.0)
             second = jnp.where(reverse[2 * pair + 1] == digit, 1.0, 0.0)
@@ -236,18 +236,20 @@
 
 def merge_kernel(masks, kept, gathered, out):
     odd = masks[CORE] > 0.5
+    core = lax.axis_index("depth") % 2
     for pair in range(VIEWS // 2):
         mine_front = masks[FRONT + pair] > 0.5
 
         def merge(chip, _):
+            place = jnp.where(core == 1, CHIPS - 1 - chip, chip)
             mine = [kept[chip, kind, pair] for kind in range(4)]
             other = [jnp.where(odd, gathered[0, chip, kind, pair], gathered[1, chip, kind, pair]) for kind in range(4)]
             through = jnp.exp(-jnp.where(mine_front, mine[3], other[3]))
             for kind in range(3):
                 front = jnp.where(mine_front, mine[kind], other[kind])
                 behind = jnp.where(mine_front, other[kind], mine[kind])
-                out[chip, kind, pair] = front + through * behind
-            out[chip, 3, pair] = mine[3] + other[3]
+                out[place, kind, pair] = front + through * behind
+            out[place, 3, pair] = mine[3] + other[3]
             return 0
 
         lax.fori_loop(0, CHIPS, merge, 0, unroll=True)
@@ -348,7 +350,7 @@
 
     gathered = lax.all_gather(given, "depth", axis=0, axis_index_groups=cores)
     merged = kernel(merge_kernel, "merge", part, [VMEM] * 3, VMEM)(masks, kept, gathered)
-    chips = [[core + 2 * chip for chip in range(CHIPS)] for core in range(2)]
+    chips = [[2 * chip for chip in range(CHIPS)], [2 * chip + 1 for chip in reversed(range(CHIPS))]]
     slabs = lax.all_to_all(merged, "depth", 0, 0, tiled=True, axis_index_groups=chips)
     return kernel(final_kernel, "composite", array(4, VIEWS, SHARE, COLS), [VMEM] * 2, VMEM)(masks, slabs)
 

time: 44.3 us -> 42.7 us (0.964)
  blocking collectives: 27.6 us -> 26 us
    all_to_all x1, blocking collectives: 22.2 us -> 20.6 us  [on_device(): lax.all_to_all(merged, 'depth', 0, 0, tiled=True, axis_index_groups=chips)]
  transfers between devices with their start and end apart: 3 -> 3, of which waited for: 1 -> 1; matrix products, arithmetic and copies ran while one was open for 0% -> 0% of each run, Pallas kernels for 8% -> 9%
where the time goes in v10:
time: 42.7 us; the launch traced here: 42.4 us
  blocking collectives  26 us (61%)
  starting transfers between devices  8.23 us (19%)
  Pallas kernels  5.1 us (12%)
  waiting for transfers between devices  1.99 us (5%)
  local copies, waits for them, and re-layouts  1.01 us (2%)
    all_to_all x1, blocking collectives, on_device(): lax.all_to_all(merged, 'depth', 0, 0, tiled=True, axis_index_groups=chips)  20.6 us
    ppermute x1, starting transfers between devices, on_device(): lax.ppermute(own_high, 'height', [(i + 1, i) for i in range(heights - 1)])  5.64 us
    all_gather x1, blocking collectives, on_device(): gathered = lax.all_gather(given, 'depth', axis=0, axis_index_groups=cores)  3.4 us
    pallas_call x1, Pallas kernels, on_device(): kernel(inner_kernel, 'inner', (shaded, array(16, COLS), array(5, 8, COLS)...  2.16 us
    all_gather x1, blocking collectives, on_device(): pair = lax.all_gather(first, 'depth', axis=0, axis_index_groups=cores)  2.01 us
    ppermute x1, waiting for transfers between devices, on_device(): lax.ppermute(own_low, 'height', [(i, i + 1) for i in range(heights - 1)])  1.98 us
    ppermute x1, starting transfers between devices, on_device(): lax.ppermute(own_low, 'height', [(i, i + 1) for i in range(heights - 1)])  1.92 us
    pallas_call x1, Pallas kernels, on_device(): kernel(render_kernel, 'render', (part, part, shaded), [VMEM, VMEM, ANY] +...  1.5 us
  transfers between devices with their start and end apart: 3, of which 1 were waited for; matrix products, arithmetic and copies ran while one was open for 0% of the time, Pallas kernels for 9%

profile of v10, /device:TPU:6, one launch (start us, length us, event | category | flops | bytes accessed | tf_op | source)
XLA Modules:
  0.0 42.4 jit_solution(6254763903416429234)
XLA Ops:
  0.0 0.0 copy-start.4
  0.0 0.0 copy-start.3
  0.0 0.0 copy-start.2
  0.0 0.0 copy-start.1
  0.0 0.0 copy-start.5
  0.0 1.0 %copy-done.5 = f32[8,64,128]{2,1,0:T(8,128)S(1)} copy-done((f32[8,64,128]{2,1,0:T(8,128)S(1)}, f32[8,64,128]{2,1,0:T(8,128)}, u32[]{:S(2)}) %copy-start.5) | copy-done | bytes 262168
  1.0 0.0 copy-start
  1.1 0.7 %collective-permute-start = (f32[2,64,128]{2,1,0:T(8,128)S(1)}, f32[2,64,128]{2,1,0:T(8,128)S(1)}, u32[]{:S(2)}, u32[]{:S(2)}) collective-permute-start(f32[2,64,128]{2,1,0:T(8,128)S(1)} %get-tuple-element.20), channel_id=1, source_target_pairs={{64,32},{128,96},{192,160},{256,224},{320,288},{384,352},{448,416}... | collective-permute-start | bytes 196616 | tf_op jit(solution)/shard_map/ppermute | solution.py:304
  1.7 2.0 %all-gather = f32[4,64,128]{2,1,0:T(8,128)S(1)} all-gather(f32[2,64,128]{2,1,0:T(8,128)S(1)} %get-tuple-element.20), channel_id=2, replica_groups={{0,32},{64,96},{128,160},{192,224},{256,288},{320,352},{384,416},{448,4..., dimensions={0}, use_global_device_ids=true | all-gather | bytes 196608 | tf_op jit(solution)/shard_map/all_gather | solution.py:305
  3.7 0.0 collective-permute-done.across
  3.8 5.6 %collective-permute-start.2 = (f32[10,32,128]{2,1,0:T(8,128)S(1)}, f32[10,32,128]{2,1,0:T(8,128)S(1)}, u32[]{:S(2)}, u32[]{:S(2)}) collective-permute-start(f32[10,32,128]{2,1,0:T(8,128)S(1)} %get-tuple-element.26), channel_id=1, source_target_pairs={{1,0},{2,1},{3,2},{4,3},{5,4},{6,5},{7,6},{8,7},{9,8},{10,9},{11,1... | collective-permute-start | bytes 491528 | tf_op jit(solution)/shard_map/ppermute | solution.py:314
  9.4 1.9 %collective-permute-start.1 = (f32[16,128]{1,0:T(8,128)S(1)}, f32[16,128]{1,0:T(8,128)S(1)}, u32[]{:S(2)}, u32[]{:S(2)}) collective-permute-start(f32[16,128]{1,0:T(8,128)S(1)} %get-tuple-element.22.refs_7_), channel_id=1, source_target_pairs={{0,1},{1,2},{2,3},{3,4},{4,5},{5,6},{6,7},{7,8},{8,9},{9,10},{10,1... | collective-permute-start | bytes 24584 | tf_op jit(solution)/shard_map/ppermute | solution.py:315
  11.4 0.0 copy-done.4
  11.4 0.0 copy-done.3
  11.4 0.0 copy-done.2
  11.4 0.0 copy-done.1
  11.4 0.0 copy-done
  11.4 2.2 %inner.1 = (f32[4,864,128]{2,1,0:T(8,128)S(1)}, f32[16,128]{1,0:T(8,128)S(1)}, f32[5,8,128]{2,1,0:T(8,128)S(1)}, s32[64]{0:T(128)S(1)}) custom-call(f32[3]{0:T(128)S(1)} %copy-done, f32[3]{0:T(128)S(1)} %copy-done.1, f32[3]{0:T(128)S(1)} %copy-done.2, s32[4]{0:T(128)S(1)} %copy-done.3, s32[4]{0:T(128)S(1)} %copy-done.4, ...), custom_call_target="tpu_custom_call" | custom-call | flops 10000000 | bytes 1048576 | tf_op jit(solution)/shard_map/inner/pallas_call | solution.py:318
  13.6 0.0 collective-permute-done.2.high
  13.6 1.5 %render.1 = (f32[8,4,2,8,128]{4,3,2,1,0:T(8,128)S(1)}, f32[8,4,2,8,128]{4,3,2,1,0:T(8,128)S(1)}, f32[4,864,128]{2,1,0:T(8,128)S(1)}) custom-call(f32[16,128]{1,0:T(8,128)S(1)} %get-tuple-element.24.table, f32[5,8,128]{2,1,0:T(8,128)S(1)} %get-tuple-element.23.masks, s32[64]{0:T(128)S(1)} %get-tuple-element.25.starts_in, ...), custom_call_target="tpu_custom_call", output_to_operand_aliasing={{2}: (6, {})} | custom-call | flops 10000000 | bytes 1048576 | tf_op jit(solution)/shard_map/render/pallas_call | solution.py:331
  15.1 2.0 %collective-permute-done.1.low = f32[16,128]{1,0:T(8,128)S(1)} collective-permute-done((f32[16,128]{1,0:T(8,128)S(1)}, f32[16,128]{1,0:T(8,128)S(1)}, u32[]{:S(2)}, u32[]{:S(2)}) %collective-permute-start.1) | collective-permute-done | bytes 8224 | tf_op jit(solution)/shard_map/ppermute | solution.py:315
  17.1 0.7 %first.1 = (f32[8,4,2,8,128]{4,3,2,1,0:T(8,128)S(1)}, f32[8,4,2,8,128]{4,3,2,1,0:T(8,128)S(1)}, f32[4,864,128]{2,1,0:T(8,128)S(1)}) custom-call(f32[16,128]{1,0:T(8,128)S(1)} %get-tuple-element.24.table, f32[5,8,128]{2,1,0:T(8,128)S(1)} %get-tuple-element.23.masks, ...), custom_call_target="tpu_custom_call", output_to_operand_aliasing={{2}: (6, {}), {0}: (7, {}), {1}: (8, {})} | custom-call | bytes 1048576 | tf_op jit(solution)/shard_map/first/pallas_call | solution.py:341
  17.7 3.4 %all-gather.1 = f32[16,4,2,8,128]{4,3,2,1,0:T(8,128)S(1)} all-gather(f32[8,4,2,8,128]{4,3,2,1,0:T(8,128)S(1)} %get-tuple-element.32), channel_id=3, replica_groups={{0,32},{64,96},{128,160},{192,224},{256,288},{320,352},{384,416},{448,4..., dimensions={0}, use_global_device_ids=true | all-gather | bytes 786432 | tf_op jit(solution)/shard_map/all_gather | solution.py:351
  21.1 0.1 merge.1
  21.2 20.6 %all_to_all.5.slabs = f32[8,4,2,8,128]{4,3,2,1,0:T(8,128)S(1)} all-to-all(f32[8,4,2,8,128]{4,3,2,1,0:T(8,128)S(1)} %merge.1), channel_id=1, replica_groups={{0,64,128,192,256,320,384,448},{480,416,352,288,224,160,96,32},{1,65,12..., dimensions={0} | all-to-all | bytes 524288 | tf_op jit(solution)/shard_map/all_to_all | solution.py:354
  41.8 0.7 %composite.1 = f32[4,4,4,128]{3,2,1,0:T(4,128)} custom-call(f32[5,8,128]{2,1,0:T(8,128)S(1)} %get-tuple-element.23.masks, f32[8,4,2,8,128]{4,3,2,1,0:T(8,128)S(1)} %all_to_all.5.slabs), custom_call_target="tpu_custom_call" | custom-call | bytes 1048576 | tf_op jit(solution)/shard_map/composite/pallas_call | solution.py:355
  (2 shorter events, 0.1 us)
Async XLA Ops:
  0.0 11.4 %copy-start.4 = (s32[4]{0:T(128)S(1)}, s32[4]{0:T(128)}, u32[]{:S(2)}) copy-start(s32[4]{0:T(128)} %refs_4_.1) | copy-start | bytes 52
  0.0 11.4 %copy-start.3 = (s32[4]{0:T(128)S(1)}, s32[4]{0:T(128)}, u32[]{:S(2)}) copy-start(s32[4]{0:T(128)} %refs_3_.1) | copy-start | bytes 52
  0.0 11.4 %copy-start.2 = (f32[3]{0:T(128)S(1)}, f32[3]{0:T(128)}, u32[]{:S(2)}) copy-start(f32[3]{0:T(128)} %refs_2_.1) | copy-start | bytes 40
  0.0 11.4 %copy-start.1 = (f32[3]{0:T(128)S(1)}, f32[3]{0:T(128)}, u32[]{:S(2)}) copy-start(f32[3]{0:T(128)} %refs_1_.1) | copy-start | bytes 40
  0.0 1.0 %copy-start.5 = (f32[8,64,128]{2,1,0:T(8,128)S(1)}, f32[8,64,128]{2,1,0:T(8,128)}, u32[]{:S(2)}) copy-start(f32[8,64,128]{2,1,0:T(8,128)} %density.1) | copy-start | bytes 786436
  1.0 10.4 %copy-start = (f32[3]{0:T(128)S(1)}, f32[3]{0:T(128)}, u32[]{:S(2)}) copy-start(f32[3]{0:T(128)} %refs_0_.1) | copy-start | bytes 40
  1.1 2.7 %collective-permute-start = (f32[2,64,128]{2,1,0:T(8,128)S(1)}, f32[2,64,128]{2,1,0:T(8,128)S(1)}, u32[]{:S(2)}, u32[]{:S(2)}) collective-permute-start(f32[2,64,128]{2,1,0:T(8,128)S(1)} %get-tuple-element.20), channel_id=1, source_target_pairs={{64,32},{128,96},{192,160},{256,224},{320,288},{384,352},{448,416}... | collective-permute-start | bytes 196616 | tf_op jit(solution)/shard_map/ppermute | solution.py:304
  3.8 9.8 %collective-permute-start.2 = (f32[10,32,128]{2,1,0:T(8,128)S(1)}, f32[10,32,128]{2,1,0:T(8,128)S(1)}, u32[]{:S(2)}, u32[]{:S(2)}) collective-permute-start(f32[10,32,128]{2,1,0:T(8,128)S(1)} %get-tuple-element.26), channel_id=1, source_target_pairs={{1,0},{2,1},{3,2},{4,3},{5,4},{6,5},{7,6},{8,7},{9,8},{10,9},{11,1... | collective-permute-start | bytes 491528 | tf_op jit(solution)/shard_map/ppermute | solution.py:314
  9.4 7.7 %collective-permute-start.1 = (f32[16,128]{1,0:T(8,128)S(1)}, f32[16,128]{1,0:T(8,128)S(1)}, u32[]{:S(2)}, u32[]{:S(2)}) collective-permute-start(f32[16,128]{1,0:T(8,128)S(1)} %get-tuple-element.22.refs_7_), channel_id=1, source_target_pairs={{0,1},{1,2},{2,3},{3,4},{4,5},{5,6},{6,7},{7,8},{8,9},{9,10},{10,1... | collective-permute-start | bytes 24584 | tf_op jit(solution)/shard_map/ppermute | solution.py:315

commit v11 on v10

--- a/solution.py
+++ b/solution.py
@@ -15,6 +15,7 @@
 SLABS = PLANES + 1
 CHIPS = GROUPS // 2
 SHARE = ROWS // GROUPS
+ORDERS = ((7, 6, 5, 4, 3, 2, 1, 0), (7, 6, 5, 4, 3, 2, 1, 0))
 PARAMS = pltpu.CompilerParams(vmem_limit_bytes=8 * 2**20)
 LIGHT, GAIN, BIAS, PLAIN, BEYOND, NEXT, NEXT_BEYOND = 0, 3, 6, 9, 10, 11, 12
 FRONT, BACK, CORE = 0, 2, 4
@@ -74,7 +75,7 @@
         table[row : row + 1, :] = jnp.full((1, COLS), scalar, jnp.float32)
     upper = lax.broadcasted_iota(jnp.int32, (8, COLS), 0) < SHARE
     core = depth % 2
-    for base, digit in ((FRONT, core), (BACK, 1 - core)):
+    for base, digit in ((FRONT, core), (BACK, 1)):
         for pair in range(VIEWS // 2):
             first = jnp.where(reverse[2 * pair] == digit, 1.0, 0.0)
             second = jnp.where(reverse[2 * pair + 1] == digit, 1.0, 0.0)
@@ -234,14 +235,18 @@
         of(PLANES)
 
 
+def place_of(core, chip):
+    return jnp.where(core == 1, ORDERS[1].index(chip), ORDERS[0].index(chip))
+
+
 def merge_kernel(masks, kept, gathered, out):
     odd = masks[CORE] > 0.5
     core = lax.axis_index("depth") % 2
     for pair in range(VIEWS // 2):
         mine_front = masks[FRONT + pair] > 0.5
 
-        def merge(chip, _):
-            place = jnp.where(core == 1, CHIPS - 1 - chip, chip)
+        for chip in range(CHIPS):
+            place = place_of(core, chip)
             mine = [kept[chip, kind, pair] for kind in range(4)]
             other = [jnp.where(odd, gathered[0, chip, kind, pair], gathered[1, chip, kind, pair]) for kind in range(4)]
             through = jnp.exp(-jnp.where(mine_front, mine[3], other[3]))
@@ -250,15 +255,13 @@
                 behind = jnp.where(mine_front, other[kind], mine[kind])
                 out[place, kind, pair] = front + through * behind
             out[place, 3, pair] = mine[3] + other[3]
-            return 0
-
-        lax.fori_loop(0, CHIPS, merge, 0, unroll=True)
 
 
 def final_kernel(masks, slabs, out):
+    places = [place_of(lax.axis_index("depth") % 2, chip) for chip in range(CHIPS)]
     for pair in range(VIEWS // 2):
         backward = masks[BACK + pair] > 0.5
-        optical = [slabs[chip, 3, pair] for chip in range(CHIPS)]
+        optical = [slabs[place, 3, pair] for place in places]
         ahead, behind = [jnp.zeros((8, COLS), jnp.float32)], [jnp.zeros((8, COLS), jnp.float32)]
         for chip in range(CHIPS - 1):
             ahead.append(ahead[-1] + optical[chip])
@@ -267,7 +270,7 @@
         sums = [jnp.zeros((8, COLS), jnp.float32)] * 3
         for chip in range(CHIPS):
             through = jnp.exp(-jnp.where(backward, behind[CHIPS - 1 - chip], ahead[chip]))
-            sums = [sums[kind] + slabs[chip, kind, pair] * through for kind in range(3)]
+            sums = [sums[kind] + slabs[places[chip], kind, pair] * through for kind in range(3)]
         cover = jnp.where(total < 0.0625, opacity_of(total), 1.0 - jnp.exp(-total))
         for kind, value in enumerate((*sums, cover)):
             out[kind, 2 * pair] = value[:SHARE]
@@ -350,8 +353,8 @@
 
     gathered = lax.all_gather(given, "depth", axis=0, axis_index_groups=cores)
     merged = kernel(merge_kernel, "merge", part, [VMEM] * 3, VMEM)(masks, kept, gathered)
-    chips = [[2 * chip for chip in range(CHIPS)], [2 * chip + 1 for chip in reversed(range(CHIPS))]]
-    slabs = lax.all_to_all(merged, "depth", 0, 0, tiled=True, axis_index_groups=chips)
+    groups = [[2 * chip + core for chip in ORDERS[core]] for core in range(2)]
+    slabs = lax.all_to_all(merged, "depth", 0, 0, tiled=True, axis_index_groups=groups)
     return kernel(final_kernel, "composite", array(4, VIEWS, SHARE, COLS), [VMEM] * 2, VMEM)(masks, slabs)
 
 

time: 42.7 us -> 41.2 us (0.965)
  blocking collectives: 26 us -> 24.3 us
    all_to_all x1, blocking collectives: 20.6 us -> 18.9 us  [on_device(): lax.all_to_all(merged, 'depth', 0, 0, tiled=True, axis_index_groups=groups)]
where the time goes in v11:
time: 41.2 us; the launch traced here: 40.8 us
  blocking collectives  24.3 us (59%)
  starting transfers between devices  8.23 us (20%)
  Pallas kernels  5.1 us (12%)
  waiting for transfers between devices  1.99 us (5%)
  local copies, waits for them, and re-layouts  1.01 us (2%)
    all_to_all x1, blocking collectives, on_device(): lax.all_to_all(merged, 'depth', 0, 0, tiled=True, axis_index_groups=groups)  18.9 us
    ppermute x1, starting transfers between devices, on_device(): lax.ppermute(own_high, 'height', [(i + 1, i) for i in range(heights - 1)])  5.64 us
    all_gather x1, blocking collectives, on_device(): gathered = lax.all_gather(given, 'depth', axis=0, axis_index_groups=cores)  3.4 us
    pallas_call x1, Pallas kernels, on_device(): kernel(inner_kernel, 'inner', (shaded, array(16, COLS), array(5, 8, COLS)...  2.16 us
    all_gather x1, blocking collectives, on_device(): pair = lax.all_gather(first, 'depth', axis=0, axis_index_groups=cores)  2.01 us
    ppermute x1, waiting for transfers between devices, on_device(): lax.ppermute(own_low, 'height', [(i, i + 1) for i in range(heights - 1)])  1.98 us
    ppermute x1, starting transfers between devices, on_device(): lax.ppermute(own_low, 'height', [(i, i + 1) for i in range(heights - 1)])  1.92 us
    pallas_call x1, Pallas kernels, on_device(): kernel(render_kernel, 'render', (part, part, shaded), [VMEM, VMEM, ANY] +...  1.5 us
  transfers between devices with their start and end apart: 3, of which 1 were waited for; matrix products, arithmetic and copies ran while one was open for 0% of the time, Pallas kernels for 9%

profile of v11, /device:TPU:6, one launch (start us, length us, event | category | flops | bytes accessed | tf_op | source)
XLA Modules:
  0.0 40.8 jit_solution(3053554340655042151)
XLA Ops:
  0.0 0.0 copy-start.4
  0.0 0.0 copy-start.3
  0.0 0.0 copy-start.2
  0.0 0.0 copy-start.1
  0.0 0.0 copy-start.5
  0.0 1.0 %copy-done.5 = f32[8,64,128]{2,1,0:T(8,128)S(1)} copy-done((f32[8,64,128]{2,1,0:T(8,128)S(1)}, f32[8,64,128]{2,1,0:T(8,128)}, u32[]{:S(2)}) %copy-start.5) | copy-done | bytes 262168
  1.0 0.0 copy-start
  1.1 0.7 %collective-permute-start = (f32[2,64,128]{2,1,0:T(8,128)S(1)}, f32[2,64,128]{2,1,0:T(8,128)S(1)}, u32[]{:S(2)}, u32[]{:S(2)}) collective-permute-start(f32[2,64,128]{2,1,0:T(8,128)S(1)} %get-tuple-element.20), channel_id=1, source_target_pairs={{64,32},{128,96},{192,160},{256,224},{320,288},{384,352},{448,416}... | collective-permute-start | bytes 196616 | tf_op jit(solution)/shard_map/ppermute | solution.py:307
  1.7 2.0 %all-gather = f32[4,64,128]{2,1,0:T(8,128)S(1)} all-gather(f32[2,64,128]{2,1,0:T(8,128)S(1)} %get-tuple-element.20), channel_id=2, replica_groups={{0,32},{64,96},{128,160},{192,224},{256,288},{320,352},{384,416},{448,4..., dimensions={0}, use_global_device_ids=true | all-gather | bytes 196608 | tf_op jit(solution)/shard_map/all_gather | solution.py:308
  3.7 0.0 collective-permute-done.across
  3.8 5.6 %collective-permute-start.2 = (f32[10,32,128]{2,1,0:T(8,128)S(1)}, f32[10,32,128]{2,1,0:T(8,128)S(1)}, u32[]{:S(2)}, u32[]{:S(2)}) collective-permute-start(f32[10,32,128]{2,1,0:T(8,128)S(1)} %get-tuple-element.26), channel_id=1, source_target_pairs={{1,0},{2,1},{3,2},{4,3},{5,4},{6,5},{7,6},{8,7},{9,8},{10,9},{11,1... | collective-permute-start | bytes 491528 | tf_op jit(solution)/shard_map/ppermute | solution.py:317
  9.4 1.9 %collective-permute-start.1 = (f32[16,128]{1,0:T(8,128)S(1)}, f32[16,128]{1,0:T(8,128)S(1)}, u32[]{:S(2)}, u32[]{:S(2)}) collective-permute-start(f32[16,128]{1,0:T(8,128)S(1)} %get-tuple-element.22.refs_7_), channel_id=1, source_target_pairs={{0,1},{1,2},{2,3},{3,4},{4,5},{5,6},{6,7},{7,8},{8,9},{9,10},{10,1... | collective-permute-start | bytes 24584 | tf_op jit(solution)/shard_map/ppermute | solution.py:318
  11.4 0.0 copy-done.4
  11.4 0.0 copy-done.3
  11.4 0.0 copy-done.2
  11.4 0.0 copy-done.1
  11.4 0.0 copy-done
  11.4 2.2 %inner.1 = (f32[4,864,128]{2,1,0:T(8,128)S(1)}, f32[16,128]{1,0:T(8,128)S(1)}, f32[5,8,128]{2,1,0:T(8,128)S(1)}, s32[64]{0:T(128)S(1)}) custom-call(f32[3]{0:T(128)S(1)} %copy-done, f32[3]{0:T(128)S(1)} %copy-done.1, f32[3]{0:T(128)S(1)} %copy-done.2, s32[4]{0:T(128)S(1)} %copy-done.3, s32[4]{0:T(128)S(1)} %copy-done.4, ...), custom_call_target="tpu_custom_call" | custom-call | flops 10000000 | bytes 1048576 | tf_op jit(solution)/shard_map/inner/pallas_call | solution.py:321
  13.6 0.0 collective-permute-done.2.high
  13.6 1.5 %render.1 = (f32[8,4,2,8,128]{4,3,2,1,0:T(8,128)S(1)}, f32[8,4,2,8,128]{4,3,2,1,0:T(8,128)S(1)}, f32[4,864,128]{2,1,0:T(8,128)S(1)}) custom-call(f32[16,128]{1,0:T(8,128)S(1)} %get-tuple-element.24.table, f32[5,8,128]{2,1,0:T(8,128)S(1)} %get-tuple-element.23.masks, s32[64]{0:T(128)S(1)} %get-tuple-element.25.starts_in, ...), custom_call_target="tpu_custom_call", output_to_operand_aliasing={{2}: (6, {})} | custom-call | flops 10000000 | bytes 1048576 | tf_op jit(solution)/shard_map/render/pallas_call | solution.py:334
  15.1 2.0 %collective-permute-done.1.low = f32[16,128]{1,0:T(8,128)S(1)} collective-permute-done((f32[16,128]{1,0:T(8,128)S(1)}, f32[16,128]{1,0:T(8,128)S(1)}, u32[]{:S(2)}, u32[]{:S(2)}) %collective-permute-start.1) | collective-permute-done | bytes 8224 | tf_op jit(solution)/shard_map/ppermute | solution.py:318
  17.1 0.7 %first.1 = (f32[8,4,2,8,128]{4,3,2,1,0:T(8,128)S(1)}, f32[8,4,2,8,128]{4,3,2,1,0:T(8,128)S(1)}, f32[4,864,128]{2,1,0:T(8,128)S(1)}) custom-call(f32[16,128]{1,0:T(8,128)S(1)} %get-tuple-element.24.table, f32[5,8,128]{2,1,0:T(8,128)S(1)} %get-tuple-element.23.masks, ...), custom_call_target="tpu_custom_call", output_to_operand_aliasing={{2}: (6, {}), {0}: (7, {}), {1}: (8, {})} | custom-call | bytes 1048576 | tf_op jit(solution)/shard_map/first/pallas_call | solution.py:344
  17.7 3.4 %all-gather.1 = f32[16,4,2,8,128]{4,3,2,1,0:T(8,128)S(1)} all-gather(f32[8,4,2,8,128]{4,3,2,1,0:T(8,128)S(1)} %get-tuple-element.32), channel_id=3, replica_groups={{0,32},{64,96},{128,160},{192,224},{256,288},{320,352},{384,416},{448,4..., dimensions={0}, use_global_device_ids=true | all-gather | bytes 786432 | tf_op jit(solution)/shard_map/all_gather | solution.py:354
  21.1 0.1 merge.1
  21.2 18.9 %all_to_all.5.slabs = f32[8,4,2,8,128]{4,3,2,1,0:T(8,128)S(1)} all-to-all(f32[8,4,2,8,128]{4,3,2,1,0:T(8,128)S(1)} %merge.1), channel_id=1, replica_groups={{448,384,320,256,192,128,64,0},{480,416,352,288,224,160,96,32},{449,385..., dimensions={0} | all-to-all | bytes 524288 | tf_op jit(solution)/shard_map/all_to_all | solution.py:357
  40.1 0.7 %composite.1 = f32[4,4,4,128]{3,2,1,0:T(4,128)} custom-call(f32[5,8,128]{2,1,0:T(8,128)S(1)} %get-tuple-element.23.masks, f32[8,4,2,8,128]{4,3,2,1,0:T(8,128)S(1)} %all_to_all.5.slabs), custom_call_target="tpu_custom_call" | custom-call | bytes 1048576 | tf_op jit(solution)/shard_map/composite/pallas_call | solution.py:358
  (2 shorter events, 0.1 us)
Async XLA Ops:
  0.0 11.4 %copy-start.4 = (s32[4]{0:T(128)S(1)}, s32[4]{0:T(128)}, u32[]{:S(2)}) copy-start(s32[4]{0:T(128)} %refs_4_.1) | copy-start | bytes 52
  0.0 11.4 %copy-start.3 = (s32[4]{0:T(128)S(1)}, s32[4]{0:T(128)}, u32[]{:S(2)}) copy-start(s32[4]{0:T(128)} %refs_3_.1) | copy-start | bytes 52
  0.0 11.4 %copy-start.2 = (f32[3]{0:T(128)S(1)}, f32[3]{0:T(128)}, u32[]{:S(2)}) copy-start(f32[3]{0:T(128)} %refs_2_.1) | copy-start | bytes 40
  0.0 11.4 %copy-start.1 = (f32[3]{0:T(128)S(1)}, f32[3]{0:T(128)}, u32[]{:S(2)}) copy-start(f32[3]{0:T(128)} %refs_1_.1) | copy-start | bytes 40
  0.0 1.0 %copy-start.5 = (f32[8,64,128]{2,1,0:T(8,128)S(1)}, f32[8,64,128]{2,1,0:T(8,128)}, u32[]{:S(2)}) copy-start(f32[8,64,128]{2,1,0:T(8,128)} %density.1) | copy-start | bytes 786436
  1.0 10.4 %copy-start = (f32[3]{0:T(128)S(1)}, f32[3]{0:T(128)}, u32[]{:S(2)}) copy-start(f32[3]{0:T(128)} %refs_0_.1) | copy-start | bytes 40
  1.1 2.7 %collective-permute-start = (f32[2,64,128]{2,1,0:T(8,128)S(1)}, f32[2,64,128]{2,1,0:T(8,128)S(1)}, u32[]{:S(2)}, u32[]{:S(2)}) collective-permute-start(f32[2,64,128]{2,1,0:T(8,128)S(1)} %get-tuple-element.20), channel_id=1, source_target_pairs={{64,32},{128,96},{192,160},{256,224},{320,288},{384,352},{448,416}... | collective-permute-start | bytes 196616 | tf_op jit(solution)/shard_map/ppermute | solution.py:307
  3.8 9.8 %collective-permute-start.2 = (f32[10,32,128]{2,1,0:T(8,128)S(1)}, f32[10,32,128]{2,1,0:T(8,128)S(1)}, u32[]{:S(2)}, u32[]{:S(2)}) collective-permute-start(f32[10,32,128]{2,1,0:T(8,128)S(1)} %get-tuple-element.26), channel_id=1, source_target_pairs={{1,0},{2,1},{3,2},{4,3},{5,4},{6,5},{7,6},{8,7},{9,8},{10,9},{11,1... | collective-permute-start | bytes 491528 | tf_op jit(solution)/shard_map/ppermute | solution.py:317
  9.4 7.7 %collective-permute-start.1 = (f32[16,128]{1,0:T(8,128)S(1)}, f32[16,128]{1,0:T(8,128)S(1)}, u32[]{:S(2)}, u32[]{:S(2)}) collective-permute-start(f32[16,128]{1,0:T(8,128)S(1)} %get-tuple-element.22.refs_7_), channel_id=1, source_target_pairs={{0,1},{1,2},{2,3},{3,4},{4,5},{5,6},{6,7},{7,8},{8,9},{9,10},{10,1... | collective-permute-start | bytes 24584 | tf_op jit(solution)/shard_map/ppermute | solution.py:318

commit v12 on v11

--- a/solution.py
+++ b/solution.py
@@ -117,9 +117,7 @@
         fields[kind, rows, :] = values[kind]
 
 
-def cut_kernel(own, pair, across, coming, high, low):
-    odd = lax.axis_index("depth") % 2 == 1
-    coming[...] = jnp.where(odd, across[...], pair[1])
+def cut_kernel(own, coming, high, low):
     high[:PLANES] = own[:, :SHEAR, :]
     high[PLANES:] = coming[:, :SHEAR, :]
     for plane in range(PLANES):
@@ -304,16 +302,10 @@
         scratch_shapes=[pltpu.SemaphoreType.DMA],
     )(density)
     cores = [[2 * chip, 2 * chip + 1] for chip in range(CHIPS)]
-    across = lax.ppermute(first, "depth", [(i + 1, i) for i in range(1, depths - 1, 2)])
-    pair = lax.all_gather(first, "depth", axis=0, axis_index_groups=cores)
-
-    coming, own_high, own_low = kernel(
-        cut_kernel,
-        "cut",
-        (array(2, ROWS, COLS), array(PLANES + 2, SHEAR, COLS), array(PLANES + 8, COLS)),
-        [VMEM] * 3,
-        (VMEM,) * 3,
-    )(own, pair, across)
+    coming = lax.ppermute(first, "depth", [(i + 1, i) for i in range(depths - 1)])
+    own_high, own_low = kernel(
+        cut_kernel, "cut", (array(PLANES + 2, SHEAR, COLS), array(PLANES + 8, COLS)), [VMEM] * 2, (VMEM,) * 2
+    )(own, coming)
     high = lax.ppermute(own_high, "height", [(i + 1, i) for i in range(heights - 1)])
     low = lax.ppermute(own_low, "height", [(i, i + 1) for i in range(heights - 1)])
 

time: 41.2 us -> 41.3 us (level)
  blocking collectives: 24.3 us -> 22 us
  waiting for transfers between devices: 1.99 us -> 3.83 us
  starting transfers between devices: 8.23 us -> 8.86 us
    all_gather x1 -> x0, blocking collectives: 2.01 us -> none  [on_device(): pair = lax.all_gather(first, 'depth', axis=0, axis_index_groups=cores)]
    ppermute x1, waiting for transfers between devices: 0.01 us -> 1.85 us  [on_device(): lax.ppermute(first, 'depth', [(i + 1, i) for i in range(depths - 1)])]
    ppermute x1, starting transfers between devices: 0.66 us -> 1.29 us  [on_device(): lax.ppermute(first, 'depth', [(i + 1, i) for i in range(depths - 1)])]
    all_to_all x1, blocking collectives: 18.9 us -> 18.5 us  [on_device(): lax.all_to_all(merged, 'depth', 0, 0, tiled=True, axis_index_groups=groups)]
  transfers between devices with their start and end apart: 3 -> 3, of which waited for: 1 -> 2; matrix products, arithmetic and copies ran while one was open for 0% -> 0% of each run, Pallas kernels for 9% -> 9%
where the time goes in v12:
time: 41.3 us; the launch traced here: 40.9 us
  blocking collectives  22 us (53%)
  starting transfers between devices  8.86 us (21%)
  Pallas kernels  5.09 us (12%)
  waiting for transfers between devices  3.83 us (9%)
  local copies, waits for them, and re-layouts  1.01 us (2%)
    all_to_all x1, blocking collectives, on_device(): lax.all_to_all(merged, 'depth', 0, 0, tiled=True, axis_index_groups=groups)  18.5 us
    ppermute x1, starting transfers between devices, on_device(): lax.ppermute(own_high, 'height', [(i + 1, i) for i in range(heights - 1)])  5.64 us
    all_gather x1, blocking collectives, on_device(): gathered = lax.all_gather(given, 'depth', axis=0, axis_index_groups=cores)  3.56 us
    pallas_call x1, Pallas kernels, on_device(): kernel(inner_kernel, 'inner', (shaded, array(16, COLS), array(5, 8, COLS)...  2.16 us
    ppermute x1, waiting for transfers between devices, on_device(): lax.ppermute(own_low, 'height', [(i, i + 1) for i in range(heights - 1)])  1.98 us
    ppermute x1, starting transfers between devices, on_device(): lax.ppermute(own_low, 'height', [(i, i + 1) for i in range(heights - 1)])  1.92 us
    ppermute x1, waiting for transfers between devices, on_device(): lax.ppermute(first, 'depth', [(i + 1, i) for i in range(depths - 1)])  1.85 us
    pallas_call x1, Pallas kernels, on_device(): kernel(render_kernel, 'render', (part, part, shaded), [VMEM, VMEM, ANY] +...  1.5 us
  transfers between devices with their start and end apart: 3, of which 2 were waited for; matrix products, arithmetic and copies ran while one was open for 0% of the time, Pallas kernels for 9%

profile of v12, /device:TPU:6, one launch (start us, length us, event | category | flops | bytes accessed | tf_op | source)
XLA Modules:
  0.0 40.9 jit_solution(3658628478663847509)
XLA Ops:
  0.0 0.0 copy-start.4
  0.0 0.0 copy-start.3
  0.0 0.0 copy-start.2
  0.0 0.0 copy-start.1
  0.0 0.0 copy-start.5
  0.0 1.0 %copy-done.5 = f32[8,64,128]{2,1,0:T(8,128)S(1)} copy-done((f32[8,64,128]{2,1,0:T(8,128)S(1)}, f32[8,64,128]{2,1,0:T(8,128)}, u32[]{:S(2)}) %copy-start.5) | copy-done | bytes 262168
  1.0 0.0 copy-start
  1.1 1.3 %collective-permute-start = (f32[2,64,128]{2,1,0:T(8,128)S(1)}, f32[2,64,128]{2,1,0:T(8,128)S(1)}, u32[]{:S(2)}, u32[]{:S(2)}) collective-permute-start(f32[2,64,128]{2,1,0:T(8,128)S(1)} %get-tuple-element.19), channel_id=1, source_target_pairs={{32,0},{64,32},{96,64},{128,96},{160,128},{192,160},{224,192},{256... | collective-permute-start | bytes 196616 | tf_op jit(solution)/shard_map/ppermute | solution.py:305
  2.4 1.8 %collective-permute-done.coming.refs_6_ = f32[2,64,128]{2,1,0:T(8,128)S(1)} collective-permute-done((f32[2,64,128]{2,1,0:T(8,128)S(1)}, f32[2,64,128]{2,1,0:T(8,128)S(1)}, u32[]{:S(2)}, u32[]{:S(2)}) %collective-permute-start) | collective-permute-done | bytes 65568 | tf_op jit(solution)/shard_map/ppermute | solution.py:305
  4.2 5.6 %collective-permute-start.2 = (f32[10,32,128]{2,1,0:T(8,128)S(1)}, f32[10,32,128]{2,1,0:T(8,128)S(1)}, u32[]{:S(2)}, u32[]{:S(2)}) collective-permute-start(f32[10,32,128]{2,1,0:T(8,128)S(1)} %get-tuple-element.24), channel_id=1, source_target_pairs={{1,0},{2,1},{3,2},{4,3},{5,4},{6,5},{7,6},{8,7},{9,8},{10,9},{11,1... | collective-permute-start | bytes 491528 | tf_op jit(solution)/shard_map/ppermute | solution.py:309
  9.9 1.9 %collective-permute-start.1 = (f32[16,128]{1,0:T(8,128)S(1)}, f32[16,128]{1,0:T(8,128)S(1)}, u32[]{:S(2)}, u32[]{:S(2)}) collective-permute-start(f32[16,128]{1,0:T(8,128)S(1)} %get-tuple-element.20.refs_7_), channel_id=1, source_target_pairs={{0,1},{1,2},{2,3},{3,4},{4,5},{5,6},{6,7},{7,8},{8,9},{9,10},{10,1... | collective-permute-start | bytes 24584 | tf_op jit(solution)/shard_map/ppermute | solution.py:310
  11.8 0.0 copy-done.4
  11.8 0.0 copy-done.3
  11.8 0.0 copy-done.2
  11.8 0.0 copy-done.1
  11.8 0.0 copy-done
  11.9 2.2 %inner.1 = (f32[4,864,128]{2,1,0:T(8,128)S(1)}, f32[16,128]{1,0:T(8,128)S(1)}, f32[5,8,128]{2,1,0:T(8,128)S(1)}, s32[64]{0:T(128)S(1)}) custom-call(f32[3]{0:T(128)S(1)} %copy-done, f32[3]{0:T(128)S(1)} %copy-done.1, f32[3]{0:T(128)S(1)} %copy-done.2, s32[4]{0:T(128)S(1)} %copy-done.3, s32[4]{0:T(128)S(1)} %copy-done.4, ...), custom_call_target="tpu_custom_call" | custom-call | flops 10000000 | bytes 1048576 | tf_op jit(solution)/shard_map/inner/pallas_call | solution.py:313
  14.0 0.0 collective-permute-done.2.high
  14.0 1.5 %render.1 = (f32[8,4,2,8,128]{4,3,2,1,0:T(8,128)S(1)}, f32[8,4,2,8,128]{4,3,2,1,0:T(8,128)S(1)}, f32[4,864,128]{2,1,0:T(8,128)S(1)}) custom-call(f32[16,128]{1,0:T(8,128)S(1)} %get-tuple-element.22.table, f32[5,8,128]{2,1,0:T(8,128)S(1)} %get-tuple-element.21.masks, s32[64]{0:T(128)S(1)} %get-tuple-element.23.starts_in, ...), custom_call_target="tpu_custom_call", output_to_operand_aliasing={{2}: (6, {})} | custom-call | flops 10000000 | bytes 1048576 | tf_op jit(solution)/shard_map/render/pallas_call | solution.py:326
  15.5 2.0 %collective-permute-done.1.low = f32[16,128]{1,0:T(8,128)S(1)} collective-permute-done((f32[16,128]{1,0:T(8,128)S(1)}, f32[16,128]{1,0:T(8,128)S(1)}, u32[]{:S(2)}, u32[]{:S(2)}) %collective-permute-start.1) | collective-permute-done | bytes 8224 | tf_op jit(solution)/shard_map/ppermute | solution.py:310
  17.5 0.7 %first.1 = (f32[8,4,2,8,128]{4,3,2,1,0:T(8,128)S(1)}, f32[8,4,2,8,128]{4,3,2,1,0:T(8,128)S(1)}, f32[4,864,128]{2,1,0:T(8,128)S(1)}) custom-call(f32[16,128]{1,0:T(8,128)S(1)} %get-tuple-element.22.table, f32[5,8,128]{2,1,0:T(8,128)S(1)} %get-tuple-element.21.masks, ...), custom_call_target="tpu_custom_call", output_to_operand_aliasing={{2}: (6, {}), {0}: (7, {}), {1}: (8, {})} | custom-call | bytes 1048576 | tf_op jit(solution)/shard_map/first/pallas_call | solution.py:336
  18.2 3.6 %all-gather = f32[16,4,2,8,128]{4,3,2,1,0:T(8,128)S(1)} all-gather(f32[8,4,2,8,128]{4,3,2,1,0:T(8,128)S(1)} %get-tuple-element.30), channel_id=2, replica_groups={{0,32},{64,96},{128,160},{192,224},{256,288},{320,352},{384,416},{448,4..., dimensions={0}, use_global_device_ids=true | all-gather | bytes 786432 | tf_op jit(solution)/shard_map/all_gather | solution.py:346
  21.8 0.1 merge.1
  21.8 18.5 %all_to_all.5.slabs = f32[8,4,2,8,128]{4,3,2,1,0:T(8,128)S(1)} all-to-all(f32[8,4,2,8,128]{4,3,2,1,0:T(8,128)S(1)} %merge.1), channel_id=1, replica_groups={{448,384,320,256,192,128,64,0},{480,416,352,288,224,160,96,32},{449,385..., dimensions={0} | all-to-all | bytes 524288 | tf_op jit(solution)/shard_map/all_to_all | solution.py:349
  40.3 0.7 %composite.1 = f32[4,4,4,128]{3,2,1,0:T(4,128)} custom-call(f32[5,8,128]{2,1,0:T(8,128)S(1)} %get-tuple-element.21.masks, f32[8,4,2,8,128]{4,3,2,1,0:T(8,128)S(1)} %all_to_all.5.slabs), custom_call_target="tpu_custom_call" | custom-call | bytes 1048576 | tf_op jit(solution)/shard_map/composite/pallas_call | solution.py:350
  (2 shorter events, 0.0 us)
Async XLA Ops:
  0.0 11.8 %copy-start.4 = (s32[4]{0:T(128)S(1)}, s32[4]{0:T(128)}, u32[]{:S(2)}) copy-start(s32[4]{0:T(128)} %refs_4_.1) | copy-start | bytes 52
  0.0 11.8 %copy-start.3 = (s32[4]{0:T(128)S(1)}, s32[4]{0:T(128)}, u32[]{:S(2)}) copy-start(s32[4]{0:T(128)} %refs_3_.1) | copy-start | bytes 52
  0.0 11.8 %copy-start.2 = (f32[3]{0:T(128)S(1)}, f32[3]{0:T(128)}, u32[]{:S(2)}) copy-start(f32[3]{0:T(128)} %refs_2_.1) | copy-start | bytes 40
  0.0 11.8 %copy-start.1 = (f32[3]{0:T(128)S(1)}, f32[3]{0:T(128)}, u32[]{:S(2)}) copy-start(f32[3]{0:T(128)} %refs_1_.1) | copy-start | bytes 40
  0.0 1.0 %copy-start.5 = (f32[8,64,128]{2,1,0:T(8,128)S(1)}, f32[8,64,128]{2,1,0:T(8,128)}, u32[]{:S(2)}) copy-start(f32[8,64,128]{2,1,0:T(8,128)} %density.1) | copy-start | bytes 786436
  1.0 10.8 %copy-start = (f32[3]{0:T(128)S(1)}, f32[3]{0:T(128)}, u32[]{:S(2)}) copy-start(f32[3]{0:T(128)} %refs_0_.1) | copy-start | bytes 40
  1.1 3.1 %collective-permute-start = (f32[2,64,128]{2,1,0:T(8,128)S(1)}, f32[2,64,128]{2,1,0:T(8,128)S(1)}, u32[]{:S(2)}, u32[]{:S(2)}) collective-permute-start(f32[2,64,128]{2,1,0:T(8,128)S(1)} %get-tuple-element.19), channel_id=1, source_target_pairs={{32,0},{64,32},{96,64},{128,96},{160,128},{192,160},{224,192},{256... | collective-permute-start | bytes 196616 | tf_op jit(solution)/shard_map/ppermute | solution.py:305
  4.2 9.8 %collective-permute-start.2 = (f32[10,32,128]{2,1,0:T(8,128)S(1)}, f32[10,32,128]{2,1,0:T(8,128)S(1)}, u32[]{:S(2)}, u32[]{:S(2)}) collective-permute-start(f32[10,32,128]{2,1,0:T(8,128)S(1)} %get-tuple-element.24), channel_id=1, source_target_pairs={{1,0},{2,1},{3,2},{4,3},{5,4},{6,5},{7,6},{8,7},{9,8},{10,9},{11,1... | collective-permute-start | bytes 491528 | tf_op jit(solution)/shard_map/ppermute | solution.py:309
  9.9 7.7 %collective-permute-start.1 = (f32[16,128]{1,0:T(8,128)S(1)}, f32[16,128]{1,0:T(8,128)S(1)}, u32[]{:S(2)}, u32[]{:S(2)}) collective-permute-start(f32[16,128]{1,0:T(8,128)S(1)} %get-tuple-element.20.refs_7_), channel_id=1, source_target_pairs={{0,1},{1,2},{2,3},{3,4},{4,5},{5,6},{6,7},{7,8},{8,9},{9,10},{10,1... | collective-permute-start | bytes 24584 | tf_op jit(solution)/shard_map/ppermute | solution.py:310

commit v13 on v12

--- a/solution.py
+++ b/solution.py
@@ -58,7 +58,7 @@
 
 
 def inner_kernel(*refs):
-    arguments, (own, coming, _, fields, table, masks, starts), scalars, semaphores = refs[:5], refs[5:12], refs[12:17], refs[17]
+    arguments, (own, coming, _, fields, table, masks, starts, heads), scalars, semaphores = refs[:5], refs[5:13], refs[13:18], refs[18]
     copies = [pltpu.make_async_copy(arguments[i], scalars[i], semaphores.at[i]) for i in range(5)]
     for copy in copies:
         copy.start()
@@ -100,8 +100,16 @@
     shade_inner(coefficient, extinction, last, own[PLANES - 2, INNER, :], coming[0, INNER, :], fields, PLANES - 1)
     shade_inner(coefficient, following, coming.at[0], last[INNER, :], coming[1, INNER, :], fields, PLANES)
 
+    plane_at = lambda plane: own.at[plane] if plane < PLANES else coming.at[plane - PLANES]
+    for plane in range(PLANES + 2):
+        for row in range(2):
+            heads[row, plane : plane + 1, :] = plane_at(plane)[row : row + 1, :]
+    for slot in range(1, SLABS):
+        first_tile(coefficient, following if slot == PLANES else extinction, plane_at, fields, slot)
+
     @pl.when(depth == 0)
     def _():
+        first_tile(coefficient, extinction, plane_at, fields, 0)
         shade_inner(coefficient, extinction, own.at[0], 0.0, own[1, INNER, :], fields, 0)
 
 
@@ -109,6 +117,14 @@
     centre = plane[INNER, :]
     values = shade(coefficient, extinction, centre, plane[7 : ROWS - 9, :], plane[9 : ROWS - 7, :], before, after)
     store(fields, slot, 8, values)
+
+
+def first_tile(coefficient, extinction, plane_at, fields, slot):
+    plane = plane_at(slot)
+    centre = plane[:8, :]
+    before = 0.0 if slot == 0 else plane_at(slot - 1)[:8, :]
+    after = plane_at(slot + 1)[:8, :]
+    store(fields, slot, 0, shade(coefficient, extinction, centre, pltpu.roll(centre, 1, 0), plane[1:9, :], before, after))
 
 
 def store(fields, slot, row, values):
@@ -166,29 +182,25 @@
     render(masks, starts, fields, given, kept, 1, ROWS // 8)
 
 
-def first_kernel(table, masks, starts_in, own, coming, low, held, *refs):
+def first_kernel(table, masks, starts_in, heads, low, held, *refs):
     del held
     given, kept, fields, starts, semaphore = refs[2:]
     copy = pltpu.make_async_copy(starts_in, starts, semaphore)
     copy.start()
     coefficient = lambda at: table[at : at + 1, :]
-    top = lax.broadcasted_iota(jnp.int32, (8, COLS), 0) == 0
-
-    def first_rows(slot):
-        plane_at = lambda plane: own.at[plane] if plane < PLANES else coming.at[plane - PLANES]
-        plane = plane_at(slot)
-        centre = plane[:8, :]
-        above = jnp.where(top, low[slot : slot + 1, :], pltpu.roll(centre, 1, 0))
-        before = 0.0 if slot == 0 else plane_at(slot - 1)[:8, :]
-        extinction = coefficient(NEXT if slot == PLANES else PLAIN)
-        store(fields, slot, 0, shade(coefficient, extinction, centre, above, plane[1:9, :], before, plane_at(slot + 1)[:8, :]))
-
+    last = lax.broadcasted_iota(jnp.int32, (8, COLS), 0) == PLANES - 1
+    extinction = jnp.where(last, coefficient(NEXT), coefficient(PLAIN))
+    centre, before, after = heads[0, 1:9, :], heads[0, 0:8, :], heads[0, 2:10, :]
+    values = shade(coefficient, extinction, centre, low[1:9, :], heads[1, 1:9, :], before, after)
     for slot in range(1, SLABS):
-        first_rows(slot)
+        for kind in range(4):
+            fields[kind, slot * TALL : slot * TALL + 1, :] = values[kind][slot - 1 : slot, :]
 
     @pl.when(lax.axis_index("depth") == 0)
     def _():
-        first_rows(0)
+        first = shade(coefficient, coefficient(PLAIN), heads[0, 0:8, :], low[0:8, :], heads[1, 0:8, :], 0.0, centre)
+        for kind in range(4):
+            fields[kind, 0:1, :] = first[kind][0:1, :]
 
     copy.wait()
     render(masks, starts, fields, given, kept, 0, 1)
@@ -310,12 +322,12 @@
     low = lax.ppermute(own_low, "height", [(i, i + 1) for i in range(heights - 1)])
 
     shaded = array(4, SLABS * TALL, COLS)
-    fields, table, masks, starts = kernel(
+    fields, table, masks, starts, heads = kernel(
         inner_kernel,
         "inner",
-        (shaded, array(16, COLS), array(5, 8, COLS), jax.ShapeDtypeStruct((64,), jnp.int32)),
+        (shaded, array(16, COLS), array(5, 8, COLS), jax.ShapeDtypeStruct((64,), jnp.int32), array(2, 16, COLS)),
         [HBM] * 5 + [VMEM] * 3,
-        (VMEM, VMEM, VMEM, SMEM),
+        (VMEM, VMEM, VMEM, SMEM, VMEM),
         flops=10**7,
         scratch_shapes=[pltpu.SMEM((3,), jnp.float32)] * 3
         + [pltpu.SMEM((VIEWS,), jnp.int32)] * 2
@@ -337,11 +349,11 @@
         first_kernel,
         "first",
         (part, part, shaded),
-        [VMEM, VMEM, ANY] + [VMEM] * 6,
+        [VMEM, VMEM, ANY] + [VMEM] * 5,
         (VMEM,) * 3,
-        input_output_aliases={6: 2, 7: 0, 8: 1},
+        input_output_aliases={5: 2, 6: 0, 7: 1},
         scratch_shapes=memory,
-    )(table, masks, starts, own, coming, low, fields, given, kept)
+    )(table, masks, starts, heads, low, fields, given, kept)
 
     gathered = lax.all_gather(given, "depth", axis=0, axis_index_groups=cores)
     merged = kernel(merge_kernel, "merge", part, [VMEM] * 3, VMEM)(masks, kept, gathered)

time: 41.3 us -> 41.3 us (level)
  no operation moved by 1% of the time
where the time goes in v13:
time: 41.3 us; the launch traced here: 40.9 us
  blocking collectives  22 us (53%)
  starting transfers between devices  8.86 us (21%)
  Pallas kernels  5.17 us (13%)
  waiting for transfers between devices  3.75 us (9%)
  local copies, waits for them, and re-layouts  1.01 us (2%)
    all_to_all x1, blocking collectives, on_device(): lax.all_to_all(merged, 'depth', 0, 0, tiled=True, axis_index_groups=groups)  18.5 us
    ppermute x1, starting transfers between devices, on_device(): lax.ppermute(own_high, 'height', [(i + 1, i) for i in range(heights - 1)])  5.64 us
    all_gather x1, blocking collectives, on_device(): gathered = lax.all_gather(given, 'depth', axis=0, axis_index_groups=cores)  3.56 us
    pallas_call x1, Pallas kernels, on_device(): kernel(inner_kernel, 'inner', (shaded, array(16, COLS), array(5, 8, COLS)...  2.25 us
    ppermute x1, starting transfers between devices, on_device(): lax.ppermute(own_low, 'height', [(i, i + 1) for i in range(heights - 1)])  1.92 us
    ppermute x1, waiting for transfers between devices, on_device(): lax.ppermute(own_low, 'height', [(i, i + 1) for i in range(heights - 1)])  1.9 us
    ppermute x1, waiting for transfers between devices, on_device(): lax.ppermute(first, 'depth', [(i + 1, i) for i in range(depths - 1)])  1.85 us
    pallas_call x1, Pallas kernels, on_device(): kernel(render_kernel, 'render', (part, part, shaded), [VMEM, VMEM, ANY] +...  1.5 us
  transfers between devices with their start and end apart: 3, of which 2 were waited for; matrix products, arithmetic and copies ran while one was open for 0% of the time, Pallas kernels for 9%

profile of v13, /device:TPU:6, one launch (start us, length us, event | category | flops | bytes accessed | tf_op | source)
XLA Modules:
  0.0 40.9 jit_solution(2435208535428652056)
XLA Ops:
  0.0 0.0 copy-start.4
  0.0 0.0 copy-start.3
  0.0 0.0 copy-start.2
  0.0 0.0 copy-start.1
  0.0 0.0 copy-start.5
  0.0 1.0 %copy-done.5 = f32[8,64,128]{2,1,0:T(8,128)S(1)} copy-done((f32[8,64,128]{2,1,0:T(8,128)S(1)}, f32[8,64,128]{2,1,0:T(8,128)}, u32[]{:S(2)}) %copy-start.5) | copy-done | bytes 262168
  1.0 0.0 copy-start
  1.1 1.3 %collective-permute-start = (f32[2,64,128]{2,1,0:T(8,128)S(1)}, f32[2,64,128]{2,1,0:T(8,128)S(1)}, u32[]{:S(2)}, u32[]{:S(2)}) collective-permute-start(f32[2,64,128]{2,1,0:T(8,128)S(1)} %get-tuple-element.20), channel_id=1, source_target_pairs={{32,0},{64,32},{96,64},{128,96},{160,128},{192,160},{224,192},{256... | collective-permute-start | bytes 196616 | tf_op jit(solution)/shard_map/ppermute | solution.py:317
  2.4 1.8 %collective-permute-done.coming.refs_6_ = f32[2,64,128]{2,1,0:T(8,128)S(1)} collective-permute-done((f32[2,64,128]{2,1,0:T(8,128)S(1)}, f32[2,64,128]{2,1,0:T(8,128)S(1)}, u32[]{:S(2)}, u32[]{:S(2)}) %collective-permute-start) | collective-permute-done | bytes 65568 | tf_op jit(solution)/shard_map/ppermute | solution.py:317
  4.2 5.6 %collective-permute-start.2 = (f32[10,32,128]{2,1,0:T(8,128)S(1)}, f32[10,32,128]{2,1,0:T(8,128)S(1)}, u32[]{:S(2)}, u32[]{:S(2)}) collective-permute-start(f32[10,32,128]{2,1,0:T(8,128)S(1)} %get-tuple-element.26), channel_id=1, source_target_pairs={{1,0},{2,1},{3,2},{4,3},{5,4},{6,5},{7,6},{8,7},{9,8},{10,9},{11,1... | collective-permute-start | bytes 491528 | tf_op jit(solution)/shard_map/ppermute | solution.py:321
  9.9 1.9 %collective-permute-start.1 = (f32[16,128]{1,0:T(8,128)S(1)}, f32[16,128]{1,0:T(8,128)S(1)}, u32[]{:S(2)}, u32[]{:S(2)}) collective-permute-start(f32[16,128]{1,0:T(8,128)S(1)} %get-tuple-element.21.refs_7_), channel_id=1, source_target_pairs={{0,1},{1,2},{2,3},{3,4},{4,5},{5,6},{6,7},{7,8},{8,9},{9,10},{10,1... | collective-permute-start | bytes 24584 | tf_op jit(solution)/shard_map/ppermute | solution.py:322
  11.8 0.0 copy-done.4
  11.8 0.0 copy-done.3
  11.8 0.0 copy-done.2
  11.8 0.0 copy-done.1
  11.8 0.0 copy-done
  11.9 2.2 %inner.1 = (f32[4,864,128]{2,1,0:T(8,128)S(1)}, f32[16,128]{1,0:T(8,128)S(1)}, f32[5,8,128]{2,1,0:T(8,128)S(1)}, s32[64]{0:T(128)S(1)}, f32[2,16,128]{2,1,0:T(8,128)S(1)}) custom-call(f32[3]{0:T(128)S(1)} %copy-done, f32[3]{0:T(128)S(1)} %copy-done.1, f32[3]{0:T(128)S(1)} %copy-done.2, s32[4]{0:T(128)S(1)} %copy-done.3, s32[4]{0:T(128)S(1)} %copy-done.4, ...), custom_call_target="tpu_custom_call" | custom-call | flops 10000000 | bytes 1048576 | tf_op jit(solution)/shard_map/inner/pallas_call | solution.py:325
  14.1 0.0 collective-permute-done.2.high
  14.1 1.5 %render.1 = (f32[8,4,2,8,128]{4,3,2,1,0:T(8,128)S(1)}, f32[8,4,2,8,128]{4,3,2,1,0:T(8,128)S(1)}, f32[4,864,128]{2,1,0:T(8,128)S(1)}) custom-call(f32[16,128]{1,0:T(8,128)S(1)} %get-tuple-element.23.table, f32[5,8,128]{2,1,0:T(8,128)S(1)} %get-tuple-element.22.masks, s32[64]{0:T(128)S(1)} %get-tuple-element.24.starts_in, ...), custom_call_target="tpu_custom_call", output_to_operand_aliasing={{2}: (6, {})} | custom-call | flops 10000000 | bytes 1048576 | tf_op jit(solution)/shard_map/render/pallas_call | solution.py:338
  15.6 1.9 %collective-permute-done.1.low = f32[16,128]{1,0:T(8,128)S(1)} collective-permute-done((f32[16,128]{1,0:T(8,128)S(1)}, f32[16,128]{1,0:T(8,128)S(1)}, u32[]{:S(2)}, u32[]{:S(2)}) %collective-permute-start.1) | collective-permute-done | bytes 8224 | tf_op jit(solution)/shard_map/ppermute | solution.py:322
  17.5 0.6 %first.1 = (f32[8,4,2,8,128]{4,3,2,1,0:T(8,128)S(1)}, f32[8,4,2,8,128]{4,3,2,1,0:T(8,128)S(1)}, f32[4,864,128]{2,1,0:T(8,128)S(1)}) custom-call(f32[16,128]{1,0:T(8,128)S(1)} %get-tuple-element.23.table, f32[5,8,128]{2,1,0:T(8,128)S(1)} %get-tuple-element.22.masks, ...), custom_call_target="tpu_custom_call", output_to_operand_aliasing={{2}: (5, {}), {0}: (6, {}), {1}: (7, {})} | custom-call | bytes 1048576 | tf_op jit(solution)/shard_map/first/pallas_call | solution.py:348
  18.2 3.6 %all-gather = f32[16,4,2,8,128]{4,3,2,1,0:T(8,128)S(1)} all-gather(f32[8,4,2,8,128]{4,3,2,1,0:T(8,128)S(1)} %get-tuple-element.32), channel_id=2, replica_groups={{0,32},{64,96},{128,160},{192,224},{256,288},{320,352},{384,416},{448,4..., dimensions={0}, use_global_device_ids=true | all-gather | bytes 786432 | tf_op jit(solution)/shard_map/all_gather | solution.py:358
  21.8 0.1 merge.1
  21.8 18.5 %all_to_all.5.slabs = f32[8,4,2,8,128]{4,3,2,1,0:T(8,128)S(1)} all-to-all(f32[8,4,2,8,128]{4,3,2,1,0:T(8,128)S(1)} %merge.1), channel_id=1, replica_groups={{448,384,320,256,192,128,64,0},{480,416,352,288,224,160,96,32},{449,385..., dimensions={0} | all-to-all | bytes 524288 | tf_op jit(solution)/shard_map/all_to_all | solution.py:361
  40.3 0.7 %composite.1 = f32[4,4,4,128]{3,2,1,0:T(4,128)} custom-call(f32[5,8,128]{2,1,0:T(8,128)S(1)} %get-tuple-element.22.masks, f32[8,4,2,8,128]{4,3,2,1,0:T(8,128)S(1)} %all_to_all.5.slabs), custom_call_target="tpu_custom_call" | custom-call | bytes 1048576 | tf_op jit(solution)/shard_map/composite/pallas_call | solution.py:362
  (2 shorter events, 0.0 us)
Async XLA Ops:
  0.0 11.8 %copy-start.4 = (s32[4]{0:T(128)S(1)}, s32[4]{0:T(128)}, u32[]{:S(2)}) copy-start(s32[4]{0:T(128)} %refs_4_.1) | copy-start | bytes 52
  0.0 11.8 %copy-start.3 = (s32[4]{0:T(128)S(1)}, s32[4]{0:T(128)}, u32[]{:S(2)}) copy-start(s32[4]{0:T(128)} %refs_3_.1) | copy-start | bytes 52
  0.0 11.8 %copy-start.2 = (f32[3]{0:T(128)S(1)}, f32[3]{0:T(128)}, u32[]{:S(2)}) copy-start(f32[3]{0:T(128)} %refs_2_.1) | copy-start | bytes 40
  0.0 11.8 %copy-start.1 = (f32[3]{0:T(128)S(1)}, f32[3]{0:T(128)}, u32[]{:S(2)}) copy-start(f32[3]{0:T(128)} %refs_1_.1) | copy-start | bytes 40
  0.0 1.0 %copy-start.5 = (f32[8,64,128]{2,1,0:T(8,128)S(1)}, f32[8,64,128]{2,1,0:T(8,128)}, u32[]{:S(2)}) copy-start(f32[8,64,128]{2,1,0:T(8,128)} %density.1) | copy-start | bytes 786436
  1.0 10.8 %copy-start = (f32[3]{0:T(128)S(1)}, f32[3]{0:T(128)}, u32[]{:S(2)}) copy-start(f32[3]{0:T(128)} %refs_0_.1) | copy-start | bytes 40
  1.1 3.1 %collective-permute-start = (f32[2,64,128]{2,1,0:T(8,128)S(1)}, f32[2,64,128]{2,1,0:T(8,128)S(1)}, u32[]{:S(2)}, u32[]{:S(2)}) collective-permute-start(f32[2,64,128]{2,1,0:T(8,128)S(1)} %get-tuple-element.20), channel_id=1, source_target_pairs={{32,0},{64,32},{96,64},{128,96},{160,128},{192,160},{224,192},{256... | collective-permute-start | bytes 196616 | tf_op jit(solution)/shard_map/ppermute | solution.py:317
  4.2 9.9 %collective-permute-start.2 = (f32[10,32,128]{2,1,0:T(8,128)S(1)}, f32[10,32,128]{2,1,0:T(8,128)S(1)}, u32[]{:S(2)}, u32[]{:S(2)}) collective-permute-start(f32[10,32,128]{2,1,0:T(8,128)S(1)} %get-tuple-element.26), channel_id=1, source_target_pairs={{1,0},{2,1},{3,2},{4,3},{5,4},{6,5},{7,6},{8,7},{9,8},{10,9},{11,1... | collective-permute-start | bytes 491528 | tf_op jit(solution)/shard_map/ppermute | solution.py:321
  9.9 7.7 %collective-permute-start.1 = (f32[16,128]{1,0:T(8,128)S(1)}, f32[16,128]{1,0:T(8,128)S(1)}, u32[]{:S(2)}, u32[]{:S(2)}) collective-permute-start(f32[16,128]{1,0:T(8,128)S(1)} %get-tuple-element.21.refs_7_), channel_id=1, source_target_pairs={{0,1},{1,2},{2,3},{3,4},{4,5},{5,6},{6,7},{7,8},{8,9},{9,10},{10,1... | collective-permute-start | bytes 24584 | tf_op jit(solution)/shard_map/ppermute | solution.py:322

commit v14 on v12

--- a/solution.py
+++ b/solution.py
@@ -15,7 +15,7 @@
 SLABS = PLANES + 1
 CHIPS = GROUPS // 2
 SHARE = ROWS // GROUPS
-ORDERS = ((7, 6, 5, 4, 3, 2, 1, 0), (7, 6, 5, 4, 3, 2, 1, 0))
+ORDERS = ((0, 7, 6, 5, 4, 3, 2, 1), (0, 7, 6, 5, 4, 3, 2, 1))
 PARAMS = pltpu.CompilerParams(vmem_limit_bytes=8 * 2**20)
 LIGHT, GAIN, BIAS, PLAIN, BEYOND, NEXT, NEXT_BEYOND = 0, 3, 6, 9, 10, 11, 12
 FRONT, BACK, CORE = 0, 2, 4

time: 41.3 us -> 43.6 us (1.056)
  blocking collectives: 22 us -> 24.5 us
    all_to_all x1, blocking collectives: 18.5 us -> 20.9 us  [on_device(): lax.all_to_all(merged, 'depth', 0, 0, tiled=True, axis_index_groups=groups)]
  transfers between devices with their start and end apart: 3 -> 3, of which waited for: 2 -> 2; matrix products, arithmetic and copies ran while one was open for 0% -> 0% of each run, Pallas kernels for 9% -> 8%
where the time goes in v14:
time: 43.6 us; the launch traced here: 43.4 us
  blocking collectives  24.5 us (56%)
  starting transfers between devices  8.86 us (20%)
  Pallas kernels  5.09 us (12%)
  waiting for transfers between devices  3.83 us (9%)
  local copies, waits for them, and re-layouts  1.01 us (2%)
    all_to_all x1, blocking collectives, on_device(): lax.all_to_all(merged, 'depth', 0, 0, tiled=True, axis_index_groups=groups)  20.9 us
    ppermute x1, starting transfers between devices, on_device(): lax.ppermute(own_high, 'height', [(i + 1, i) for i in range(heights - 1)])  5.64 us
    all_gather x1, blocking collectives, on_device(): gathered = lax.all_gather(given, 'depth', axis=0, axis_index_groups=cores)  3.56 us
    pallas_call x1, Pallas kernels, on_device(): kernel(inner_kernel, 'inner', (shaded, array(16, COLS), array(5, 8, COLS)...  2.16 us
    ppermute x1, waiting for transfers between devices, on_device(): lax.ppermute(own_low, 'height', [(i, i + 1) for i in range(heights - 1)])  1.98 us
    ppermute x1, starting transfers between devices, on_device(): lax.ppermute(own_low, 'height', [(i, i + 1) for i in range(heights - 1)])  1.92 us
    ppermute x1, waiting for transfers between devices, on_device(): lax.ppermute(first, 'depth', [(i + 1, i) for i in range(depths - 1)])  1.85 us
    pallas_call x1, Pallas kernels, on_device(): kernel(render_kernel, 'render', (part, part, shaded), [VMEM, VMEM, ANY] +...  1.5 us
  transfers between devices with their start and end apart: 3, of which 2 were waited for; matrix products, arithmetic and copies ran while one was open for 0% of the time, Pallas kernels for 8%

profile of v14, /device:TPU:6, one launch (start us, length us, event | category | flops | bytes accessed | tf_op | source)
XLA Modules:
  0.0 43.4 jit_solution(7202290370373694811)
XLA Ops:
  0.0 0.0 copy-start.4
  0.0 0.0 copy-start.3
  0.0 0.0 copy-start.2
  0.0 0.0 copy-start.1
  0.0 0.0 copy-start.5
  0.0 1.0 %copy-done.5 = f32[8,64,128]{2,1,0:T(8,128)S(1)} copy-done((f32[8,64,128]{2,1,0:T(8,128)S(1)}, f32[8,64,128]{2,1,0:T(8,128)}, u32[]{:S(2)}) %copy-start.5) | copy-done | bytes 262168
  1.0 0.0 copy-start
  1.1 1.3 %collective-permute-start = (f32[2,64,128]{2,1,0:T(8,128)S(1)}, f32[2,64,128]{2,1,0:T(8,128)S(1)}, u32[]{:S(2)}, u32[]{:S(2)}) collective-permute-start(f32[2,64,128]{2,1,0:T(8,128)S(1)} %get-tuple-element.19), channel_id=1, source_target_pairs={{32,0},{64,32},{96,64},{128,96},{160,128},{192,160},{224,192},{256... | collective-permute-start | bytes 196616 | tf_op jit(solution)/shard_map/ppermute | solution.py:305
  2.4 1.8 %collective-permute-done.coming.refs_6_ = f32[2,64,128]{2,1,0:T(8,128)S(1)} collective-permute-done((f32[2,64,128]{2,1,0:T(8,128)S(1)}, f32[2,64,128]{2,1,0:T(8,128)S(1)}, u32[]{:S(2)}, u32[]{:S(2)}) %collective-permute-start) | collective-permute-done | bytes 65568 | tf_op jit(solution)/shard_map/ppermute | solution.py:305
  4.2 5.6 %collective-permute-start.2 = (f32[10,32,128]{2,1,0:T(8,128)S(1)}, f32[10,32,128]{2,1,0:T(8,128)S(1)}, u32[]{:S(2)}, u32[]{:S(2)}) collective-permute-start(f32[10,32,128]{2,1,0:T(8,128)S(1)} %get-tuple-element.24), channel_id=1, source_target_pairs={{1,0},{2,1},{3,2},{4,3},{5,4},{6,5},{7,6},{8,7},{9,8},{10,9},{11,1... | collective-permute-start | bytes 491528 | tf_op jit(solution)/shard_map/ppermute | solution.py:309
  9.9 1.9 %collective-permute-start.1 = (f32[16,128]{1,0:T(8,128)S(1)}, f32[16,128]{1,0:T(8,128)S(1)}, u32[]{:S(2)}, u32[]{:S(2)}) collective-permute-start(f32[16,128]{1,0:T(8,128)S(1)} %get-tuple-element.20.refs_7_), channel_id=1, source_target_pairs={{0,1},{1,2},{2,3},{3,4},{4,5},{5,6},{6,7},{7,8},{8,9},{9,10},{10,1... | collective-permute-start | bytes 24584 | tf_op jit(solution)/shard_map/ppermute | solution.py:310
  11.8 0.0 copy-done.4
  11.8 0.0 copy-done.3
  11.8 0.0 copy-done.2
  11.8 0.0 copy-done.1
  11.8 0.0 copy-done
  11.9 2.2 %inner.1 = (f32[4,864,128]{2,1,0:T(8,128)S(1)}, f32[16,128]{1,0:T(8,128)S(1)}, f32[5,8,128]{2,1,0:T(8,128)S(1)}, s32[64]{0:T(128)S(1)}) custom-call(f32[3]{0:T(128)S(1)} %copy-done, f32[3]{0:T(128)S(1)} %copy-done.1, f32[3]{0:T(128)S(1)} %copy-done.2, s32[4]{0:T(128)S(1)} %copy-done.3, s32[4]{0:T(128)S(1)} %copy-done.4, ...), custom_call_target="tpu_custom_call" | custom-call | flops 10000000 | bytes 1048576 | tf_op jit(solution)/shard_map/inner/pallas_call | solution.py:313
  14.0 0.0 collective-permute-done.2.high
  14.0 1.5 %render.1 = (f32[8,4,2,8,128]{4,3,2,1,0:T(8,128)S(1)}, f32[8,4,2,8,128]{4,3,2,1,0:T(8,128)S(1)}, f32[4,864,128]{2,1,0:T(8,128)S(1)}) custom-call(f32[16,128]{1,0:T(8,128)S(1)} %get-tuple-element.22.table, f32[5,8,128]{2,1,0:T(8,128)S(1)} %get-tuple-element.21.masks, s32[64]{0:T(128)S(1)} %get-tuple-element.23.starts_in, ...), custom_call_target="tpu_custom_call", output_to_operand_aliasing={{2}: (6, {})} | custom-call | flops 10000000 | bytes 1048576 | tf_op jit(solution)/shard_map/render/pallas_call | solution.py:326
  15.5 2.0 %collective-permute-done.1.low = f32[16,128]{1,0:T(8,128)S(1)} collective-permute-done((f32[16,128]{1,0:T(8,128)S(1)}, f32[16,128]{1,0:T(8,128)S(1)}, u32[]{:S(2)}, u32[]{:S(2)}) %collective-permute-start.1) | collective-permute-done | bytes 8224 | tf_op jit(solution)/shard_map/ppermute | solution.py:310
  17.5 0.7 %first.1 = (f32[8,4,2,8,128]{4,3,2,1,0:T(8,128)S(1)}, f32[8,4,2,8,128]{4,3,2,1,0:T(8,128)S(1)}, f32[4,864,128]{2,1,0:T(8,128)S(1)}) custom-call(f32[16,128]{1,0:T(8,128)S(1)} %get-tuple-element.22.table, f32[5,8,128]{2,1,0:T(8,128)S(1)} %get-tuple-element.21.masks, ...), custom_call_target="tpu_custom_call", output_to_operand_aliasing={{2}: (6, {}), {0}: (7, {}), {1}: (8, {})} | custom-call | bytes 1048576 | tf_op jit(solution)/shard_map/first/pallas_call | solution.py:336
  18.2 3.6 %all-gather = f32[16,4,2,8,128]{4,3,2,1,0:T(8,128)S(1)} all-gather(f32[8,4,2,8,128]{4,3,2,1,0:T(8,128)S(1)} %get-tuple-element.30), channel_id=2, replica_groups={{0,32},{64,96},{128,160},{192,224},{256,288},{320,352},{384,416},{448,4..., dimensions={0}, use_global_device_ids=true | all-gather | bytes 786432 | tf_op jit(solution)/shard_map/all_gather | solution.py:346
  21.8 0.1 merge.1
  21.8 20.9 %all_to_all.5.slabs = f32[8,4,2,8,128]{4,3,2,1,0:T(8,128)S(1)} all-to-all(f32[8,4,2,8,128]{4,3,2,1,0:T(8,128)S(1)} %merge.1), channel_id=1, replica_groups={{0,448,384,320,256,192,128,64},{32,480,416,352,288,224,160,96},{1,449,3..., dimensions={0} | all-to-all | bytes 524288 | tf_op jit(solution)/shard_map/all_to_all | solution.py:349
  42.7 0.7 %composite.1 = f32[4,4,4,128]{3,2,1,0:T(4,128)} custom-call(f32[5,8,128]{2,1,0:T(8,128)S(1)} %get-tuple-element.21.masks, f32[8,4,2,8,128]{4,3,2,1,0:T(8,128)S(1)} %all_to_all.5.slabs), custom_call_target="tpu_custom_call" | custom-call | bytes 1048576 | tf_op jit(solution)/shard_map/composite/pallas_call | solution.py:350
  (2 shorter events, 0.0 us)
Async XLA Ops:
  0.0 11.8 %copy-start.4 = (s32[4]{0:T(128)S(1)}, s32[4]{0:T(128)}, u32[]{:S(2)}) copy-start(s32[4]{0:T(128)} %refs_4_.1) | copy-start | bytes 52
  0.0 11.8 %copy-start.3 = (s32[4]{0:T(128)S(1)}, s32[4]{0:T(128)}, u32[]{:S(2)}) copy-start(s32[4]{0:T(128)} %refs_3_.1) | copy-start | bytes 52
  0.0 11.8 %copy-start.2 = (f32[3]{0:T(128)S(1)}, f32[3]{0:T(128)}, u32[]{:S(2)}) copy-start(f32[3]{0:T(128)} %refs_2_.1) | copy-start | bytes 40
  0.0 11.8 %copy-start.1 = (f32[3]{0:T(128)S(1)}, f32[3]{0:T(128)}, u32[]{:S(2)}) copy-start(f32[3]{0:T(128)} %refs_1_.1) | copy-start | bytes 40
  0.0 1.0 %copy-start.5 = (f32[8,64,128]{2,1,0:T(8,128)S(1)}, f32[8,64,128]{2,1,0:T(8,128)}, u32[]{:S(2)}) copy-start(f32[8,64,128]{2,1,0:T(8,128)} %density.1) | copy-start | bytes 786436
  1.0 10.8 %copy-start = (f32[3]{0:T(128)S(1)}, f32[3]{0:T(128)}, u32[]{:S(2)}) copy-start(f32[3]{0:T(128)} %refs_0_.1) | copy-start | bytes 40
  1.1 3.1 %collective-permute-start = (f32[2,64,128]{2,1,0:T(8,128)S(1)}, f32[2,64,128]{2,1,0:T(8,128)S(1)}, u32[]{:S(2)}, u32[]{:S(2)}) collective-permute-start(f32[2,64,128]{2,1,0:T(8,128)S(1)} %get-tuple-element.19), channel_id=1, source_target_pairs={{32,0},{64,32},{96,64},{128,96},{160,128},{192,160},{224,192},{256... | collective-permute-start | bytes 196616 | tf_op jit(solution)/shard_map/ppermute | solution.py:305
  4.2 9.8 %collective-permute-start.2 = (f32[10,32,128]{2,1,0:T(8,128)S(1)}, f32[10,32,128]{2,1,0:T(8,128)S(1)}, u32[]{:S(2)}, u32[]{:S(2)}) collective-permute-start(f32[10,32,128]{2,1,0:T(8,128)S(1)} %get-tuple-element.24), channel_id=1, source_target_pairs={{1,0},{2,1},{3,2},{4,3},{5,4},{6,5},{7,6},{8,7},{9,8},{10,9},{11,1... | collective-permute-start | bytes 491528 | tf_op jit(solution)/shard_map/ppermute | solution.py:309
  9.9 7.7 %collective-permute-start.1 = (f32[16,128]{1,0:T(8,128)S(1)}, f32[16,128]{1,0:T(8,128)S(1)}, u32[]{:S(2)}, u32[]{:S(2)}) collective-permute-start(f32[16,128]{1,0:T(8,128)S(1)} %get-tuple-element.20.refs_7_), channel_id=1, source_target_pairs={{0,1},{1,2},{2,3},{3,4},{4,5},{5,6},{6,7},{7,8},{8,9},{9,10},{10,1... | collective-permute-start | bytes 24584 | tf_op jit(solution)/shard_map/ppermute | solution.py:310

commit v15 on v14

--- a/solution.py
+++ b/solution.py
@@ -15,7 +15,7 @@
 SLABS = PLANES + 1
 CHIPS = GROUPS // 2
 SHARE = ROWS // GROUPS
-ORDERS = ((0, 7, 6, 5, 4, 3, 2, 1), (0, 7, 6, 5, 4, 3, 2, 1))
+ORDERS = ((7, 6, 5, 4, 3, 2, 1, 0), (7, 6, 5, 4, 3, 2, 0, 1))
 PARAMS = pltpu.CompilerParams(vmem_limit_bytes=8 * 2**20)
 LIGHT, GAIN, BIAS, PLAIN, BEYOND, NEXT, NEXT_BEYOND = 0, 3, 6, 9, 10, 11, 12
 FRONT, BACK, CORE = 0, 2, 4

time: 43.6 us -> 41.3 us (0.947)
  blocking collectives: 24.5 us -> 21.9 us
    all_to_all x1, blocking collectives: 20.9 us -> 18.4 us  [on_device(): lax.all_to_all(merged, 'depth', 0, 0, tiled=True, axis_index_groups=groups)]
  transfers between devices with their start and end apart: 3 -> 3, of which waited for: 2 -> 2; matrix products, arithmetic and copies ran while one was open for 0% -> 0% of each run, Pallas kernels for 8% -> 9%
where the time goes in v15:
time: 41.3 us; the launch traced here: 40.9 us
  blocking collectives  21.9 us (53%)
  starting transfers between devices  8.86 us (21%)
  Pallas kernels  5.09 us (12%)
  waiting for transfers between devices  3.83 us (9%)
  local copies, waits for them, and re-layouts  1.01 us (2%)
    all_to_all x1, blocking collectives, on_device(): lax.all_to_all(merged, 'depth', 0, 0, tiled=True, axis_index_groups=groups)  18.4 us
    ppermute x1, starting transfers between devices, on_device(): lax.ppermute(own_high, 'height', [(i + 1, i) for i in range(heights - 1)])  5.64 us
    all_gather x1, blocking collectives, on_device(): gathered = lax.all_gather(given, 'depth', axis=0, axis_index_groups=cores)  3.56 us
    pallas_call x1, Pallas kernels, on_device(): kernel(inner_kernel, 'inner', (shaded, array(16, COLS), array(5, 8, COLS)...  2.16 us
    ppermute x1, waiting for transfers between devices, on_device(): lax.ppermute(own_low, 'height', [(i, i + 1) for i in range(heights - 1)])  1.98 us
    ppermute x1, starting transfers between devices, on_device(): lax.ppermute(own_low, 'height', [(i, i + 1) for i in range(heights - 1)])  1.92 us
    ppermute x1, waiting for transfers between devices, on_device(): lax.ppermute(first, 'depth', [(i + 1, i) for i in range(depths - 1)])  1.85 us
    pallas_call x1, Pallas kernels, on_device(): kernel(render_kernel, 'render', (part, part, shaded), [VMEM, VMEM, ANY] +...  1.5 us
  transfers between devices with their start and end apart: 3, of which 2 were waited for; matrix products, arithmetic and copies ran while one was open for 0% of the time, Pallas kernels for 9%

profile of v15, /device:TPU:6, one launch (start us, length us, event | category | flops | bytes accessed | tf_op | source)
XLA Modules:
  0.0 40.9 jit_solution(13183745137035455150)
XLA Ops:
  0.0 0.0 copy-start.4
  0.0 0.0 copy-start.3
  0.0 0.0 copy-start.2
  0.0 0.0 copy-start.1
  0.0 0.0 copy-start.5
  0.0 1.0 %copy-done.5 = f32[8,64,128]{2,1,0:T(8,128)S(1)} copy-done((f32[8,64,128]{2,1,0:T(8,128)S(1)}, f32[8,64,128]{2,1,0:T(8,128)}, u32[]{:S(2)}) %copy-start.5) | copy-done | bytes 262168
  1.0 0.0 copy-start
  1.1 1.3 %collective-permute-start = (f32[2,64,128]{2,1,0:T(8,128)S(1)}, f32[2,64,128]{2,1,0:T(8,128)S(1)}, u32[]{:S(2)}, u32[]{:S(2)}) collective-permute-start(f32[2,64,128]{2,1,0:T(8,128)S(1)} %get-tuple-element.19), channel_id=1, source_target_pairs={{32,0},{64,32},{96,64},{128,96},{160,128},{192,160},{224,192},{256... | collective-permute-start | bytes 196616 | tf_op jit(solution)/shard_map/ppermute | solution.py:305
  2.4 1.8 %collective-permute-done.coming.refs_6_ = f32[2,64,128]{2,1,0:T(8,128)S(1)} collective-permute-done((f32[2,64,128]{2,1,0:T(8,128)S(1)}, f32[2,64,128]{2,1,0:T(8,128)S(1)}, u32[]{:S(2)}, u32[]{:S(2)}) %collective-permute-start) | collective-permute-done | bytes 65568 | tf_op jit(solution)/shard_map/ppermute | solution.py:305
  4.2 5.6 %collective-permute-start.2 = (f32[10,32,128]{2,1,0:T(8,128)S(1)}, f32[10,32,128]{2,1,0:T(8,128)S(1)}, u32[]{:S(2)}, u32[]{:S(2)}) collective-permute-start(f32[10,32,128]{2,1,0:T(8,128)S(1)} %get-tuple-element.24), channel_id=1, source_target_pairs={{1,0},{2,1},{3,2},{4,3},{5,4},{6,5},{7,6},{8,7},{9,8},{10,9},{11,1... | collective-permute-start | bytes 491528 | tf_op jit(solution)/shard_map/ppermute | solution.py:309
  9.9 1.9 %collective-permute-start.1 = (f32[16,128]{1,0:T(8,128)S(1)}, f32[16,128]{1,0:T(8,128)S(1)}, u32[]{:S(2)}, u32[]{:S(2)}) collective-permute-start(f32[16,128]{1,0:T(8,128)S(1)} %get-tuple-element.20.refs_7_), channel_id=1, source_target_pairs={{0,1},{1,2},{2,3},{3,4},{4,5},{5,6},{6,7},{7,8},{8,9},{9,10},{10,1... | collective-permute-start | bytes 24584 | tf_op jit(solution)/shard_map/ppermute | solution.py:310
  11.8 0.0 copy-done.4
  11.8 0.0 copy-done.3
  11.8 0.0 copy-done.2
  11.8 0.0 copy-done.1
  11.8 0.0 copy-done
  11.9 2.2 %inner.1 = (f32[4,864,128]{2,1,0:T(8,128)S(1)}, f32[16,128]{1,0:T(8,128)S(1)}, f32[5,8,128]{2,1,0:T(8,128)S(1)}, s32[64]{0:T(128)S(1)}) custom-call(f32[3]{0:T(128)S(1)} %copy-done, f32[3]{0:T(128)S(1)} %copy-done.1, f32[3]{0:T(128)S(1)} %copy-done.2, s32[4]{0:T(128)S(1)} %copy-done.3, s32[4]{0:T(128)S(1)} %copy-done.4, ...), custom_call_target="tpu_custom_call" | custom-call | flops 10000000 | bytes 1048576 | tf_op jit(solution)/shard_map/inner/pallas_call | solution.py:313
  14.0 0.0 collective-permute-done.2.high
  14.0 1.5 %render.1 = (f32[8,4,2,8,128]{4,3,2,1,0:T(8,128)S(1)}, f32[8,4,2,8,128]{4,3,2,1,0:T(8,128)S(1)}, f32[4,864,128]{2,1,0:T(8,128)S(1)}) custom-call(f32[16,128]{1,0:T(8,128)S(1)} %get-tuple-element.22.table, f32[5,8,128]{2,1,0:T(8,128)S(1)} %get-tuple-element.21.masks, s32[64]{0:T(128)S(1)} %get-tuple-element.23.starts_in, ...), custom_call_target="tpu_custom_call", output_to_operand_aliasing={{2}: (6, {})} | custom-call | flops 10000000 | bytes 1048576 | tf_op jit(solution)/shard_map/render/pallas_call | solution.py:326
  15.5 2.0 %collective-permute-done.1.low = f32[16,128]{1,0:T(8,128)S(1)} collective-permute-done((f32[16,128]{1,0:T(8,128)S(1)}, f32[16,128]{1,0:T(8,128)S(1)}, u32[]{:S(2)}, u32[]{:S(2)}) %collective-permute-start.1) | collective-permute-done | bytes 8224 | tf_op jit(solution)/shard_map/ppermute | solution.py:310
  17.5 0.7 %first.1 = (f32[8,4,2,8,128]{4,3,2,1,0:T(8,128)S(1)}, f32[8,4,2,8,128]{4,3,2,1,0:T(8,128)S(1)}, f32[4,864,128]{2,1,0:T(8,128)S(1)}) custom-call(f32[16,128]{1,0:T(8,128)S(1)} %get-tuple-element.22.table, f32[5,8,128]{2,1,0:T(8,128)S(1)} %get-tuple-element.21.masks, ...), custom_call_target="tpu_custom_call", output_to_operand_aliasing={{2}: (6, {}), {0}: (7, {}), {1}: (8, {})} | custom-call | bytes 1048576 | tf_op jit(solution)/shard_map/first/pallas_call | solution.py:336
  18.2 3.6 %all-gather = f32[16,4,2,8,128]{4,3,2,1,0:T(8,128)S(1)} all-gather(f32[8,4,2,8,128]{4,3,2,1,0:T(8,128)S(1)} %get-tuple-element.30), channel_id=2, replica_groups={{0,32},{64,96},{128,160},{192,224},{256,288},{320,352},{384,416},{448,4..., dimensions={0}, use_global_device_ids=true | all-gather | bytes 786432 | tf_op jit(solution)/shard_map/all_gather | solution.py:346
  21.8 0.1 merge.1
  21.8 18.4 %all_to_all.5.slabs = f32[8,4,2,8,128]{4,3,2,1,0:T(8,128)S(1)} all-to-all(f32[8,4,2,8,128]{4,3,2,1,0:T(8,128)S(1)} %merge.1), channel_id=1, replica_groups={{448,384,320,256,192,128,64,0},{480,416,352,288,224,160,32,96},{449,385..., dimensions={0} | all-to-all | bytes 524288 | tf_op jit(solution)/shard_map/all_to_all | solution.py:349
  40.2 0.7 %composite.1 = f32[4,4,4,128]{3,2,1,0:T(4,128)} custom-call(f32[5,8,128]{2,1,0:T(8,128)S(1)} %get-tuple-element.21.masks, f32[8,4,2,8,128]{4,3,2,1,0:T(8,128)S(1)} %all_to_all.5.slabs), custom_call_target="tpu_custom_call" | custom-call | bytes 1048576 | tf_op jit(solution)/shard_map/composite/pallas_call | solution.py:350
  (2 shorter events, 0.0 us)
Async XLA Ops:
  0.0 11.8 %copy-start.4 = (s32[4]{0:T(128)S(1)}, s32[4]{0:T(128)}, u32[]{:S(2)}) copy-start(s32[4]{0:T(128)} %refs_4_.1) | copy-start | bytes 52
  0.0 11.8 %copy-start.3 = (s32[4]{0:T(128)S(1)}, s32[4]{0:T(128)}, u32[]{:S(2)}) copy-start(s32[4]{0:T(128)} %refs_3_.1) | copy-start | bytes 52
  0.0 11.8 %copy-start.2 = (f32[3]{0:T(128)S(1)}, f32[3]{0:T(128)}, u32[]{:S(2)}) copy-start(f32[3]{0:T(128)} %refs_2_.1) | copy-start | bytes 40
  0.0 11.8 %copy-start.1 = (f32[3]{0:T(128)S(1)}, f32[3]{0:T(128)}, u32[]{:S(2)}) copy-start(f32[3]{0:T(128)} %refs_1_.1) | copy-start | bytes 40
  0.0 1.0 %copy-start.5 = (f32[8,64,128]{2,1,0:T(8,128)S(1)}, f32[8,64,128]{2,1,0:T(8,128)}, u32[]{:S(2)}) copy-start(f32[8,64,128]{2,1,0:T(8,128)} %density.1) | copy-start | bytes 786436
  1.0 10.8 %copy-start = (f32[3]{0:T(128)S(1)}, f32[3]{0:T(128)}, u32[]{:S(2)}) copy-start(f32[3]{0:T(128)} %refs_0_.1) | copy-start | bytes 40
  1.1 3.1 %collective-permute-start = (f32[2,64,128]{2,1,0:T(8,128)S(1)}, f32[2,64,128]{2,1,0:T(8,128)S(1)}, u32[]{:S(2)}, u32[]{:S(2)}) collective-permute-start(f32[2,64,128]{2,1,0:T(8,128)S(1)} %get-tuple-element.19), channel_id=1, source_target_pairs={{32,0},{64,32},{96,64},{128,96},{160,128},{192,160},{224,192},{256... | collective-permute-start | bytes 196616 | tf_op jit(solution)/shard_map/ppermute | solution.py:305
  4.2 9.8 %collective-permute-start.2 = (f32[10,32,128]{2,1,0:T(8,128)S(1)}, f32[10,32,128]{2,1,0:T(8,128)S(1)}, u32[]{:S(2)}, u32[]{:S(2)}) collective-permute-start(f32[10,32,128]{2,1,0:T(8,128)S(1)} %get-tuple-element.24), channel_id=1, source_target_pairs={{1,0},{2,1},{3,2},{4,3},{5,4},{6,5},{7,6},{8,7},{9,8},{10,9},{11,1... | collective-permute-start | bytes 491528 | tf_op jit(solution)/shard_map/ppermute | solution.py:309
  9.9 7.7 %collective-permute-start.1 = (f32[16,128]{1,0:T(8,128)S(1)}, f32[16,128]{1,0:T(8,128)S(1)}, u32[]{:S(2)}, u32[]{:S(2)}) collective-permute-start(f32[16,128]{1,0:T(8,128)S(1)} %get-tuple-element.20.refs_7_), channel_id=1, source_target_pairs={{0,1},{1,2},{2,3},{3,4},{4,5},{5,6},{6,7},{7,8},{8,9},{9,10},{10,1... | collective-permute-start | bytes 24584 | tf_op jit(solution)/shard_map/ppermute | solution.py:310

commit v16 on v15

--- a/solution.py
+++ b/solution.py
@@ -15,7 +15,7 @@
 SLABS = PLANES + 1
 CHIPS = GROUPS // 2
 SHARE = ROWS // GROUPS
-ORDERS = ((7, 6, 5, 4, 3, 2, 1, 0), (7, 6, 5, 4, 3, 2, 0, 1))
+ORDERS = ((7, 6, 5, 4, 3, 2, 0, 1), (7, 6, 5, 4, 3, 2, 1, 0))
 PARAMS = pltpu.CompilerParams(vmem_limit_bytes=8 * 2**20)
 LIGHT, GAIN, BIAS, PLAIN, BEYOND, NEXT, NEXT_BEYOND = 0, 3, 6, 9, 10, 11, 12
 FRONT, BACK, CORE = 0, 2, 4

time: 41.3 us -> 41.6 us (level)
  no operation moved by 1% of the time
where the time goes in v16:
time: 41.6 us; the launch traced here: 41 us
  blocking collectives  22.1 us (53%)
  starting transfers between devices  8.86 us (21%)
  Pallas kernels  5.09 us (12%)
  waiting for transfers between devices  3.83 us (9%)
  local copies, waits for them, and re-layouts  1.01 us (2%)
    all_to_all x1, blocking collectives, on_device(): lax.all_to_all(merged, 'depth', 0, 0, tiled=True, axis_index_groups=groups)  18.5 us
    ppermute x1, starting transfers between devices, on_device(): lax.ppermute(own_high, 'height', [(i + 1, i) for i in range(heights - 1)])  5.64 us
    all_gather x1, blocking collectives, on_device(): gathered = lax.all_gather(given, 'depth', axis=0, axis_index_groups=cores)  3.56 us
    pallas_call x1, Pallas kernels, on_device(): kernel(inner_kernel, 'inner', (shaded, array(16, COLS), array(5, 8, COLS)...  2.16 us
    ppermute x1, waiting for transfers between devices, on_device(): lax.ppermute(own_low, 'height', [(i, i + 1) for i in range(heights - 1)])  1.98 us
    ppermute x1, starting transfers between devices, on_device(): lax.ppermute(own_low, 'height', [(i, i + 1) for i in range(heights - 1)])  1.92 us
    ppermute x1, waiting for transfers between devices, on_device(): lax.ppermute(first, 'depth', [(i + 1, i) for i in range(depths - 1)])  1.85 us
    pallas_call x1, Pallas kernels, on_device(): kernel(render_kernel, 'render', (part, part, shaded), [VMEM, VMEM, ANY] +...  1.5 us
  transfers between devices with their start and end apart: 3, of which 2 were waited for; matrix products, arithmetic and copies ran while one was open for 0% of the time, Pallas kernels for 9%

profile of v16, /device:TPU:6, one launch (start us, length us, event | category | flops | bytes accessed | tf_op | source)
XLA Modules:
  0.0 41.0 jit_solution(1851022835174417584)
XLA Ops:
  0.0 0.0 copy-start.4
  0.0 0.0 copy-start.3
  0.0 0.0 copy-start.2
  0.0 0.0 copy-start.1
  0.0 0.0 copy-start.5
  0.0 1.0 %copy-done.5 = f32[8,64,128]{2,1,0:T(8,128)S(1)} copy-done((f32[8,64,128]{2,1,0:T(8,128)S(1)}, f32[8,64,128]{2,1,0:T(8,128)}, u32[]{:S(2)}) %copy-start.5) | copy-done | bytes 262168
  1.0 0.0 copy-start
  1.1 1.3 %collective-permute-start = (f32[2,64,128]{2,1,0:T(8,128)S(1)}, f32[2,64,128]{2,1,0:T(8,128)S(1)}, u32[]{:S(2)}, u32[]{:S(2)}) collective-permute-start(f32[2,64,128]{2,1,0:T(8,128)S(1)} %get-tuple-element.19), channel_id=1, source_target_pairs={{32,0},{64,32},{96,64},{128,96},{160,128},{192,160},{224,192},{256... | collective-permute-start | bytes 196616 | tf_op jit(solution)/shard_map/ppermute | solution.py:305
  2.4 1.8 %collective-permute-done.coming.refs_6_ = f32[2,64,128]{2,1,0:T(8,128)S(1)} collective-permute-done((f32[2,64,128]{2,1,0:T(8,128)S(1)}, f32[2,64,128]{2,1,0:T(8,128)S(1)}, u32[]{:S(2)}, u32[]{:S(2)}) %collective-permute-start) | collective-permute-done | bytes 65568 | tf_op jit(solution)/shard_map/ppermute | solution.py:305
  4.2 5.6 %collective-permute-start.2 = (f32[10,32,128]{2,1,0:T(8,128)S(1)}, f32[10,32,128]{2,1,0:T(8,128)S(1)}, u32[]{:S(2)}, u32[]{:S(2)}) collective-permute-start(f32[10,32,128]{2,1,0:T(8,128)S(1)} %get-tuple-element.24), channel_id=1, source_target_pairs={{1,0},{2,1},{3,2},{4,3},{5,4},{6,5},{7,6},{8,7},{9,8},{10,9},{11,1... | collective-permute-start | bytes 491528 | tf_op jit(solution)/shard_map/ppermute | solution.py:309
  9.9 1.9 %collective-permute-start.1 = (f32[16,128]{1,0:T(8,128)S(1)}, f32[16,128]{1,0:T(8,128)S(1)}, u32[]{:S(2)}, u32[]{:S(2)}) collective-permute-start(f32[16,128]{1,0:T(8,128)S(1)} %get-tuple-element.20.refs_7_), channel_id=1, source_target_pairs={{0,1},{1,2},{2,3},{3,4},{4,5},{5,6},{6,7},{7,8},{8,9},{9,10},{10,1... | collective-permute-start | bytes 24584 | tf_op jit(solution)/shard_map/ppermute | solution.py:310
  11.8 0.0 copy-done.4
  11.8 0.0 copy-done.3
  11.8 0.0 copy-done.2
  11.8 0.0 copy-done.1
  11.8 0.0 copy-done
  11.9 2.2 %inner.1 = (f32[4,864,128]{2,1,0:T(8,128)S(1)}, f32[16,128]{1,0:T(8,128)S(1)}, f32[5,8,128]{2,1,0:T(8,128)S(1)}, s32[64]{0:T(128)S(1)}) custom-call(f32[3]{0:T(128)S(1)} %copy-done, f32[3]{0:T(128)S(1)} %copy-done.1, f32[3]{0:T(128)S(1)} %copy-done.2, s32[4]{0:T(128)S(1)} %copy-done.3, s32[4]{0:T(128)S(1)} %copy-done.4, ...), custom_call_target="tpu_custom_call" | custom-call | flops 10000000 | bytes 1048576 | tf_op jit(solution)/shard_map/inner/pallas_call | solution.py:313
  14.0 0.0 collective-permute-done.2.high
  14.0 1.5 %render.1 = (f32[8,4,2,8,128]{4,3,2,1,0:T(8,128)S(1)}, f32[8,4,2,8,128]{4,3,2,1,0:T(8,128)S(1)}, f32[4,864,128]{2,1,0:T(8,128)S(1)}) custom-call(f32[16,128]{1,0:T(8,128)S(1)} %get-tuple-element.22.table, f32[5,8,128]{2,1,0:T(8,128)S(1)} %get-tuple-element.21.masks, s32[64]{0:T(128)S(1)} %get-tuple-element.23.starts_in, ...), custom_call_target="tpu_custom_call", output_to_operand_aliasing={{2}: (6, {})} | custom-call | flops 10000000 | bytes 1048576 | tf_op jit(solution)/shard_map/render/pallas_call | solution.py:326
  15.5 2.0 %collective-permute-done.1.low = f32[16,128]{1,0:T(8,128)S(1)} collective-permute-done((f32[16,128]{1,0:T(8,128)S(1)}, f32[16,128]{1,0:T(8,128)S(1)}, u32[]{:S(2)}, u32[]{:S(2)}) %collective-permute-start.1) | collective-permute-done | bytes 8224 | tf_op jit(solution)/shard_map/ppermute | solution.py:310
  17.5 0.7 %first.1 = (f32[8,4,2,8,128]{4,3,2,1,0:T(8,128)S(1)}, f32[8,4,2,8,128]{4,3,2,1,0:T(8,128)S(1)}, f32[4,864,128]{2,1,0:T(8,128)S(1)}) custom-call(f32[16,128]{1,0:T(8,128)S(1)} %get-tuple-element.22.table, f32[5,8,128]{2,1,0:T(8,128)S(1)} %get-tuple-element.21.masks, ...), custom_call_target="tpu_custom_call", output_to_operand_aliasing={{2}: (6, {}), {0}: (7, {}), {1}: (8, {})} | custom-call | bytes 1048576 | tf_op jit(solution)/shard_map/first/pallas_call | solution.py:336
  18.2 3.6 %all-gather = f32[16,4,2,8,128]{4,3,2,1,0:T(8,128)S(1)} all-gather(f32[8,4,2,8,128]{4,3,2,1,0:T(8,128)S(1)} %get-tuple-element.30), channel_id=2, replica_groups={{0,32},{64,96},{128,160},{192,224},{256,288},{320,352},{384,416},{448,4..., dimensions={0}, use_global_device_ids=true | all-gather | bytes 786432 | tf_op jit(solution)/shard_map/all_gather | solution.py:346
  21.8 0.1 merge.1
  21.8 18.5 %all_to_all.5.slabs = f32[8,4,2,8,128]{4,3,2,1,0:T(8,128)S(1)} all-to-all(f32[8,4,2,8,128]{4,3,2,1,0:T(8,128)S(1)} %merge.1), channel_id=1, replica_groups={{448,384,320,256,192,128,0,64},{480,416,352,288,224,160,96,32},{449,385..., dimensions={0} | all-to-all | bytes 524288 | tf_op jit(solution)/shard_map/all_to_all | solution.py:349
  40.4 0.7 %composite.1 = f32[4,4,4,128]{3,2,1,0:T(4,128)} custom-call(f32[5,8,128]{2,1,0:T(8,128)S(1)} %get-tuple-element.21.masks, f32[8,4,2,8,128]{4,3,2,1,0:T(8,128)S(1)} %all_to_all.5.slabs), custom_call_target="tpu_custom_call" | custom-call | bytes 1048576 | tf_op jit(solution)/shard_map/composite/pallas_call | solution.py:350
  (2 shorter events, 0.0 us)
Async XLA Ops:
  0.0 11.8 %copy-start.4 = (s32[4]{0:T(128)S(1)}, s32[4]{0:T(128)}, u32[]{:S(2)}) copy-start(s32[4]{0:T(128)} %refs_4_.1) | copy-start | bytes 52
  0.0 11.8 %copy-start.3 = (s32[4]{0:T(128)S(1)}, s32[4]{0:T(128)}, u32[]{:S(2)}) copy-start(s32[4]{0:T(128)} %refs_3_.1) | copy-start | bytes 52
  0.0 11.8 %copy-start.2 = (f32[3]{0:T(128)S(1)}, f32[3]{0:T(128)}, u32[]{:S(2)}) copy-start(f32[3]{0:T(128)} %refs_2_.1) | copy-start | bytes 40
  0.0 11.8 %copy-start.1 = (f32[3]{0:T(128)S(1)}, f32[3]{0:T(128)}, u32[]{:S(2)}) copy-start(f32[3]{0:T(128)} %refs_1_.1) | copy-start | bytes 40
  0.0 1.0 %copy-start.5 = (f32[8,64,128]{2,1,0:T(8,128)S(1)}, f32[8,64,128]{2,1,0:T(8,128)}, u32[]{:S(2)}) copy-start(f32[8,64,128]{2,1,0:T(8,128)} %density.1) | copy-start | bytes 786436
  1.0 10.8 %copy-start = (f32[3]{0:T(128)S(1)}, f32[3]{0:T(128)}, u32[]{:S(2)}) copy-start(f32[3]{0:T(128)} %refs_0_.1) | copy-start | bytes 40
  1.1 3.1 %collective-permute-start = (f32[2,64,128]{2,1,0:T(8,128)S(1)}, f32[2,64,128]{2,1,0:T(8,128)S(1)}, u32[]{:S(2)}, u32[]{:S(2)}) collective-permute-start(f32[2,64,128]{2,1,0:T(8,128)S(1)} %get-tuple-element.19), channel_id=1, source_target_pairs={{32,0},{64,32},{96,64},{128,96},{160,128},{192,160},{224,192},{256... | collective-permute-start | bytes 196616 | tf_op jit(solution)/shard_map/ppermute | solution.py:305
  4.2 9.8 %collective-permute-start.2 = (f32[10,32,128]{2,1,0:T(8,128)S(1)}, f32[10,32,128]{2,1,0:T(8,128)S(1)}, u32[]{:S(2)}, u32[]{:S(2)}) collective-permute-start(f32[10,32,128]{2,1,0:T(8,128)S(1)} %get-tuple-element.24), channel_id=1, source_target_pairs={{1,0},{2,1},{3,2},{4,3},{5,4},{6,5},{7,6},{8,7},{9,8},{10,9},{11,1... | collective-permute-start | bytes 491528 | tf_op jit(solution)/shard_map/ppermute | solution.py:309
  9.9 7.7 %collective-permute-start.1 = (f32[16,128]{1,0:T(8,128)S(1)}, f32[16,128]{1,0:T(8,128)S(1)}, u32[]{:S(2)}, u32[]{:S(2)}) collective-permute-start(f32[16,128]{1,0:T(8,128)S(1)} %get-tuple-element.20.refs_7_), channel_id=1, source_target_pairs={{0,1},{1,2},{2,3},{3,4},{4,5},{5,6},{6,7},{7,8},{8,9},{9,10},{10,1... | collective-permute-start | bytes 24584 | tf_op jit(solution)/shard_map/ppermute | solution.py:310
